TPU v7x, 128 devices: a whole 4x4x4 slice. The times are simulated.
128 devices in a mesh: ctx: 32 (over x, y, core), fsdp: 4 (over z).
Axes of the slice: x: 4, y: 4, z: 4, core: 2. Of those that a mesh axis runs over, the one named last changes fastest.
Arguments:
- tokens: bfloat16 [4, 2, 2048, 1024], P('fsdp', None, 'ctx'), may hold values from -6 to 6
- doc_start: int32 [4, 2, 2048], P('fsdp', None, 'ctx'), may hold values from 0 to 4095, as said below
- cotangent: bfloat16 [4, 2, 2048, 1024], P('fsdp', None, 'ctx'), may hold values from -6 to 6
- w_in: bfloat16 [1024, 4096], P('fsdp'), may hold values from -0.1875 to 0.1875
- w_dt: bfloat16 [1024, 24], P('fsdp'), may hold values from -0.1875 to 0.1875
- conv_weight: bfloat16 [4, 1792], P(None, 'fsdp'), may hold values from -3 to 3
- conv_bias: bfloat16 [1792], P('fsdp'), may hold values from -0.5 to 0.5
- dt_bias: bfloat16 [24], P('fsdp'), may hold values from -3 to 0.5
- a_log: bfloat16 [24], P('fsdp'), may hold values from -9 to -1
- skip_gain: bfloat16 [24], P('fsdp'), may hold values from 0.5 to 1.5
- inner_gain: bfloat16 [1536], P('fsdp'), may hold values from 0.5 to 1.5
- mamba_out: bfloat16 [1536, 1024], P('fsdp'), may hold values from -0.15625 to 0.15625
- attn_out: bfloat16 [512, 1024], P('fsdp'), may hold values from -3 to 3
- mixer_gain: bfloat16 [1024], P('fsdp'), may hold values from 0.5 to 1.5
- ffn_gain: bfloat16 [1024], P('fsdp'), may hold values from 0.5 to 1.5
- w_gate_up: bfloat16 [1024, 4096], P('fsdp'), may hold values from -0.1875 to 0.1875
- w_down: bfloat16 [2048, 1024], P('fsdp'), may hold values from -0.125 to 0.125
Outputs:
- mixed: bfloat16 [4, 2, 2048, 1024], P('fsdp', None, 'ctx')
- grad_tokens: float32 [4, 2, 2048, 1024], P('fsdp', None, 'ctx')
- grad_w_in: float32 [1024, 4096], P('fsdp')
- grad_w_dt: float32 [1024, 24], P('fsdp')
- grad_conv_weight: float32 [4, 1792], P(None, 'fsdp')
- grad_conv_bias: float32 [1792], P('fsdp')
- grad_dt_bias: float32 [24], P('fsdp')
- grad_a_log: float32 [24], P('fsdp')
- grad_skip_gain: float32 [24], P('fsdp')
- grad_inner_gain: float32 [1536], P('fsdp')
- grad_mamba_out: float32 [1536, 1024], P('fsdp')
- grad_attn_out: float32 [512, 1024], P('fsdp')
- grad_mixer_gain: float32 [1024], P('fsdp')
- grad_ffn_gain: float32 [1024], P('fsdp')
- grad_w_gate_up: float32 [1024, 4096], P('fsdp')
- grad_w_down: float32 [2048, 1024], P('fsdp')
Inputs may be any that keep to these rules, and one draw needn't show every extreme that they name: `doc_start`: the value at each place is the position of the first token of the document that holds that place's token; documents are contiguous runs of positions, so it never exceeds the place's own position and is constant within a document. In every sequence one document begins in the first 64 positions and runs through position 2111.
All inputs are finite; a program needn't handle non-finite values.
Results may differ from a plain program's by a relative error of at most 0.022.
Values may be sent and summed in bfloat16 or wider, within the bound.
No kernel may reach another device: no remote copies, remote signals or barrier semaphores. Data moves between devices by JAX's collectives and lax.ppermute only.
A program may use at most 320 MiB of HBM per device.

v0:
```python
import math

import jax
import jax.numpy as jnp
from jax import lax
from jax.sharding import PartitionSpec as P

FF = 2048
QHEADS = 8
KVHEADS = 2
HDIM = 64
MHEADS = 24
MDIM = 64
NSTATE = 128
KCONV = 4


HIGH = lax.Precision.HIGHEST
EPS = 1e-05
ROPE_BASE = 100000000000.0
NEG = -1e30


def with_halo(shard, sides, width):
    for axis, dim in sides:
        size, length = (lax.axis_size(axis), shard.shape[dim])
        up = [(i, (i + 1) % size) for i in range(size - 1)]
        down = [(j, i) for i, j in up]
        last = lax.slice_in_dim(shard, length - width, length, axis=dim)
        initial = lax.slice_in_dim(shard, 0, width, axis=dim)
        before = lax.ppermute(last, axis, up)
        after = lax.ppermute(initial, axis, down)
        shard = jnp.concatenate([before, shard, after], axis=dim)
    return shard


def carried_in(shard, axis, combine, identity, reverse):
    length, index = (lax.axis_size(axis), lax.axis_index(axis))
    everything = jax.tree.map(lambda part: lax.all_gather(part, axis), shard)
    start = jax.tree.map(
        lambda part, zero: jnp.broadcast_to(jnp.asarray(zero, part.dtype), part.shape),
        shard,
        identity,
    )

    def carried_step(k, before):
        at = length - 1 - k if reverse else k
        reached = at > index if reverse else at < index
        new = combine(before, jax.tree.map(lambda part: part[at], everything))
        return jax.tree.map(lambda a, b: jnp.where(reached, a, b), new, before)

    return lax.fori_loop(0, length, carried_step, start)


def prefix(shard, axis, combine, identity):
    length, index = (lax.axis_size(axis), lax.axis_index(axis))
    everything = jax.tree.map(
        lambda part, kind: lax.all_gather(part.astype(kind), axis),
        shard,
        jax.tree.map(lambda a: jnp.bfloat16 if a.dtype == jnp.float32 else a.dtype, shard),
    )
    start = jax.tree.map(
        lambda part, zero: jnp.broadcast_to(jnp.asarray(zero, part.dtype), part.shape),
        shard,
        identity,
    )

    def prefix_step(k, before):
        reached = k < index
        new = combine(
            before, jax.tree.map(lambda part, own: part[k].astype(own.dtype), everything, shard)
        )
        return jax.tree.map(lambda a, b: jnp.where(reached, a, b), new, before)

    return lax.fori_loop(0, length, prefix_step, start)


def rms_scale(values, gain):
    return values * lax.rsqrt(jnp.mean(values * values, axis=-1, keepdims=True) + EPS) * gain


def gated_norm(mamba_y, gate_z, gain):
    return rms_scale(mamba_y * jax.nn.silu(gate_z), gain)


def swiglu(gate_val, up_val):
    return jax.nn.silu(gate_val) * up_val


def rope_tables(positions, width):
    middle = width // 2
    freq = jnp.exp(jnp.arange(middle, dtype=jnp.float32) * (-2.0 * math.log(ROPE_BASE) / width))
    angle = positions.astype(jnp.float32)[:, None] * freq[None, :]
    return (jnp.cos(angle), jnp.sin(angle))


def rotate(values, cos_table, sin_table):
    middle = values.shape[-1] // 2
    leading = values[..., :middle]
    trailing = values[..., middle:]
    cosine = cos_table[:, None, :]
    sine_part = sin_table[:, None, :]
    return jnp.concatenate(
        [leading * cosine - trailing * sine_part, trailing * cosine + leading * sine_part], axis=-1
    )


def unrotate(values, cos_table, sin_table):
    middle = values.shape[-1] // 2
    leading = values[..., :middle]
    trailing = values[..., middle:]
    cosine = cos_table[:, None, :]
    sine_part = sin_table[:, None, :]
    return jnp.concatenate(
        [leading * cosine + trailing * sine_part, trailing * cosine - leading * sine_part], axis=-1
    )


def mamba_inputs(extended, raw_dt, positions, starts, conv_weight, conv_bias, dt_bias, a_log):
    length = positions.shape[0]
    tap_count = conv_weight.shape[0]
    summed = jnp.zeros((length, conv_weight.shape[1]), dtype=extended.dtype) + conv_bias
    for offset in range(tap_count):
        back_steps = tap_count - 1 - offset
        usable = (positions - back_steps >= starts)[:, None]
        summed = summed + jnp.where(
            usable, conv_weight[offset] * extended[offset : offset + length], 0.0
        )
    mixed_in = jax.nn.silu(summed)
    inner_width = MHEADS * MDIM
    states_x = mixed_in[:, :inner_width].reshape(length, MHEADS, MDIM)
    input_mat = mixed_in[:, inner_width : inner_width + NSTATE]
    output_mat = mixed_in[:, inner_width + NSTATE :]
    step_size = jax.nn.softplus(raw_dt + dt_bias)
    log_decay = -step_size * jnp.exp(a_log)
    return (states_x, input_mat, output_mat, step_size, log_decay)


def ssd_local(states_x, input_mat, output_mat, step_size, log_decay, positions, starts, skip_gain):
    running = jnp.cumsum(log_decay, axis=0)
    allowed = (positions[None, :] <= positions[:, None]) & (positions[None, :] >= starts[:, None])
    spread = running.T[:, :, None] - running.T[:, None, :]
    decay_mat = jnp.where(allowed[None], jnp.exp(jnp.where(allowed[None], spread, 0.0)), 0.0)
    intersection = jnp.dot(output_mat, input_mat.T, precision=HIGH)
    mixing = decay_mat * intersection[None] * step_size.T[:, None, :]
    result = (
        jnp.einsum("hij,jhp->ihp", mixing, states_x, precision=HIGH)
        + skip_gain[None, :, None] * states_x
    )
    carried = (starts < positions[0]).astype(running.dtype)
    state_weight = jnp.exp(running) * carried[:, None]
    final_weight = decay_mat[:, -1, :] * step_size.T
    state_out = jnp.einsum("hj,jhp,jn->hpn", final_weight, states_x, input_mat, precision=HIGH)
    return (result, state_out, state_weight)


def state_term(output_mat, state_weight, state_in):
    return state_weight[:, :, None] * jnp.einsum(
        "in,hpn->ihp", output_mat, state_in, precision=HIGH
    )


def chain_step(earlier, later):
    return (earlier[0] * later[0], later[0][:, None, None] * earlier[1] + later[1])


def paired_step(earlier, later):
    return (chain_step(earlier[0], later[0]), chain_step(later[1], earlier[1]))


def key_positions(count, block_len, ctx_size):
    places = jnp.arange(count, dtype=jnp.int32)
    mirrored = (2 * ctx_size - 1 - places // block_len) * block_len + places % block_len
    return jnp.concatenate([places, mirrored])


def per_device(
    tokens,
    doc_start,
    cotangent,
    w_in,
    w_dt,
    conv_weight,
    conv_bias,
    dt_bias,
    a_log,
    skip_gain,
    inner_gain,
    mamba_out,
    attn_out,
    mixer_gain,
    ffn_gain,
    w_gate_up,
    w_down,
):
    (
        full_in,
        full_dt,
        full_conv,
        full_conv_bias,
        full_dt_bias,
        full_a_log,
        full_skip,
        full_inner,
        full_mamba_out,
        full_attn_out,
        full_mixer,
        full_ffn,
        full_gate_up,
        full_down,
    ) = (
        lax.all_gather(w_in, "fsdp", axis=0, tiled=True),
        lax.all_gather(w_dt, "fsdp", axis=0, tiled=True),
        lax.all_gather(conv_weight, "fsdp", axis=1, tiled=True),
        lax.all_gather(conv_bias, "fsdp", axis=0, tiled=True),
        lax.all_gather(dt_bias, "fsdp", axis=0, tiled=True),
        lax.all_gather(a_log, "fsdp", axis=0, tiled=True),
        lax.all_gather(skip_gain, "fsdp", axis=0, tiled=True),
        lax.all_gather(inner_gain, "fsdp", axis=0, tiled=True),
        lax.all_gather(mamba_out, "fsdp", axis=0, tiled=True),
        lax.all_gather(attn_out, "fsdp", axis=0, tiled=True),
        lax.all_gather(mixer_gain, "fsdp", axis=0, tiled=True),
        lax.all_gather(ffn_gain, "fsdp", axis=0, tiled=True),
        lax.all_gather(w_gate_up, "fsdp", axis=0, tiled=True),
        lax.all_gather(w_down, "fsdp", axis=0, tiled=True),
    )
    conv_taps = full_conv.astype(jnp.float32)
    conv_shift = full_conv_bias.astype(jnp.float32)
    step_bias = full_dt_bias.astype(jnp.float32)
    decay_log = full_a_log.astype(jnp.float32)
    skip_term = full_skip.astype(jnp.float32)
    inner_scale = full_inner.astype(jnp.float32)
    mixer_scale = full_mixer.astype(jnp.float32)
    ffn_scale = full_ffn.astype(jnp.float32)
    block_len = tokens.shape[2]
    row_count = 2 * block_len
    model_width = tokens.shape[3]
    ctx_size = lax.axis_size("ctx")
    ctx_index = lax.axis_index("ctx")
    block_ids = jnp.stack([ctx_index, 2 * ctx_size - 1 - ctx_index])
    positions = block_ids[:, None] * block_len + jnp.arange(block_len, dtype=jnp.int32)[None, :]
    starts = doc_start[0]
    flat_pos = positions.reshape(row_count)
    flat_start = starts.reshape(row_count)
    last_device = ctx_index == ctx_size - 1
    inner_width = MHEADS * MDIM
    conv_width = inner_width + 2 * NSTATE
    query_width = QHEADS * HDIM
    kv_width = KVHEADS * HDIM
    groups = QHEADS // KVHEADS
    score_scale = HDIM ** (-0.5)
    rim = KCONV - 1
    hidden_in = tokens[0].reshape(row_count, model_width).astype(jnp.float32)
    act_one = rms_scale(hidden_in, mixer_scale).astype(jnp.bfloat16)
    projected = jnp.dot(act_one, full_in, preferred_element_type=jnp.float32)
    raw_dt = jnp.dot(act_one, full_dt, preferred_element_type=jnp.float32)
    gate_z = projected[:, :inner_width]
    conv_in = projected[:, inner_width : inner_width + conv_width].reshape(2, block_len, conv_width)
    query_start = inner_width + conv_width
    kv_start = query_start + query_width
    query_raw = projected[:, query_start:kv_start].reshape(row_count, QHEADS, HDIM)
    key_raw = projected[:, kv_start : kv_start + kv_width].reshape(row_count, KVHEADS, HDIM)
    value_raw = projected[:, kv_start + kv_width :]
    tails = conv_in[:, block_len - rim :, :]
    rim_ext = with_halo(jnp.concatenate([tails[1], tails[0]], axis=0), (("ctx", 0),), rim)
    from_left = rim_ext[:rim]
    from_right = rim_ext[3 * rim :]
    prev_second = jnp.where(last_device, tails[0], from_right)
    conv_ext = jnp.concatenate([jnp.stack([from_left, prev_second]), conv_in], axis=1)
    raw_dt3 = raw_dt.reshape(2, block_len, MHEADS)
    states_x, input_mat, output_mat, step_size, log_decay = jax.vmap(
        mamba_inputs, in_axes=(0, 0, 0, 0, None, None, None, None)
    )(conv_ext, raw_dt3, positions, starts, conv_taps, conv_shift, step_bias, decay_log)
    local_y, state_out, state_weight = jax.vmap(ssd_local, in_axes=(0, 0, 0, 0, 0, 0, 0, None))(
        states_x, input_mat, output_mat, step_size, log_decay, positions, starts, skip_term
    )
    block_decay = state_weight[:, -1, :]
    identity = (jnp.ones((MHEADS,), jnp.float32), jnp.zeros((MHEADS, MDIM, NSTATE), jnp.float32))
    first_elem = (block_decay[0], state_out[0])
    before = carried_in((block_decay[0], state_out[0]), "ctx", chain_step, identity, False)
    after = carried_in(
        ((block_decay[1], state_out[1]), (block_decay[0], state_out[0])),
        "ctx",
        paired_step,
        (identity, identity),
        True,
    )
    through = chain_step(chain_step(before, first_elem), after[1])
    entry_second = chain_step(through, after[0])
    state_in = jnp.stack([before[1], entry_second[1]])
    mamba_y = local_y + jax.vmap(state_term)(output_mat, state_weight, state_in)
    y_flat = mamba_y.reshape(row_count, inner_width)
    act_mamba = gated_norm(y_flat, gate_z, inner_scale).astype(jnp.bfloat16)
    cos_table, sin_table = rope_tables(flat_pos, HDIM)
    query4 = (
        rotate(query_raw, cos_table, sin_table)
        .astype(jnp.bfloat16)
        .reshape(row_count, KVHEADS, groups, HDIM)
    )
    key_rot = (
        rotate(key_raw, cos_table, sin_table).astype(jnp.bfloat16).reshape(row_count, kv_width)
    )
    kv_local = jnp.concatenate([key_rot, value_raw.astype(jnp.bfloat16)], axis=-1).reshape(
        2, block_len, 2 * kv_width
    )

    def split_keys(piece):
        count = piece.shape[1]
        key_pos = key_positions(count, block_len, ctx_size)
        rows_all = piece.reshape(2 * count, 2 * kv_width)
        key_part = rows_all[:, :kv_width].reshape(2 * count, KVHEADS, HDIM)
        value_part = rows_all[:, kv_width:].reshape(2 * count, KVHEADS, HDIM)
        allowed = (key_pos[None, :] <= flat_pos[:, None]) & (
            key_pos[None, :] >= flat_start[:, None]
        )
        scores = (
            jnp.einsum("qkgd,tkd->kgqt", query4, key_part, preferred_element_type=jnp.float32)
            * score_scale
        )
        return (count, key_part, value_part, allowed, jnp.where(allowed, scores, NEG))

    run_max = jnp.full((KVHEADS, groups, row_count), NEG, jnp.float32)
    count, key_part, value_part, allowed, scores = split_keys(
        lax.all_gather(kv_local, "ctx", axis=1, tiled=True)
    )
    new_max = jnp.maximum(run_max, jnp.max(scores, axis=-1))
    weights = jnp.where(allowed, jnp.exp(scores - new_max[..., None]), 0.0)
    run_sum = jnp.sum(weights, axis=-1)
    run_acc = jnp.einsum("kgqt,tkd->kgqd", weights, value_part.astype(jnp.float32), precision=HIGH)
    run_max, run_sum, run_acc = (new_max, run_sum, run_acc)
    attn_o = run_acc / run_sum[..., None]
    log_total = run_max + jnp.log(run_sum)
    act_attn = attn_o.transpose(2, 0, 1, 3).reshape(row_count, query_width).astype(jnp.bfloat16)
    mixer = jnp.dot(act_mamba, full_mamba_out, preferred_element_type=jnp.float32) + jnp.dot(
        act_attn, full_attn_out, preferred_element_type=jnp.float32
    )
    middle = hidden_in + mixer
    act_two = rms_scale(middle, ffn_scale).astype(jnp.bfloat16)
    gate_up = jnp.dot(act_two, full_gate_up, preferred_element_type=jnp.float32)
    gate_val = gate_up[:, :FF]
    up_val = gate_up[:, FF:]
    inner = swiglu(gate_val, up_val).astype(jnp.bfloat16)
    result = middle + jnp.dot(inner, full_down, preferred_element_type=jnp.float32)
    mixed = result.astype(jnp.bfloat16).reshape(1, 2, block_len, model_width)
    back_in, back_dt, back_mamba_out = (full_in, full_dt, full_mamba_out)
    back_attn_out, back_gate_up, back_down = (full_attn_out, full_gate_up, full_down)
    grad_out = cotangent[0].reshape(row_count, model_width).astype(jnp.float32)
    grad_ffn = grad_out.astype(jnp.bfloat16)
    grad_down = jnp.einsum("ti,tj->ij", inner, grad_ffn, preferred_element_type=jnp.float32)
    grad_inner = jnp.einsum("tj,ij->ti", grad_ffn, back_down, preferred_element_type=jnp.float32)
    _, swiglu_back = jax.vjp(swiglu, gate_val, up_val)
    grad_gate, grad_up = swiglu_back(grad_inner)
    grad_gu = jnp.concatenate([grad_gate, grad_up], axis=-1).astype(jnp.bfloat16)
    grad_gate_up = jnp.einsum("ti,tj->ij", act_two, grad_gu, preferred_element_type=jnp.float32)
    grad_act_two = jnp.einsum(
        "tj,ij->ti", grad_gu, back_gate_up, preferred_element_type=jnp.float32
    )
    _, norm_two_back = jax.vjp(rms_scale, middle, ffn_scale)
    grad_mid_norm, grad_ffn_gain = norm_two_back(grad_act_two)
    grad_middle = grad_out + grad_mid_norm
    grad_mix = grad_middle.astype(jnp.bfloat16)
    grad_mamba_out = jnp.einsum(
        "ti,tj->ij", act_mamba, grad_mix, preferred_element_type=jnp.float32
    )
    grad_attn_out = jnp.einsum("ti,tj->ij", act_attn, grad_mix, preferred_element_type=jnp.float32)
    grad_mamba_act = jnp.einsum(
        "tj,ij->ti", grad_mix, back_mamba_out, preferred_element_type=jnp.float32
    )
    grad_attn_b = jnp.einsum(
        "tj,ij->ti", grad_mix, back_attn_out, preferred_element_type=jnp.float32
    ).astype(jnp.bfloat16)
    grad_o4 = grad_attn_b.reshape(row_count, KVHEADS, groups, HDIM)
    grad_o32 = grad_o4.astype(jnp.float32)
    query32 = query4.astype(jnp.float32)
    delta = jnp.einsum("qkgd,kgqd->kgq", grad_o32, attn_o)
    count, key_part, value_part, allowed, scores = split_keys(
        lax.all_gather(kv_local, "ctx", axis=1, tiled=True)
    )
    probs = jnp.where(allowed, jnp.exp(scores - log_total[..., None]), 0.0)
    grad_probs = jnp.einsum(
        "qkgd,tkd->kgqt", grad_o4, value_part, preferred_element_type=jnp.float32
    )
    grad_scores = probs * (grad_probs - delta[..., None])
    grad_query = (
        jnp.einsum("kgqt,tkd->kgqd", grad_scores, key_part.astype(jnp.float32), precision=HIGH)
        * score_scale
    )
    grad_key = jnp.einsum("kgqt,qkgd->tkd", grad_scores, query32, precision=HIGH) * score_scale
    grad_value = jnp.einsum("kgqt,qkgd->tkd", probs, grad_o32, precision=HIGH)
    block = jnp.concatenate(
        [grad_key.reshape(2 * count, kv_width), grad_value.reshape(2 * count, kv_width)], axis=-1
    ).reshape(2, count, 2 * kv_width)
    grad_keys = block
    grad_query, grad_keys = (grad_query, grad_keys)
    grad_kv = (
        lax.psum_scatter(grad_keys.astype(jnp.bfloat16), "ctx", scatter_dimension=1, tiled=True)
        .astype(jnp.float32)
        .reshape(row_count, 2 * kv_width)
    )
    grad_key_raw = unrotate(
        grad_kv[:, :kv_width].reshape(row_count, KVHEADS, HDIM), cos_table, sin_table
    )
    grad_query_raw = unrotate(
        grad_query.transpose(2, 0, 1, 3).reshape(row_count, QHEADS, HDIM), cos_table, sin_table
    )
    _, gated_back = jax.vjp(gated_norm, y_flat, gate_z, inner_scale)
    grad_y_flat, grad_z, grad_inner_gain = gated_back(grad_mamba_act)
    grad_y = grad_y_flat.reshape(2, block_len, MHEADS, MDIM)
    leak = jnp.einsum("bih,bihp,bin->bhpn", state_weight, grad_y, output_mat, precision=HIGH)
    second_back = (block_decay[1], leak[1])
    later = prefix((block_decay[1], leak[1]), "ctx", chain_step, identity)
    rest = carried_in(
        ((block_decay[0], leak[0]), (block_decay[1], leak[1])),
        "ctx",
        paired_step,
        (identity, identity),
        True,
    )
    all_second = chain_step(chain_step(later, second_back), rest[1])
    grad_first = chain_step(all_second, rest[0])[1]
    grad_state = jnp.stack([grad_first, later[1]])

    def mamba_block(
        extended, raw_steps, taps_val, shift_val, bias_val, alog_val, skip_val, entry_state
    ):
        xs_val, in_val, out_val, step_val, decay_val = jax.vmap(
            mamba_inputs, in_axes=(0, 0, 0, 0, None, None, None, None)
        )(extended, raw_steps, positions, starts, taps_val, shift_val, bias_val, alog_val)
        block_y, block_state, block_weight = jax.vmap(
            ssd_local, in_axes=(0, 0, 0, 0, 0, 0, 0, None)
        )(xs_val, in_val, out_val, step_val, decay_val, positions, starts, skip_val)
        block_y = block_y + jax.vmap(state_term)(out_val, block_weight, entry_state)
        exit_state = block_weight[:, -1, :, None, None] * entry_state + block_state
        return (block_y, exit_state)

    _, block_back = jax.vjp(
        mamba_block,
        conv_ext,
        raw_dt3,
        conv_taps,
        conv_shift,
        step_bias,
        decay_log,
        skip_term,
        state_in,
    )
    (
        grad_ext,
        grad_raw_dt,
        grad_conv_weight,
        grad_conv_bias,
        grad_dt_bias,
        grad_a_log,
        grad_skip,
        _,
    ) = block_back((grad_y, grad_state))
    grad_prev = grad_ext[:, :rim, :]
    send_rows = jnp.concatenate([grad_prev[0], jnp.where(last_device, 0.0, grad_prev[1])], axis=0)
    back_ext = with_halo(send_rows.astype(jnp.bfloat16), (("ctx", 0),), rim).astype(send_rows.dtype)
    to_second = back_ext[:rim]
    to_first = back_ext[3 * rim :] + jnp.where(last_device, grad_prev[1], 0.0)
    grad_conv_in = grad_ext[:, rim:, :]
    grad_conv_in = grad_conv_in.at[0, block_len - rim :, :].add(to_first)
    grad_conv_in = grad_conv_in.at[1, block_len - rim :, :].add(to_second)
    grad_proj = jnp.concatenate(
        [
            grad_z,
            grad_conv_in.reshape(row_count, conv_width),
            grad_query_raw.reshape(row_count, query_width),
            grad_key_raw.reshape(row_count, kv_width),
            grad_kv[:, kv_width:],
        ],
        axis=-1,
    ).astype(jnp.bfloat16)
    grad_dt_b = grad_raw_dt.reshape(row_count, MHEADS).astype(jnp.bfloat16)
    grad_w_in = jnp.einsum("ti,tj->ij", act_one, grad_proj, preferred_element_type=jnp.float32)
    grad_w_dt = jnp.einsum("ti,tj->ij", act_one, grad_dt_b, preferred_element_type=jnp.float32)
    grad_act_one = jnp.einsum(
        "tj,ij->ti", grad_proj, back_in, preferred_element_type=jnp.float32
    ) + jnp.einsum("tj,ij->ti", grad_dt_b, back_dt, preferred_element_type=jnp.float32)
    _, norm_one_back = jax.vjp(rms_scale, hidden_in, mixer_scale)
    grad_hidden_norm, grad_mixer_gain = norm_one_back(grad_act_one)
    grad_tokens = (grad_middle + grad_hidden_norm).reshape(1, 2, block_len, model_width)
    (
        shard_w_in,
        shard_w_dt,
        shard_conv_w,
        shard_conv_b,
        shard_dt_bias,
        shard_a_log,
        shard_skip,
        shard_inner,
        shard_mamba_out,
        shard_attn_out,
        shard_mixer,
        shard_ffn,
        shard_gate_up,
        shard_down,
    ) = (
        lax.psum_scatter(
            grad_w_in.astype(jnp.bfloat16), "fsdp", scatter_dimension=0, tiled=True
        ).astype(jnp.float32),
        lax.psum_scatter(
            grad_w_dt.astype(jnp.bfloat16), "fsdp", scatter_dimension=0, tiled=True
        ).astype(jnp.float32),
        lax.psum_scatter(
            grad_conv_weight.astype(jnp.bfloat16), "fsdp", scatter_dimension=1, tiled=True
        ).astype(jnp.float32),
        lax.psum_scatter(
            grad_conv_bias.astype(jnp.bfloat16), "fsdp", scatter_dimension=0, tiled=True
        ).astype(jnp.float32),
        lax.psum_scatter(
            grad_dt_bias.astype(jnp.bfloat16), "fsdp", scatter_dimension=0, tiled=True
        ).astype(jnp.float32),
        lax.psum_scatter(
            grad_a_log.astype(jnp.bfloat16), "fsdp", scatter_dimension=0, tiled=True
        ).astype(jnp.float32),
        lax.psum_scatter(
            grad_skip.astype(jnp.bfloat16), "fsdp", scatter_dimension=0, tiled=True
        ).astype(jnp.float32),
        lax.psum_scatter(
            grad_inner_gain.astype(jnp.bfloat16), "fsdp", scatter_dimension=0, tiled=True
        ).astype(jnp.float32),
        lax.psum_scatter(
            grad_mamba_out.astype(jnp.bfloat16), "fsdp", scatter_dimension=0, tiled=True
        ).astype(jnp.float32),
        lax.psum_scatter(
            grad_attn_out.astype(jnp.bfloat16), "fsdp", scatter_dimension=0, tiled=True
        ).astype(jnp.float32),
        lax.psum_scatter(
            grad_mixer_gain.astype(jnp.bfloat16), "fsdp", scatter_dimension=0, tiled=True
        ).astype(jnp.float32),
        lax.psum_scatter(
            grad_ffn_gain.astype(jnp.bfloat16), "fsdp", scatter_dimension=0, tiled=True
        ).astype(jnp.float32),
        lax.psum_scatter(
            grad_gate_up.astype(jnp.bfloat16), "fsdp", scatter_dimension=0, tiled=True
        ).astype(jnp.float32),
        lax.psum_scatter(
            grad_down.astype(jnp.bfloat16), "fsdp", scatter_dimension=0, tiled=True
        ).astype(jnp.float32),
    )
    totals = (
        lax.psum(shard_w_in.astype(jnp.bfloat16), "ctx").astype(jnp.float32),
        lax.psum(shard_w_dt.astype(jnp.bfloat16), "ctx").astype(jnp.float32),
        lax.psum(shard_conv_w.astype(jnp.bfloat16), "ctx").astype(jnp.float32),
        lax.psum(shard_conv_b.astype(jnp.bfloat16), "ctx").astype(jnp.float32),
        lax.psum(shard_dt_bias.astype(jnp.bfloat16), "ctx").astype(jnp.float32),
        lax.psum(shard_a_log.astype(jnp.bfloat16), "ctx").astype(jnp.float32),
        lax.psum(shard_skip.astype(jnp.bfloat16), "ctx").astype(jnp.float32),
        lax.psum(shard_inner.astype(jnp.bfloat16), "ctx").astype(jnp.float32),
        lax.psum(shard_mamba_out.astype(jnp.bfloat16), "ctx").astype(jnp.float32),
        lax.psum(shard_attn_out.astype(jnp.bfloat16), "ctx").astype(jnp.float32),
        lax.psum(shard_mixer.astype(jnp.bfloat16), "ctx").astype(jnp.float32),
        lax.psum(shard_ffn.astype(jnp.bfloat16), "ctx").astype(jnp.float32),
        lax.psum(shard_gate_up.astype(jnp.bfloat16), "ctx").astype(jnp.float32),
        lax.psum(shard_down.astype(jnp.bfloat16), "ctx").astype(jnp.float32),
    )
    return (
        mixed,
        grad_tokens,
        totals[0],
        totals[1],
        totals[2],
        totals[3],
        totals[4],
        totals[5],
        totals[6],
        totals[7],
        totals[8],
        totals[9],
        totals[10],
        totals[11],
        totals[12],
        totals[13],
    )


def solution(mesh):
    placed = (
        P("fsdp", None, "ctx", None),
        P("fsdp", None, "ctx"),
        P("fsdp", None, "ctx", None),
        P("fsdp", None),
        P("fsdp", None),
        P(None, "fsdp"),
        P("fsdp"),
        P("fsdp"),
        P("fsdp"),
        P("fsdp"),
        P("fsdp"),
        P("fsdp", None),
        P("fsdp", None),
        P("fsdp"),
        P("fsdp"),
        P("fsdp", None),
        P("fsdp", None),
    )
    return jax.shard_map(
        per_device,
        mesh=mesh,
        in_specs=placed,
        out_specs=(
            P("fsdp", None, "ctx", None),
            P("fsdp", None, "ctx", None),
            P("fsdp", None),
            P("fsdp", None),
            P(None, "fsdp"),
            P("fsdp"),
            P("fsdp"),
            P("fsdp"),
            P("fsdp"),
            P("fsdp"),
            P("fsdp", None),
            P("fsdp", None),
            P("fsdp"),
            P("fsdp"),
            P("fsdp", None),
            P("fsdp", None),
        ),
        check_vma=False,
    )
```

profile of v0, /device:TPU:1, one launch (start us, length us, event | category | flops | bytes accessed | tf_op | source)
XLA Modules:
  0.0 1469.4 jit_solution(12884448403998586166)
XLA Ops:
  11.1 11.2 all-reduce.27
  29.0 10.0 all-gather.3
  39.2 10.2 all_gather.80
  51.2 45.8 %all-gather.19.cloned.1.call-done = bf16[1024,4096]{1,0:T(8,128)(2,1)} async-done(((bf16[256,4096]{1,0:T(8,128)(2,1)}), bf16[1024,4096]{1,0:T(8,128)(2,1)}) %all-gather.19.cloned.1.call-update) | async-done | bytes 8388624 | tf_op jit(solution)/shard_map/all_gather | solution.py:212
  150.5 32.0 %all-gather = f32[32,1,24]{2,1,0:T(1,128)} all-gather(f32[1,1,24]{2,1,0:T(1,128)S(1)} %copy.338), channel_id=2, replica_groups=mesh['ctx'=32,'fsdp'=4] {'ctx'}, dimensions={0}, use_global_device_ids=true | all-gather | bytes 3168 | tf_op jit(solution)/shard_map/all_gather | solution.py:39
  182.5 22.4 %all-gather.1 = f32[32,1,24]{2,1,0:T(1,128)} all-gather(f32[1,1,24]{2,1,0:T(1,128)S(1)} %copy.340), channel_id=3, replica_groups=mesh['ctx'=32,'fsdp'=4] {'ctx'}, dimensions={0}, use_global_device_ids=true | all-gather | bytes 3168 | tf_op jit(solution)/shard_map/all_gather | solution.py:39
  232.0 10.6 fusion.102
  242.7 93.6 %all-gather.23.cloned.1.call-done = f32[32,24,64,128]{3,2,1,0:T(8,128)} async-done(((f32[1,24,64,128]{3,2,1,0:T(8,128)}), f32[32,24,64,128]{3,2,1,0:T(8,128)}) %all-gather.23.cloned.1.call-update) | async-done | bytes 25165840 | tf_op jit(solution)/shard_map/all_gather | solution.py:39
  336.2 152.4 %while.75 = (s32[]{:T(128)}, f32[24]{0:T(128)S(1)}, f32[24,64,128]{2,1,0:T(8,128)}, f32[24]{0:T(128)S(1)}, f32[24,64,128]{2,1,0:T(8,128)}, /*index=5*/s32[]{:T(1...) while((s32[]{:T(128)}, f32[24]{0:T(128)S(1)}, ...), condition=%wide.region_5.6_spmd.clone, body=%wide.region_4.5_spmd.clone.sunk | while | flops 1573016 | bytes 4719775 | solution.py:52
  488.6 65.1 %while.74 = (s32[]{:T(128)}, f32[24,64,128]{2,1,0:T(8,128)S(1)}, s32[]{:T(128)}, f32[32,24]{1,0:T(8,128)}, f32[32,24,64,128]{3,2,1,0:T(8,128)}, /*index=5*/s32[]{:T(128)}, s32[]{:T(128)}) while((s32[]{:T(128)}, f32[24,64,128]{2,1,0:T(8,128)S(1)}, s32[]{:T(128)}, f32[32,24]{1,0:T(8,128)}, f32[32,24,64,128]{3,2,1,0:T(8,128)}, ...), condition=%wide.region_3.4_spmd.clone, body=%wide.region_2.3_spmd.clone.sunk | while | flops 786436 | bytes 2359697 | solution.py:52
  594.9 17.4 %fusion.28 = bf16[4096,2,64]{0,2,1:T(8,128)(2,1)} fusion(bf16[128,2,4,64]{0,3,2,1:T(8,128)(2,1)S(1)} %bitcast.431, f32[2,4096,128,4]{2,1,3,0:T(8,128)} %copy-done.10, f32[2,4,128]{2,1,0:T(4,128)S(1)} %copy-done.130, pred[128,4096]{0,1:T(8,128)(4,1)} %compare_and_fusion), kind=kOutput, calls=%fused_computation.57 | convolution fusion | flops 3238526976 | bytes 18485248 | tf_op jit(solution)/shard_map/kgqt,qkgd->tkd/dot_general | solution.py:389
  612.3 9.3 fusion.8
  627.4 10.6 fusion.27
  683.1 21.0 %all-gather.2 = bf16[32,1,24]{2,1,0:T(2,128)(2,1)S(1)} all-gather(bf16[1,1,24]{2,1,0:T(2,128)(2,1)S(1)} %copy.355), channel_id=4, replica_groups=mesh['ctx'=32,'fsdp'=4] {'ctx'}, dimensions={0}, use_global_device_ids=true | all-gather | bytes 1584 | tf_op jit(solution)/shard_map/all_gather | solution.py:58
  705.5 13.2 convolution_multiply_fusion
  740.1 56.5 %all-gather.39.cloned.1.call-done = bf16[32,24,64,128]{3,2,1,0:T(8,128)(2,1)} async-done(((bf16[1,24,64,128]{3,2,1,0:T(8,128)(2,1)}), bf16[32,24,64,128]{3,2,1,0:T(8,128)(2,1)}) %all-gather.39.cloned.1.call-update) | async-done | bytes 12582928 | tf_op jit(solution)/shard_map/all_gather | solution.py:58
  796.6 39.6 %while.77 = (s32[]{:T(128)}, f32[24,64,128]{2,1,0:T(8,128)S(1)}, s32[]{:T(128)}, bf16[32,24]{1,0:T(8,128)(2,1)S(1)}, bf16[32,24,64,128]{3,2,1,0:T(8,128)(2,1)}, /*index=5*/s32[]{:T(128)}, s32[]{:T(128)}) while((s32[]{:T(128)}, f32[24,64,128]{2,1,0:T(8,128)S(1)}, s32[]{:T(128)}, bf16[32,24]{1,0:T(8,128)(2,1)S(1)}, ...), condition=%wide.region_16.17_spmd.clone, body=%wide.region_15.16_spmd.clone.sunk | while | flops 983068 | bytes 1966433 | solution.py:75
  836.2 54.3 %all-gather.37.cloned.1.call-done = f32[32,24,64,128]{3,2,1,0:T(8,128)} async-done(((f32[1,24,64,128]{3,2,1,0:T(8,128)}), f32[32,24,64,128]{3,2,1,0:T(8,128)}) %all-gather.37.cloned.1.call-update) | async-done | bytes 25165840 | tf_op jit(solution)/shard_map/all_gather | solution.py:39
  890.5 93.6 %all-gather.35.cloned.1.call-done = f32[32,24,64,128]{3,2,1,0:T(8,128)} async-done(((f32[1,24,64,128]{3,2,1,0:T(8,128)}), f32[32,24,64,128]{3,2,1,0:T(8,128)}) %all-gather.35.cloned.1.call-update) | async-done | bytes 25165840 | tf_op jit(solution)/shard_map/all_gather | solution.py:39
  984.1 148.6 %while.76 = (s32[]{:T(128)}, f32[24]{0:T(128)S(1)}, f32[24,64,128]{2,1,0:T(8,128)}, f32[24]{0:T(128)S(1)}, f32[24,64,128]{2,1,0:T(8,128)}, /*index=5*/s32[]{:T(1...) while((s32[]{:T(128)}, f32[24]{0:T(128)S(1)}, ...), condition=%wide.region_14.15_spmd.clone, body=%wide.region_13.14_spmd.clone.sunk | while | flops 1573016 | bytes 4719775 | solution.py:52
  1203.8 73.0 %reduce-scatter.13.cloned.1.call-done = bf16[256,4096]{1,0:T(8,128)(2,1)} async-done(((bf16[1024,4096]{1,0:T(8,128)(2,1)}), bf16[256,4096]{1,0:T(8,128)(2,1)}) %reduce-scatter.13.cloned.1.call-update) | async-done | bytes 2097168 | tf_op jit(solution)/shard_map/reduce_scatter | solution.py:500
  1290.3 11.2 all-reduce.26
  1304.2 17.3 %reduce-scatter.15.cloned.1.call-done = bf16[256,24]{0,1:T(8,128)(2,1)} async-done(((bf16[1024,24]{0,1:T(8,128)(2,1)}), bf16[256,24]{0,1:T(8,128)(2,1)}) %reduce-scatter.15.cloned.1.call-update) | async-done | bytes 12304 | tf_op jit(solution)/shard_map/reduce_scatter | solution.py:503
  1321.5 124.1 %all-reduce.24 = (bf16[256,24]{0,1:T(8,128)(2,1)S(1)}, bf16[4,448]{1,0:T(4,128)(2,1)S(1)}, bf16[448]{0:T(512)(128)(2,1)S(1)}, bf16[6]{0:T(256)(128)(2,1)S(1)}, b...) all-reduce(bf16[256,24]{0,1:T(8,128)(2,1)} %reduce-scatter.15.clone, ...), channel_id=1, replica_groups=mesh['ctx'=32,'fsdp'=4] {'ctx'}, use_global_device_ids=true, to_apply=%region_29.30 | all-reduce | flops 9298 | bytes 37192 | tf_op jit(solution)/shard_map/psum | solution.py:545
  (932 shorter events, 709.2 us)
Async XLA Ops:
  7.3 89.7 %all-gather.19.cloned.1.call-start = ((), (), s32[]{:S(2)}) async-start(), calls=%async_computation.8 | async-start | bytes 10485760 | tf_op jit(solution)/shard_map/all_gather | solution.py:212
  8.0 206.0 %all-gather.27.cloned.1.call-start = ((), (), s32[]{:S(2)}) async-start(), calls=%async_computation.12 | async-start | bytes 2162688 | tf_op jit(solution)/shard_map/all_gather | solution.py:324
  104.0 138.7 %all-gather.21.cloned.1.call-start = ((), (), s32[]{:S(2)}) async-start(), calls=%async_computation.9 | async-start | bytes 25952256 | tf_op jit(solution)/shard_map/all_gather | solution.py:39
  106.9 6.7 collective-permute-start.1
  110.6 4.0 collective-permute-start
  129.4 206.9 %all-gather.23.cloned.1.call-start = ((), (), s32[]{:S(2)}) async-start(), calls=%async_computation.10 | async-start | bytes 25952256 | tf_op jit(solution)/shard_map/all_gather | solution.py:39
  130.0 441.1 %all-gather.25.cloned.1.call-start = ((), (), s32[]{:S(2)}) async-start(), calls=%async_computation.11 | async-start | bytes 3932160 | tf_op jit(solution)/shard_map/all_gather | solution.py:220
  130.6 444.1 %all-gather.29.cloned.1.call-start = ((), (), s32[]{:S(2)}) async-start(), calls=%async_computation.13 | async-start | bytes 1310720 | tf_op jit(solution)/shard_map/all_gather | solution.py:221
  131.2 445.4 %all-gather.31.cloned.1.call-start = ((), (), s32[]{:S(2)}) async-start(), calls=%async_computation.14 | async-start | bytes 10485760 | tf_op jit(solution)/shard_map/all_gather | solution.py:224
  131.9 450.8 %all-gather.33.cloned.1.call-start = ((), (), s32[]{:S(2)}) async-start(), calls=%async_computation.15 | async-start | bytes 5242880 | tf_op jit(solution)/shard_map/all_gather | solution.py:225
  132.7 606.5 %reduce-scatter.11.cloned.1.call-start = ((), (), s32[]{:S(2)}) async-start(), calls=%async_computation.19 | async-start | bytes 2162688 | tf_op jit(solution)/shard_map/reduce_scatter | solution.py:396
  653.8 142.8 %all-gather.39.cloned.1.call-start = ((), (), s32[]{:S(2)}) async-start(), calls=%async_computation.18 | async-start | bytes 12976128 | tf_op jit(solution)/shard_map/all_gather | solution.py:58
  670.7 219.8 %all-gather.37.cloned.1.call-start = ((), (), s32[]{:S(2)}) async-start(), calls=%async_computation.17 | async-start | bytes 25952256 | tf_op jit(solution)/shard_map/all_gather | solution.py:39
  673.5 310.5 %all-gather.35.cloned.1.call-start = ((), (), s32[]{:S(2)}) async-start(), calls=%async_computation.16 | async-start | bytes 25952256 | tf_op jit(solution)/shard_map/all_gather | solution.py:39
  674.1 529.5 %reduce-scatter.19.cloned.1.call-start = ((), (), s32[]{:S(2)}) async-start(), calls=%async_computation.23 | async-start | bytes 1310720 | tf_op jit(solution)/shard_map/reduce_scatter | solution.py:527
  675.6 528.1 %reduce-scatter.17.cloned.1.call-start = ((), (), s32[]{:S(2)}) async-start(), calls=%async_computation.22 | async-start | bytes 3932160 | tf_op jit(solution)/shard_map/reduce_scatter | solution.py:524
  678.5 525.2 %reduce-scatter.23.cloned.1.call-start = ((), (), s32[]{:S(2)}) async-start(), calls=%async_computation.25 | async-start | bytes 5242880 | tf_op jit(solution)/shard_map/reduce_scatter | solution.py:539
  682.9 520.9 %reduce-scatter.21.cloned.1.call-start = ((), (), s32[]{:S(2)}) async-start(), calls=%async_computation.24 | async-start | bytes 10485760 | tf_op jit(solution)/shard_map/reduce_scatter | solution.py:536
  739.2 537.6 %reduce-scatter.13.cloned.1.call-start = ((), (), s32[]{:S(2)}) async-start(), calls=%async_computation.20 | async-start | bytes 10485760 | tf_op jit(solution)/shard_map/reduce_scatter | solution.py:500
  1169.0 6.5 collective-permute-start.2
  1172.0 5.4 collective-permute-start.3
  1193.6 109.7 %reduce-scatter.25.cloned.1.call-start = ((), (), s32[]{:S(2)}) async-start(), calls=%async_computation.26 | async-start | bytes 573440
  1201.6 119.9 %reduce-scatter.15.cloned.1.call-start = ((), (), s32[]{:S(2)}) async-start(), calls=%async_computation.21 | async-start | bytes 61440 | tf_op jit(solution)/shard_map/reduce_scatter | solution.py:503
  1203.4 247.2 %all-reduce.30.cloned.1.call-start = ((), (), s32[]{:S(2)}) async-start(), calls=%async_computation.27 | async-start | bytes 12582912 | tf_op jit(solution)/shard_map/psum | solution.py:544
  (161 other events, 2925.4 us)
Sparse Core Ops, SparseCore 0:
  9.8 87.1 all-gather.18
  104.1 44.9 all-gather.26
  151.4 91.2 all-gather.20
  244.8 91.3 all-gather.22
  337.8 38.7 all-gather.24
  378.1 23.3 all-gather.28
  403.1 84.6 all-gather.30
  489.4 49.3 all-gather.32
  653.9 75.8 reduce-scatter.10
  732.4 64.1 all-gather.38
  798.9 91.5 all-gather.36
  892.6 91.4 all-gather.34
  986.5 20.6 reduce-scatter.18
  1010.2 40.1 reduce-scatter.16
  1053.3 46.5 reduce-scatter.22
  1102.3 80.2 reduce-scatter.20
  1193.7 82.9 reduce-scatter.12
  1279.5 19.2 reduce-scatter.24
  1301.9 19.5 reduce-scatter.14
  1325.2 118.0 all-reduce.29
where the time goes:
time: 1490 us; the launch traced here: 1470 us
  other arithmetic  455 us (31%)
  waiting for transfers between devices  442 us (30%)
  blocking collectives  262 us (18%)
  matrix products  167 us (11%)
  local copies, waits for them, and re-layouts  109 us (7%)
  between operations  20.7 us (1%)
    select_n x224, other arithmetic, carried_step(): return jax.tree.map(lambda a, b: jnp.where(reached, a, b), new, before)  343 us
    all_gather x4, waiting for transfers between devices, carried_in(): everything = jax.tree.map(lambda part: lax.all_gather(part, axis), shard)  242 us
    psum x1, blocking collectives, per_device(): lax.psum(shard_w_dt.astype(jnp.bfloat16), 'ctx').astype(jnp.float32)  124 us
    reduce_scatter x1, waiting for transfers between devices, per_device(): lax.psum_scatter(grad_w_in.astype(jnp.bfloat16), 'fsdp', scatter_dimensio...  73 us
    all_gather x1, waiting for transfers between devices, prefix(): lax.all_gather(part.astype(kind), axis)  56.5 us
    all_gather x2, blocking collectives, carried_in(): everything = jax.tree.map(lambda part: lax.all_gather(part, axis), shard)  54.5 us
    all_gather x1, waiting for transfers between devices, per_device(): lax.all_gather(w_in, 'fsdp', axis=0, tiled=True)  45.8 us
    select_n x32, other arithmetic, prefix_step(): return jax.tree.map(lambda a, b: jnp.where(reached, a, b), new, before)  38.3 us
  transfers between devices with their start and end apart: 24, of which 10 were waited for; matrix products, arithmetic and copies ran while one was open for 43% of the time, Pallas kernels for 0%

commit v1 on v0

v1 whole, which is shorter than its diff:
```python
import functools
import math

import jax
import jax.numpy as jnp
from jax import lax
from jax.experimental import pallas as pl
from jax.experimental.pallas import tpu as pltpu
from jax.sharding import PartitionSpec as P

D = 1024
FF = 2048
BLK = 64
HDIM = 64
NSTATE = 128
LOCAL_HEADS = 6
LX = 384
LBC = 256
LCONV = LX + LBC
LPROJ = 1280
EXT = 72
EPS = 1e-05
ROPE_BASE = 100000000000.0
NEG = -1e30
F32 = jnp.float32
BF16 = jnp.bfloat16
NN = ((1,), (0,))
NT = ((1,), (1,))
TN = ((0,), (0,))


def dotf(a, b, dims):
    return lax.dot_general(
        a, b, (dims, ((), ())), precision=lax.Precision.HIGHEST, preferred_element_type=F32
    )


def dotb(a, b, dims):
    return lax.dot_general(
        a.astype(BF16), b.astype(BF16), (dims, ((), ())), preferred_element_type=F32
    )


def iota(shape, dim):
    return lax.broadcasted_iota(jnp.int32, shape, dim)


def sigmoid(v):
    return 1.0 / (1.0 + jnp.exp(-v))


def ssd_prep(ext, dtr, st, base, pv):
    tpos = base + iota((BLK, LCONV), 0)
    stc = jnp.broadcast_to(st[:, :1], (BLK, LCONV))
    pre = jnp.broadcast_to(pv[4:5], (BLK, LCONV))
    for tap in range(4):
        use = (tpos - (3 - tap)) >= stc
        pre = pre + jnp.where(use, pv[tap : tap + 1] * ext[5 + tap : 5 + tap + BLK], 0.0)
    sg = sigmoid(pre)
    xc = pre * sg
    lin = dtr + pv[5:6, :128]
    dt = jnp.maximum(lin, 0.0) + jnp.log1p(jnp.exp(-jnp.abs(lin)))
    ea = jnp.exp(pv[6:7, :128])
    ell = -dt * ea
    tri = (iota((BLK, BLK), 1) <= iota((BLK, BLK), 0)).astype(F32)
    eye = (iota((BLK, BLK), 1) == iota((BLK, BLK), 0)).astype(F32)
    run = dotf(tri, ell, NN)
    run_t = dotf(ell, tri, ((0,), (1,)))
    dt_t = dotf(dt, eye, TN)
    allowed = (iota((BLK, BLK), 1) <= iota((BLK, BLK), 0)) & (
        (base + iota((BLK, BLK), 1)) >= st[:, :BLK]
    )
    sw = jnp.where(st < base, jnp.exp(run), 0.0)
    last_ok = (base + iota((BLK, 128), 0)) >= st[BLK - 1 : BLK]
    fwd_decay = jnp.where(
        last_ok, jnp.exp(jnp.where(last_ok, run[BLK - 1 : BLK] - run, 0.0)), 0.0
    )
    sel = (iota((128, LX), 1) // HDIM == iota((128, LX), 0)).astype(F32)
    return dict(
        pre=pre, sg=sg, xc=xc, lin=lin, dt=dt, ea=ea, ell=ell, run=run, run_t=run_t, dt_t=dt_t,
        allowed=allowed, sw=sw, fd=fwd_decay, fw=fwd_decay * dt, sel=sel, tri=tri, tpos=tpos, stc=stc,
    )


def decay_of(p, h):
    spread = p["run"][:, h : h + 1] - p["run_t"][h : h + 1, :]
    return jnp.where(p["allowed"], jnp.exp(jnp.where(p["allowed"], spread, 0.0)), 0.0)


def to_chunks(state, out_ref, nk, pr, extra):
    for k in range(nk):
        rows = [state[h * HDIM + k * pr : h * HDIM + (k + 1) * pr] for h in range(LOCAL_HEADS)]
        out_ref[0, k, 0] = jnp.concatenate(rows + extra, axis=0).astype(BF16)


def from_chunks(ref, nk, pr):
    parts = [ref[0, k, 0].astype(F32) for k in range(nk)]
    rows = []
    for h in range(LOCAL_HEADS):
        for k in range(nk):
            rows.append(parts[k][h * pr : (h + 1) * pr])
    return jnp.concatenate(rows, axis=0)


def block_base(idx_ref, nctx):
    half = pl.program_id(0) % 2
    i = idx_ref[0]
    return jnp.where(half == 0, i, 2 * nctx - 1 - i) * BLK


def ssd_fwd_kernel(nctx, nk, pr, idx_ref, ext_ref, dtr_ref, st_ref, pv_ref, y_ref, swx_ref, c_ref, s_ref):
    base = block_base(idx_ref, nctx)
    st = st_ref[0]
    p = ssd_prep(ext_ref[0], dtr_ref[0, 8:], st, base, pv_ref[...])
    x = p["xc"][:, :LX]
    bm = p["xc"][:, LX : LX + NSTATE].astype(BF16)
    cm = p["xc"][:, LX + NSTATE :].astype(BF16)
    inter = dotb(cm, bm, NT)
    xb = x.astype(BF16)
    outs = []
    for h in range(LOCAL_HEADS):
        mix = decay_of(p, h) * inter * p["dt_t"][h : h + 1]
        outs.append(dotb(mix, xb[:, h * HDIM : (h + 1) * HDIM], NN))
    y_ref[0] = jnp.concatenate(outs, axis=1) + pv_ref[7:8, :LX] * x
    swx_ref[0] = dotf(p["sw"], p["sel"], NN)
    c_ref[0] = cm
    fwx = dotf(p["fw"], p["sel"], NN)
    state = dotb(fwx * x, bm, TN)
    dec = jnp.where(
        st[BLK - 1 : BLK] < base,
        jnp.broadcast_to(jnp.exp(p["run_t"][:8, BLK - 1 : BLK]), (8, 128)),
        0.0,
    )
    high = dec.astype(BF16).astype(F32)
    to_chunks(state, s_ref, nk, pr, [high, dec - high])


def ssd_out_kernel(nk, pr, y_ref, swx_ref, c_ref, s_ref, z_ref, gain_ref, dep_ref, out_ref, u_ref, ss_ref):
    s_in = from_chunks(s_ref, nk, pr)
    y = y_ref[0] + swx_ref[0] * dotb(c_ref[0], s_in, NT)
    z = z_ref[0]
    u = y * (z * sigmoid(z))
    out_ref[0] = y
    u_ref[0] = (u * gain_ref[...]).astype(BF16)
    ss_ref[0] = jnp.broadcast_to(jnp.sum(u * u, axis=1, keepdims=True), (BLK, 128))


def split_in_kernel(w_ref, out_ref):
    for zz in range(4):
        kv = HDIM * (zz // 2)
        out_ref[zz, :, :LX] = w_ref[:, LX * zz : LX * zz + LX]
        out_ref[zz, :, LX : 2 * LX] = w_ref[:, 1536 + LX * zz : 1536 + LX * zz + LX]
        out_ref[zz, :, 2 * LX : 1024] = w_ref[:, 3072:3328]
        out_ref[zz, :, 1024:1152] = w_ref[:, 3328 + 128 * zz : 3456 + 128 * zz]
        out_ref[zz, :, 1152:1280] = jnp.concatenate(
            [w_ref[:, 3840 + kv : 3904 + kv], w_ref[:, 3968 + kv : 4032 + kv]], axis=1
        )


def split_gate_up_kernel(w_ref, out_ref):
    for zz in range(4):
        out_ref[zz, :, :512] = w_ref[:, 512 * zz : 512 * zz + 512]
        out_ref[zz, :, 512:] = w_ref[:, FF + 512 * zz : FF + 512 * zz + 512]


def total_kernel(n, got_ref, *refs):
    out_ref = refs[-1]

    def step(j, acc):
        return acc + got_ref[j].astype(F32)

    out_ref[...] = lax.fori_loop(1, n, step, got_ref[0].astype(F32))


def leak_kernel(nk, pr, dy_ref, swx_ref, c_ref, out_ref):
    to_chunks(dotb(swx_ref[0] * dy_ref[0], c_ref[0], TN), out_ref, nk, pr, [])


def ssd_bwd_kernel(
    nctx, nk, pr, idx_ref, ext_ref, dtr_ref, st_ref, pv_ref, dy_ref, s_ref, g_ref, *refs
):
    dext_ref, ddt_ref, misc_ref = refs[-3:]
    base = block_base(idx_ref, nctx)
    st = st_ref[0]
    ext = ext_ref[0]
    pv = pv_ref[...]
    p = ssd_prep(ext, dtr_ref[0, 8:], st, base, pv)
    sel = p["sel"]
    x = p["xc"][:, :LX]
    bm = p["xc"][:, LX : LX + NSTATE]
    cm = p["xc"][:, LX + NSTATE :]
    bmb, cmb, xb = bm.astype(BF16), cm.astype(BF16), x.astype(BF16)
    dy = dy_ref[0]
    dyb = dy.astype(BF16)
    s_in = from_chunks(s_ref, nk, pr)
    g_out = from_chunks(g_ref, nk, pr)
    s_inb, g_outb = s_in.astype(BF16), g_out.astype(BF16)
    inter = dotb(cmb, bmb, NT)
    swx = dotf(p["sw"], sel, NN)
    fwx = dotf(p["fw"], sel, NN)
    skip = pv[7:8, :LX]
    lane = iota((BLK, 128), 1)
    d_inter = jnp.zeros((BLK, BLK), F32)
    drun = jnp.zeros((BLK, 128), F32)
    dx_parts = []
    col_rows = []
    for h in range(LOCAL_HEADS):
        sl = slice(h * HDIM, (h + 1) * HDIM)
        dec = decay_of(p, h)
        dt_row = p["dt_t"][h : h + 1]
        dec_inter = dec * inter
        d_mix = dotb(dyb[:, sl], xb[:, sl], NT)
        dx_parts.append(dotb(dec_inter * dt_row, dyb[:, sl], TN))
        d_inter = d_inter + d_mix * dec * dt_row
        f = d_mix * dec_inter
        row = jnp.sum(f * dt_row, axis=1, keepdims=True)
        drun = drun + jnp.where(lane == h, row, 0.0)
        col_rows.append(jnp.sum(f, axis=0, keepdims=True))
    col_rows.append(jnp.zeros((2, BLK), F32))
    cols = jnp.concatenate(col_rows, axis=0)
    pick = (iota((8, 128), 0) == iota((8, 128), 1)).astype(F32)
    col = dotf(cols, pick, TN)
    ddt = col
    drun = drun - p["dt"] * col
    dx = jnp.concatenate(dx_parts, axis=1) + skip * dy
    dcm = dotb(d_inter, bmb, NN)
    dbm = dotb(d_inter, cmb, TN)
    swdy = swx * dy
    yin = dotb(cmb, s_inb, NT)
    drun = drun + dotf(swdy * yin, sel, NT)
    dcm = dcm + dotb(swdy, s_inb, NN)
    back = dotb(bmb, g_outb, NT)
    dbm = dbm + dotb(fwx * x, g_outb, NN)
    dx = dx + fwx * back
    dfw = dotf(x * back, sel, NT)
    ddt = ddt + dfw * p["fd"]
    tail = dfw * p["fw"]
    drun = drun - tail
    carry = jnp.sum(s_in * g_out, axis=1, keepdims=True)
    sel_t = (iota((LX, 128), 0) // HDIM == iota((LX, 128), 1)).astype(F32)
    last = jnp.sum(tail, axis=0, keepdims=True) + p["sw"][BLK - 1 : BLK] * jnp.sum(
        carry * sel_t, axis=0, keepdims=True
    )
    drun = drun + jnp.where(iota((BLK, 128), 0) == BLK - 1, last, 0.0)
    dell = dotf(p["tri"], drun, TN)
    ddt = ddt - p["ea"] * dell
    ddtraw = ddt * sigmoid(p["lin"])
    ddtraw = jnp.where(lane < LOCAL_HEADS, ddtraw, 0.0)
    zero8 = jnp.zeros((8, 128), F32)
    ddt_ref[0] = jnp.concatenate([zero8, ddtraw], axis=0).astype(BF16)
    dxc = jnp.concatenate([dx, dbm, dcm], axis=1)
    dpre = dxc * (p["sg"] * (1.0 + p["pre"] * (1.0 - p["sg"])))
    dext = jnp.zeros((EXT, LCONV), F32)
    rows = []
    for tap in range(4):
        use = (p["tpos"] - (3 - tap)) >= p["stc"]
        term = jnp.where(use, dpre, 0.0)
        rows.append(jnp.sum(term * ext[5 + tap : 5 + tap + BLK], axis=0, keepdims=True))
        term = term * pv[tap : tap + 1]
        pieces = [jnp.zeros((5 + tap, LCONV), F32), term]
        if tap < 3:
            pieces.append(jnp.zeros((3 - tap, LCONV), F32))
        dext = dext + jnp.concatenate(pieces, axis=0)
    dext_ref[0] = dext.astype(BF16)
    rows.append(jnp.sum(dpre, axis=0, keepdims=True))
    pad = jnp.zeros((1, LCONV - LX), F32)
    rows.append(jnp.concatenate([jnp.sum(dy * x, axis=0, keepdims=True), pad], axis=1))
    pad = jnp.zeros((1, LCONV - 128), F32)
    rows.append(jnp.concatenate([jnp.sum(ddtraw, axis=0, keepdims=True), pad], axis=1))
    rows.append(jnp.concatenate([jnp.sum(dell * p["ell"], axis=0, keepdims=True), pad], axis=1))
    misc_ref[0] = jnp.concatenate(rows, axis=0)


def scan_kernel(reverse, n, pr, st_ref, dec_ref, dep_ref, out_ref):
    rows = LOCAL_HEADS * pr

    def step(j, half, s):
        out_ref[j, half] = s.astype(BF16)
        d = dec_ref[j, half, rows : rows + 16].astype(F32)
        d = d[:LOCAL_HEADS] + d[8 : 8 + LOCAL_HEADS]
        d = jnp.broadcast_to(d[:, None, :], (LOCAL_HEADS, pr, 128)).reshape(rows, 128)
        return d * s + st_ref[j, half, :rows].astype(F32)

    first, second = (1, 0) if reverse else (0, 1)
    s = jnp.zeros((rows, 128), F32)
    s = lax.fori_loop(0, n, lambda j, s: step(j, first, s), s)
    lax.fori_loop(0, n, lambda j, s: step(n - 1 - j, second, s), s)


def unit_of(u, gi):
    if u < 4:
        return 1, 0, u
    is_a = u < 5 + gi
    rowset = jnp.where(is_a, 0, 1)
    half = jnp.where(is_a, 0, 1)
    return rowset, half, jnp.where(is_a, u - 4, u - 5)


def unit_mask(nctx, gs, i, rowset, half, g, st):
    shape = (2 * BLK, gs * BLK)
    row = iota(shape, 0) % BLK
    col = iota(shape, 1)
    qpos = jnp.where(rowset == 0, i, 2 * nctx - 1 - i) * BLK + row
    block = g * gs + col // BLK
    kpos = jnp.where(half == 0, block, 2 * nctx - 1 - block) * BLK + col % BLK
    return (kpos <= qpos) & (kpos >= st)


def attn_fwd_kernel(nctx, gs, idx_ref, q_ref, kv_ref, st_ref, dep_a, dep_b, o_ref, lse_ref, s_ref, m_ref, l_ref, acc_ref):
    i = idx_ref[0]
    gi = i // gs
    m_ref[...] = jnp.full(m_ref.shape, NEG, F32)
    l_ref[...] = jnp.zeros(l_ref.shape, F32)
    acc_ref[...] = jnp.zeros(acc_ref.shape, F32)
    for u in range(9):
        rowset, half, g = unit_of(u, gi)
        kv = kv_ref[pl.ds(g * gs, gs), 0, half].reshape(gs * BLK, 128)
        s = dotb(q_ref[0, rowset], kv[:, :HDIM], NT)
        ok = unit_mask(nctx, gs, i, rowset, half, g, st_ref[0, rowset, :, :1])
        s = jnp.where(ok, s, NEG)
        s_ref[u] = s
        m_ref[rowset] = jnp.maximum(m_ref[rowset], jnp.max(s, axis=1, keepdims=True))
    for u in range(9):
        rowset, half, g = unit_of(u, gi)
        kv = kv_ref[pl.ds(g * gs, gs), 0, half].reshape(gs * BLK, 128)
        w = jnp.exp(s_ref[u] - m_ref[rowset, :, :1])
        l_ref[rowset] = l_ref[rowset] + jnp.sum(w, axis=1, keepdims=True)
        acc_ref[rowset] = acc_ref[rowset] + dotb(w, kv[:, HDIM:], NN)
    o_ref[0] = acc_ref[...] / l_ref[:, :, :HDIM]
    lse_ref[0] = m_ref[...] + jnp.log(l_ref[...])


def attn_bwd_kernel(
    nctx, gs, idx_ref, q_ref, kv_ref, st_ref, o_ref, lse_ref, do_ref, dq_ref, dkv_ref, del_ref, acc_ref
):
    i = idx_ref[0]
    gi = i // gs
    acc_ref[...] = jnp.zeros(acc_ref.shape, F32)
    dq_ref[...] = jnp.zeros(dq_ref.shape, F32)
    delta = jnp.sum(do_ref[0].astype(F32) * o_ref[0], axis=2, keepdims=True)
    del_ref[...] = jnp.broadcast_to(delta, del_ref.shape)
    for u in range(9):
        rowset, half, g = unit_of(u, gi)
        kv = kv_ref[pl.ds(g * gs, gs), 0, half].reshape(gs * BLK, 128)
        q = q_ref[0, rowset]
        do = do_ref[0, rowset]
        s = dotb(q, kv[:, :HDIM], NT)
        ok = unit_mask(nctx, gs, i, rowset, half, g, st_ref[0, rowset, :, :1])
        prob = jnp.exp(jnp.where(ok, s, NEG) - lse_ref[0, rowset, :, :1])
        dp = dotb(do, kv[:, HDIM:], NT)
        ds = (prob * (dp - del_ref[rowset, :, :1])).astype(BF16)
        dkv = jnp.concatenate([dotb(ds, q, TN), dotb(prob, do, TN)], axis=1)
        acc_ref[half, g] = acc_ref[half, g] + dkv
        dq_ref[0, rowset] = dq_ref[0, rowset] + dotb(ds, kv[:, :HDIM], NN)
    dq_ref[...] = dq_ref[...] * (HDIM**-0.5)
    for g in range(4):
        for half in range(2):
            dkv_ref[g * gs : (g + 1) * gs, 0, half] = (
                acc_ref[half, g].astype(BF16).reshape(gs, BLK, 128)
            )


def spec(shape, index):
    return pl.BlockSpec(shape, index)


def per_pair(shape):
    return pl.BlockSpec((1,) + shape, lambda j: (j,) + (0,) * len(shape))


def whole(shape):
    return pl.BlockSpec(shape, lambda *j: (0,) * len(shape))


def chunk_spec(nk, rows):
    return pl.BlockSpec((1, nk, 1, rows, 128), lambda j: (j // 2, 0, j % 2, 0, 0))


ANY = pl.BlockSpec(memory_space=pl.ANY)
VMEM = pl.BlockSpec(memory_space=pltpu.VMEM)
SMEM = pl.BlockSpec(memory_space=pltpu.SMEM)
PARAMS = pltpu.CompilerParams(vmem_limit_bytes=48 * 1024 * 1024)


def cost(flops, moved, trans=0):
    return pl.CostEstimate(flops=flops // 1000, bytes_accessed=moved // 1000, transcendentals=0)


def sds(shape, dtype):
    return jax.ShapeDtypeStruct(shape, dtype)


def exchange(parts, axis):
    return lax.all_to_all(parts, axis, 0, 0, tiled=True)


def spread(part, axis):
    return exchange(jnp.broadcast_to(part[None], (lax.axis_size(axis),) + part.shape), axis)


def shifts():
    return [(k, [(a, (a + k) % 4) for a in range(4)]) for k in (1, 2, 3)]


def ring_exchange(parts, z):
    out = parts
    for k, perm in shifts():
        sent = lax.dynamic_index_in_dim(parts, (z + k) % 4, 0, keepdims=False)
        got = lax.ppermute(sent, "fsdp", perm)
        out = lax.dynamic_update_index_in_dim(out, got, (z - k) % 4, 0)
    return out


def ring_spread(part, z):
    out = jnp.broadcast_to(part[None], (4,) + part.shape)
    for k, perm in shifts():
        got = lax.ppermute(part, "fsdp", perm)
        out = lax.dynamic_update_index_in_dim(out, got, (z - k) % 4, 0)
    return out


def ring_sum(rows, z):
    parts = rows.astype(BF16).reshape((4, -1) + rows.shape[1:])
    total = lax.dynamic_index_in_dim(parts, z, 0, keepdims=False).astype(F32)
    for k, perm in shifts():
        sent = lax.dynamic_index_in_dim(parts, (z + k) % 4, 0, keepdims=False)
        total = total + lax.ppermute(sent, "fsdp", perm).astype(F32)
    return total


def as_rows(column):
    high = lax.reduce_precision(column, 8, 7)
    pair = jnp.stack([high, column - high], axis=-2).astype(BF16)
    pads = [(0, 0)] * (pair.ndim - 2) + [(0, 14), (0, D - 128)]
    return jnp.pad(pair, pads)


def from_rows(rows):
    pair = rows[..., :2, :128].astype(F32)
    return pair[..., 0, :] + pair[..., 1, :]


def rms_of(v):
    return lax.rsqrt(jnp.mean(v * v, axis=-1, keepdims=True) + EPS)


def rms_back(v, r, dn):
    n = v * r
    return r * (dn - n * jnp.mean(dn * n, axis=-1, keepdims=True))


def turn(values, cosine, sine):
    a, b = values[..., : HDIM // 2], values[..., HDIM // 2 :]
    return jnp.concatenate([a * cosine - b * sine, b * cosine + a * sine], axis=-1)


def matmul(a, b, dims=NN):
    return lax.dot_general(a, b, (dims, ((), ())), preferred_element_type=F32)


def per_device(
    tokens,
    doc_start,
    cotangent,
    w_in,
    w_dt,
    conv_weight,
    conv_bias,
    dt_bias,
    a_log,
    skip_gain,
    inner_gain,
    mamba_out,
    attn_out,
    mixer_gain,
    ffn_gain,
    w_gate_up,
    w_down,
):
    nctx = lax.axis_size("ctx")
    i = lax.axis_index("ctx")
    z = lax.axis_index("fsdp")
    nk = nctx // 4
    pr = HDIM // nk
    gs = nctx // 4
    rpc = 256 // nctx
    idx = i.astype(jnp.int32).reshape(1)
    last_device = i == nctx - 1
    up = [(a, a + 1) for a in range(nctx - 1)]
    down = [(b, a) for a, b in up]

    send_in = pl.pallas_call(
        split_in_kernel,
        in_specs=[VMEM],
        out_specs=VMEM,
        out_shape=sds((4, 256, LPROJ), BF16),
        compiler_params=PARAMS,
        cost_estimate=cost(0, 5 * 10**6),
        name="split_in",
    )(w_in)
    send_gu = pl.pallas_call(
        split_gate_up_kernel,
        in_specs=[VMEM],
        out_specs=VMEM,
        out_shape=sds((4, 256, 1024), BF16),
        compiler_params=PARAMS,
        cost_estimate=cost(0, 4 * 10**6),
        name="split_gate_up",
    )(w_gate_up)
    tok = tokens[0]
    tails = tok[:, BLK - 3 :, :]
    halo_first = lax.ppermute(tails[0], "ctx", up)
    halo_second = lax.ppermute(tails[1], "ctx", down)
    halo = jnp.stack([halo_first, jnp.where(last_device, tails[0], halo_second)])
    starts_own = doc_start[0]
    flat = jnp.concatenate(
        [
            w_dt.reshape(-1),
            conv_weight.reshape(-1),
            conv_bias,
            mixer_gain,
            ffn_gain,
            (starts_own // 64).astype(BF16).reshape(-1),
            (starts_own % 64).astype(BF16).reshape(-1),
        ]
    )
    flat = jnp.pad(flat, (0, 10 * D - flat.shape[0])).reshape(2, 5, D)
    wide = spread(jnp.concatenate([flat, halo, tok], axis=1), "fsdp")
    own_in = exchange(send_in, "fsdp").reshape(D, LPROJ)
    own_gu = ring_exchange(send_gu, z).reshape(D, 1024)
    grad_own = cotangent[0].reshape(128, D)
    grad_all = ring_spread(grad_own, z).reshape(512, D)
    flat = wide[:, :, :5, :].reshape(4, 10 * D)
    full_dt = flat[:, :6144].reshape(D, 24)
    own_dt = jnp.pad(lax.dynamic_slice_in_dim(full_dt, 6 * z, 6, axis=1), ((0, 0), (0, 122)))
    full_conv = flat[:, 6144:7936].reshape(4, 4, 448).transpose(1, 0, 2).reshape(4, 1792)
    full_bias = flat[:, 7936:8384].reshape(1, 1792)
    full_taps = jnp.concatenate([full_conv, full_bias], axis=0).astype(F32)
    mixer_scale = flat[:, 8384:8640].reshape(D).astype(F32)
    ffn_scale = flat[:, 8640:8896].reshape(D).astype(F32)
    starts = (
        flat[:, 8896:9024].astype(jnp.int32) * 64 + flat[:, 9024:9152].astype(jnp.int32)
    ).reshape(8, BLK)
    own_taps = jnp.concatenate(
        [lax.dynamic_slice_in_dim(full_taps, LX * z, LX, axis=1), full_taps[:, 1536:]], axis=1
    )

    def lanes(v):
        return jnp.pad(v.astype(F32), (0, LCONV - v.shape[0]))[None]

    pv = jnp.concatenate(
        [own_taps, lanes(dt_bias), lanes(a_log), lanes(jnp.repeat(skip_gain, HDIM))], axis=0
    )
    inner_scale = inner_gain.astype(F32)

    rows = 8 * EXT
    hidden_all = wide.reshape(rows, D).astype(F32)
    norm_one = hidden_all * rms_of(hidden_all)
    act_one = (norm_one * mixer_scale).astype(BF16)
    projected = matmul(act_one, own_in).reshape(8, EXT, LPROJ)
    raw_dt = matmul(act_one, own_dt).reshape(8, EXT, 128)
    gate_z = projected[:, 8:, :LX]
    conv_ext = projected[:, :, LX : LX + LCONV]

    blocks = jnp.stack([i, 2 * nctx - 1 - i])
    positions = blocks[:, None] * BLK + jnp.arange(BLK, dtype=jnp.int32)[None, :]
    freq = jnp.exp(
        jnp.arange(HDIM // 2, dtype=F32) * (-2.0 * math.log(ROPE_BASE) / HDIM)
    )
    angle = positions.astype(F32)[:, :, None] * freq
    cosine, sine = jnp.cos(angle), jnp.sin(angle)
    tables = (cosine[None, :, :, None, :], sine[None, :, :, None, :])
    query = projected[:, 8:, 1024:1152].reshape(4, 2, BLK, 2, HDIM)
    query = turn(query, *tables).astype(BF16) * jnp.asarray(HDIM**-0.5, BF16)
    query = query.transpose(0, 1, 3, 2, 4).reshape(4, 2, 2 * BLK, HDIM)
    key = projected[:, 8:, 1152:1216].reshape(4, 2, BLK, 1, HDIM)
    key = turn(key, *tables).astype(BF16).reshape(4, 2, BLK, HDIM)
    value = projected[:, 8:, 1216:1280].astype(BF16).reshape(4, 2, BLK, HDIM)
    kv_own = jnp.concatenate([key, value], axis=-1)

    st_wide = jnp.broadcast_to(starts[:, :, None], (8, BLK, 128))
    srows = LOCAL_HEADS * pr
    ssd_in = (idx, conv_ext, raw_dt, st_wide, pv)
    ssd_in_specs = [
        SMEM,
        per_pair((EXT, LCONV)),
        per_pair((EXT, 128)),
        per_pair((BLK, 128)),
        whole((8, LCONV)),
    ]
    y_local, swx, c_mat, state_out = pl.pallas_call(
        functools.partial(ssd_fwd_kernel, nctx, nk, pr),
        grid=(8,),
        in_specs=ssd_in_specs,
        out_specs=[
            per_pair((BLK, LX)),
            per_pair((BLK, LX)),
            per_pair((BLK, 128)),
            chunk_spec(nk, srows + 16),
        ],
        out_shape=[
            sds((8, BLK, LX), F32),
            sds((8, BLK, LX), F32),
            sds((8, BLK, 128), BF16),
            sds((4, nk, 2, srows + 16, 128), BF16),
        ],
        compiler_params=PARAMS,
        cost_estimate=cost(2 * 10**9, 6 * 10**6),
        name="ssd_fwd",
    )(*ssd_in)
    got = exchange(state_out.reshape(nctx, 2, srows + 16, 128), "ctx")
    kv_all = lax.all_gather(kv_own, "ctx")

    def chain(reverse, terms, after):
        return pl.pallas_call(
            functools.partial(scan_kernel, reverse, nctx, pr),
            in_specs=[VMEM, VMEM, ANY],
            out_specs=VMEM,
            out_shape=sds((nctx, 2, srows, 128), BF16),
            compiler_params=PARAMS,
            cost_estimate=cost(10**7, 3 * 10**6),
            name="chain",
        )(terms, got, after)

    entry = exchange(chain(False, got, kv_all), "ctx").reshape(4, nk, 2, srows, 128)

    st_rows = jnp.broadcast_to(
        starts.reshape(4, 2, 1, BLK, 1), (4, 2, 2, BLK, 128)
    ).reshape(4, 2, 2 * BLK, 128)
    row_spec = pl.BlockSpec((1, 2, 2 * BLK, HDIM), lambda s: (s, 0, 0, 0))
    wide_spec = pl.BlockSpec((1, 2, 2 * BLK, 128), lambda s: (s, 0, 0, 0))
    kv_spec = pl.BlockSpec((nctx, 1, 2, BLK, 128), lambda s: (0, s, 0, 0, 0))
    attn_o, lse = pl.pallas_call(
        functools.partial(attn_fwd_kernel, nctx, gs),
        grid=(4,),
        in_specs=[SMEM, row_spec, kv_spec, wide_spec, ANY, ANY],
        out_specs=[row_spec, wide_spec],
        out_shape=[sds((4, 2, 2 * BLK, HDIM), F32), sds((4, 2, 2 * BLK, 128), F32)],
        scratch_shapes=[
            pltpu.VMEM((9, 2 * BLK, gs * BLK), F32),
            pltpu.VMEM((2, 2 * BLK, 128), F32),
            pltpu.VMEM((2, 2 * BLK, 128), F32),
            pltpu.VMEM((2, 2 * BLK, HDIM), F32),
        ],
        compiler_params=PARAMS,
        cost_estimate=cost(4 * 10**9, 8 * 10**6, 2 * 10**6),
        name="attn_fwd",
    )(idx, query, kv_all, st_rows, own_gu, grad_all)
    act_attn = (
        attn_o.reshape(4, 2, 2, BLK, HDIM).transpose(0, 1, 3, 2, 4).reshape(512, 128).astype(BF16)
    )

    mamba_y, scaled_u, squares = pl.pallas_call(
        functools.partial(ssd_out_kernel, nk, pr),
        grid=(8,),
        in_specs=[
            per_pair((BLK, LX)),
            per_pair((BLK, LX)),
            per_pair((BLK, 128)),
            chunk_spec(nk, srows),
            per_pair((BLK, LX)),
            whole((1, LX)),
            ANY,
        ],
        out_specs=[per_pair((BLK, LX)), per_pair((BLK, LX)), per_pair((BLK, 128))],
        out_shape=[
            sds((8, BLK, LX), F32),
            sds((8, BLK, LX), BF16),
            sds((8, BLK, 128), F32),
        ],
        compiler_params=PARAMS,
        cost_estimate=cost(10**9, 6 * 10**6),
        name="ssd_out",
    )(y_local, swx, c_mat, entry, gate_z, inner_scale[None], attn_o)

    def gather_sum(part_rows):
        got_rows = exchange(part_rows.astype(BF16).reshape((4, -1) + part_rows.shape[1:]), "fsdp")
        return jnp.sum(got_rows.astype(F32), axis=0)

    attn_mid = ring_sum(matmul(act_attn, attn_out), z)
    scaled_part = matmul(scaled_u.reshape(512, LX), mamba_out).astype(BF16).reshape(4, 128, D)
    square_rows = as_rows(squares[:, :, 0].reshape(4, 128))
    got_part = exchange(jnp.concatenate([scaled_part, square_rows], axis=1), "fsdp")
    scaled_mid = jnp.sum(got_part[:, :128].astype(F32), axis=0)
    square_sum = jnp.sum(from_rows(got_part[:, 128:]), axis=0)
    own_r = lax.rsqrt(square_sum.reshape(128, 1) * (1.0 / 1536) + EPS)
    mamba_mid = scaled_mid * own_r
    middle = tok.reshape(128, D).astype(F32) + mamba_mid + attn_mid
    mid_r = rms_of(middle)
    norm_two = middle * mid_r
    def spread_rows(values, column):
        sent = jnp.concatenate([values.astype(BF16), as_rows(column.reshape(128))], axis=0)
        got_rows = spread(sent, "fsdp").reshape(4, 144, D)
        return got_rows[:, :128].reshape(512, D), from_rows(got_rows[:, 128:]).reshape(512, 1)

    act_two, inner_r = spread_rows(norm_two * ffn_scale, own_r)
    y_flat = mamba_y.reshape(512, LX)
    z_flat = gate_z.reshape(512, LX)
    z_sig = sigmoid(z_flat)
    z_silu = z_flat * z_sig
    norm_in = y_flat * z_silu * inner_r
    act_mamba = (norm_in * inner_scale).astype(BF16)

    gate_up = matmul(act_two, own_gu)
    gate_val, up_val = gate_up[:, :512], gate_up[:, 512:]
    gate_sig = sigmoid(gate_val)
    gate_silu = gate_val * gate_sig
    inner = (gate_silu * up_val).astype(BF16)
    grad_inner = matmul(grad_all, w_down, NT)
    grad_gate = grad_inner * up_val * (gate_sig * (1.0 + gate_val * (1.0 - gate_sig)))
    grad_gu = jnp.concatenate([grad_gate, grad_inner * gate_silu], axis=1).astype(BF16)
    grad_act_two = gather_sum(matmul(grad_gu, own_gu, NT))
    mixed = (middle + ring_sum(matmul(inner, w_down), z)).astype(BF16).reshape(1, 2, BLK, D)
    grad_down = matmul(inner, grad_all, TN).astype(BF16)
    grad_gate_up = matmul(act_two, grad_gu, TN).astype(BF16)
    grad_ffn_gain = jnp.sum(grad_act_two * norm_two, axis=0)
    grad_middle = grad_own.astype(F32) + rms_back(middle, mid_r, grad_act_two * ffn_scale)
    own_mix = grad_middle.astype(BF16)
    own_dots = jnp.sum(own_mix.astype(F32) * mamba_mid, axis=1) * (1.0 / 1536)
    grad_mix, dots = spread_rows(own_mix, own_dots)

    grad_m = matmul(grad_mix, mamba_out, NT)
    grad_n = grad_m * inner_scale
    grad_attn = matmul(grad_mix, attn_out, NT).astype(BF16)
    grad_attn = (
        grad_attn.reshape(4, 2, BLK, 2, HDIM).transpose(0, 1, 3, 2, 4).reshape(4, 2, 2 * BLK, HDIM)
    )
    grad_mamba_out = matmul(act_mamba, grad_mix, TN).astype(BF16)
    grad_attn_out = matmul(act_attn, grad_mix, TN).astype(BF16)
    totals = lax.psum((grad_gate_up, grad_down, grad_mamba_out, grad_attn_out), "ctx")
    total_gate_up, total_down, total_mamba_out, total_attn_out = totals
    total_gate_up = ring_exchange(total_gate_up.reshape(4, 256, 1024), z)
    total_gate_up = total_gate_up.reshape(4, 256, 2, 512).transpose(1, 2, 0, 3).reshape(256, 4096)
    grad_inner_gain = jnp.sum(grad_m * norm_in, axis=0)
    grad_u = inner_r * (grad_n - norm_in * dots)
    grad_y = (grad_u * z_silu).reshape(8, BLK, LX)
    grad_z = grad_u * y_flat * (z_sig * (1.0 + z_flat * (1.0 - z_sig)))

    leak = pl.pallas_call(
        functools.partial(leak_kernel, nk, pr),
        grid=(8,),
        in_specs=[per_pair((BLK, LX)), per_pair((BLK, LX)), per_pair((BLK, 128))],
        out_specs=chunk_spec(nk, srows),
        out_shape=sds((4, nk, 2, srows, 128), BF16),
        compiler_params=PARAMS,
        cost_estimate=cost(10**9, 4 * 10**6),
        name="leak",
    )(grad_y, swx, c_mat)
    got_leak = exchange(leak.reshape(nctx, 2, srows, 128), "ctx")
    grad_query, grad_kv = pl.pallas_call(
        functools.partial(attn_bwd_kernel, nctx, gs),
        grid=(4,),
        in_specs=[SMEM, row_spec, kv_spec, wide_spec, row_spec, wide_spec, row_spec],
        out_specs=[row_spec, kv_spec],
        out_shape=[sds((4, 2, 2 * BLK, HDIM), F32), sds((nctx, 4, 2, BLK, 128), BF16)],
        scratch_shapes=[
            pltpu.VMEM((2, 2 * BLK, 128), F32),
            pltpu.VMEM((2, 4, gs * BLK, 128), F32),
        ],
        compiler_params=PARAMS,
        cost_estimate=cost(8 * 10**9, 16 * 10**6, 2 * 10**6),
        name="attn_bwd",
    )(idx, query, kv_all, st_rows, attn_o, lse, grad_attn)
    grad_exit = exchange(chain(True, got_leak, grad_kv), "ctx").reshape(4, nk, 2, srows, 128)
    grad_kv = pl.pallas_call(
        functools.partial(total_kernel, nctx),
        in_specs=[VMEM] + [ANY] * 4,
        out_specs=VMEM,
        out_shape=sds((4, 2, BLK, 128), F32),
        compiler_params=PARAMS,
        cost_estimate=cost(2 * 10**6, 4 * 10**6),
        name="total_kv",
    )(exchange(grad_kv, "ctx"), *totals)
    back = (tables[0], -tables[1])
    grad_key = turn(grad_kv[..., :HDIM].reshape(4, 2, BLK, 1, HDIM), *back).reshape(8, BLK, HDIM)
    grad_value = grad_kv[..., HDIM:].reshape(8, BLK, HDIM)
    grad_query = grad_query.reshape(4, 2, 2, BLK, HDIM).transpose(0, 1, 3, 2, 4)
    grad_query = turn(grad_query, *back).reshape(8, BLK, 128)

    grad_ext, grad_dt, misc = pl.pallas_call(
        functools.partial(ssd_bwd_kernel, nctx, nk, pr),
        grid=(8,),
        in_specs=ssd_in_specs
        + [per_pair((BLK, LX)), chunk_spec(nk, srows), chunk_spec(nk, srows)],
        out_specs=[per_pair((EXT, LCONV)), per_pair((EXT, 128)), per_pair((8, LCONV))],
        out_shape=[
            sds((8, EXT, LCONV), BF16),
            sds((8, EXT, 128), BF16),
            sds((8, 8, LCONV), F32),
        ],
        compiler_params=PARAMS,
        cost_estimate=cost(4 * 10**9, 8 * 10**6),
        name="ssd_bwd",
    )(*ssd_in, grad_y, entry, grad_exit)

    def lead(v):
        return jnp.pad(v.astype(BF16), ((0, 0), (8, 0), (0, 0)))

    grad_proj = jnp.concatenate(
        [
            lead(grad_z.reshape(8, BLK, LX)),
            grad_ext,
            lead(jnp.concatenate([grad_query, grad_key, grad_value], axis=-1)),
        ],
        axis=-1,
    ).reshape(rows, LPROJ)
    grad_dt = grad_dt.reshape(rows, 128)
    grad_act = matmul(grad_proj, own_in, NT) + matmul(grad_dt, own_dt, NT)

    got_act = ring_sum(grad_act, z).reshape(2, EXT, D)
    halo_back = got_act[:, 5:8].astype(BF16)
    to_first = lax.ppermute(halo_back[0], "ctx", down).astype(F32)
    to_second = lax.ppermute(jnp.where(last_device, 0.0, halo_back[1]), "ctx", up).astype(F32)
    to_first = to_first + jnp.where(last_device, got_act[1, 5:8], 0.0)
    tail_add = jnp.pad(jnp.stack([to_first, to_second]), ((0, 0), (BLK - 3, 0), (0, 0)))
    own_act = (got_act[:, 8:] + tail_add).reshape(128, D)
    hidden = tok.reshape(128, D).astype(F32)
    grad_tokens = grad_middle + rms_back(hidden, rms_of(hidden), own_act * mixer_scale)
    grad_tokens = grad_tokens.reshape(1, 2, BLK, D)

    def permuted(v):
        return v.reshape(4, nctx, rpc, -1).swapaxes(0, 1)

    grad_in = matmul(act_one, grad_proj, TN).astype(BF16)
    grad_dtw = matmul(act_one, grad_dt, TN)
    misc = jnp.sum(misc, axis=0)
    grad_skip = jnp.sum(misc[5, :LX].reshape(LOCAL_HEADS, HDIM), axis=1)
    small = jnp.concatenate(
        [misc[:5].reshape(-1), misc[6, :6], misc[7, :6], grad_skip, grad_inner_gain]
    )
    small = jnp.pad(small, (0, 3840 - small.shape[0])).reshape(1, 256, 15)
    small = jnp.broadcast_to(small, (4, 256, 15)).reshape(D, 15)
    grad_mixer_gain = jnp.sum(grad_act * norm_one, axis=0)
    extras = jnp.concatenate(
        [
            grad_dtw[:, :6],
            grad_mixer_gain[:, None],
            grad_ffn_gain[:, None],
            small,
            jnp.zeros((D, 105), F32),
        ],
        axis=1,
    ).astype(BF16)
    sent = permuted(jnp.concatenate([grad_in, extras], axis=1))
    summed = pl.pallas_call(
        functools.partial(total_kernel, nctx),
        in_specs=[VMEM],
        out_specs=VMEM,
        out_shape=sds((4, rpc, LPROJ + 128), F32),
        compiler_params=PARAMS,
        cost_estimate=cost(2 * 10**6, 4 * 10**6),
        name="total",
    )(exchange(sent, "ctx"))
    owned = exchange(summed, "fsdp")

    def side(lo, hi):
        return jnp.concatenate([owned[zz, :, lo:hi] for zz in range(4)], axis=1)

    def shared(lo, hi):
        return jnp.concatenate(
            [owned[0, :, lo:hi] + owned[1, :, lo:hi], owned[2, :, lo:hi] + owned[3, :, lo:hi]], axis=1
        )

    final = jnp.concatenate(
        [
            side(0, 384),
            side(384, 768),
            jnp.sum(owned[:, :, 768:1024], axis=0),
            side(1024, 1152),
            shared(1152, 1216),
            shared(1216, 1280),
            side(1280, 1304),
            jnp.zeros((rpc, 32), F32),
        ],
        axis=1,
    ).astype(BF16)
    final = spread(final, "ctx").reshape(256, 4224).astype(F32)
    total_in = final[:, :4096]
    extra = final[:, 4096:4192].reshape(256, 4, 24)
    total_dt = extra[:, :, :6].reshape(256, 24)
    total_mixer = jnp.sum(extra[:, :, 6], axis=1)
    total_ffn = jnp.sum(extra[:, :, 7], axis=1)
    small = extra[:, :, 8:23].transpose(1, 0, 2).reshape(4, 3840)
    taps = small[:, :3200].reshape(4, 5, LCONV)
    taps = jnp.concatenate(
        [
            taps[:, :, :LX].transpose(1, 0, 2).reshape(5, 1536),
            jnp.sum(taps[:, :, LX:], axis=0),
        ],
        axis=1,
    )
    taps = lax.dynamic_slice_in_dim(taps, 448 * z, 448, axis=1)
    mine = lax.dynamic_slice_in_dim(small, z, 1, axis=0)[0]
    return (
        mixed,
        grad_tokens,
        total_in,
        total_dt,
        taps[:4],
        taps[4],
        mine[3200:3206],
        mine[3206:3212],
        mine[3212:3218],
        mine[3218:3602],
        total_mamba_out.astype(F32),
        total_attn_out.astype(F32),
        total_mixer,
        total_ffn,
        total_gate_up.astype(F32),
        total_down.astype(F32),
    )


def solution(mesh):
    row = P("fsdp", None)
    vec = P("fsdp")
    act = P("fsdp", None, "ctx", None)
    return jax.shard_map(
        per_device,
        mesh=mesh,
        in_specs=(
            act, P("fsdp", None, "ctx"), act, row, row, P(None, "fsdp"), vec, vec, vec, vec, vec,
            row, row, vec, vec, row, row,
        ),
        out_specs=(
            act, act, row, row, P(None, "fsdp"), vec, vec, vec, vec, vec, row, row, vec, vec, row, row,
        ),
        check_vma=False,
    )
```

time: 1490 us -> 697 us (0.47)
  the two profiles are of different devices: /device:TPU:1 before, /device:TPU:6 now
where the time goes in v1:
time: 697 us; the launch traced here: 686 us
  waiting for transfers between devices  232 us (33%)
  local copies, waits for them, and re-layouts  124 us (18%)
  starting transfers between devices  111 us (16%)
  Pallas kernels  67.9 us (10%)
  blocking collectives  54.2 us (8%)
  other arithmetic  43.2 us (6%)
  matrix products  37 us (5%)
  between operations  15.8 us (2%)
    psum x1, waiting for transfers between devices, per_device(): lax.psum((grad_gate_up, grad_down, grad_mamba_out, grad_attn_out), 'ctx')  106 us
    all_to_all x11, waiting for transfers between devices, exchange(): return lax.all_to_all(parts, axis, 0, 0, tiled=True)  72.4 us
    all_to_all x11, starting transfers between devices, exchange(): return lax.all_to_all(parts, axis, 0, 0, tiled=True)  67.5 us
    all_to_all x3, blocking collectives, exchange(): return lax.all_to_all(parts, axis, 0, 0, tiled=True)  54.2 us
    unnamed x198, local copies, waits for them, and re-layouts  42.3 us
    dot_general x18, matrix products, matmul(): return lax.dot_general(a, b, (dims, ((), ())), preferred_element_type=F32)  37 us
    ppermute x1, waiting for transfers between devices, per_device(): lax.ppermute(jnp.where(last_device, 0.0, halo_back[1]), 'ctx', up)  19.8 us
    convert_element_type x3, local copies, waits for them, and re-layouts, per_device(): total_gate_up.astype(F32)  18.1 us
  transfers between devices with their start and end apart: 35, of which 14 were waited for; matrix products, arithmetic and copies ran while one was open for 16% of the time, Pallas kernels for 9%

profile of v1, /device:TPU:6, one launch (start us, length us, event | category | flops | bytes accessed | tf_op | source)
XLA Modules:
  0.0 685.7 jit_solution(15451491238603233348)
XLA Ops:
  30.6 12.8 %all-to-all-done = bf16[4,2,72,1024]{3,2,1,0:T(8,128)(2,1)} async-done(((bf16[4,2,72,1024]{3,2,1,0:T(8,128)(2,1)}), bf16[4,2,72,1024]{3,2,1,0:T(8,128)(2,1)}, u32[]{:S(2)}, u32[]{:S(2)}) %all-to-all-start) | async-done | bytes 1179680 | tf_op jit(solution)/shard_map/all_to_all | solution.py:394
  53.6 23.2 %all-to-all-done.1 = bf16[4,256,1280]{2,1,0:T(8,128)(2,1)} async-done(((bf16[4,256,1280]{2,1,0:T(8,128)(2,1)}), bf16[4,256,1280]{2,1,0:T(8,128)(2,1)}, u32[]{:S(2)}, u32[]{:S(2)}) %all-to-all-start.1) | async-done | bytes 2621472 | tf_op jit(solution)/shard_map/all_to_all | solution.py:394
  91.6 8.9 %ssd_fwd.1 = (f32[8,64,384]{2,1,0:T(8,128)S(1)}, f32[8,64,384]{2,1,0:T(8,128)S(1)}, bf16[8,64,128]{2,1,0:T(8,128)(2,1)S(1)}, bf16[4,8,2,64,128]{4,3,2,1,0:T(8,128)(2,1)}) custom-call(s32[1]{0:T(128)} %bitcast.1.idx_ref, f32[8,72,640]{2,1,0:T(8,128)S(1)} %slice.413.ext_ref, f32[8,72,128]{2,1,0:T(8,128)S(1)} %fusion.40.dtr_ref, ...), custom_call_target="tpu_custom_call" | custom-call | flops 2000000 | bytes 6000 | tf_op jit(solution)/shard_map/ssd_fwd/pallas_call | solution.py:591
  103.5 9.4 %all-to-all-start.2 = ((bf16[32,2,64,128]{3,2,1,0:T(8,128)(2,1)}), bf16[32,2,64,128]{3,2,1,0:T(8,128)(2,1)S(1)}, u32[]{:S(2)}, u32[]{:S(2)}) async-start(bf16[32,2,64,128]{3,2,1,0:T(8,128)(2,1)} %bitcast.14), calls=%async_computation.2 | async-start | bytes 2097152 | tf_op jit(solution)/shard_map/all_to_all | solution.py:394
  121.8 9.5 %collective-permute-done.5 = bf16[128,1024]{1,0:T(8,128)(2,1)S(1)} collective-permute-done((bf16[128,1024]{1,0:T(8,128)(2,1)S(1)}, bf16[128,1024]{1,0:T(8,128)(2,1)S(1)}, u32[]{:S(2)}, u32[]{:S(2)}) %collective-permute-start.5) | collective-permute-done | bytes 262176 | tf_op jit(solution)/shard_map/ppermute | solution.py:417
  132.8 6.2 collective-permute-done.7
  144.0 7.7 %all-to-all-start.3 = ((bf16[32,2,48,128]{3,2,1,0:T(8,128)(2,1)}), bf16[32,2,48,128]{3,2,1,0:T(8,128)(2,1)S(1)}, u32[]{:S(2)}, u32[]{:S(2)}) async-start(bf16[32,2,48,128]{3,2,1,0:T(8,128)(2,1)} %copy-done.21), calls=%async_computation.3 | async-start | bytes 1572864 | tf_op jit(solution)/shard_map/all_to_all | solution.py:394
  162.9 13.4 %attn_fwd.1 = (f32[4,2,128,64]{3,2,1,0:T(8,128)S(1)}, f32[4,2,128,128]{3,2,1,0:T(8,128)S(1)}) custom-call(s32[1]{0:T(128)} %bitcast.1.idx_ref, bf16[4,2,128,64]{3,2,1,0:T(8,128)(2,1)S(1)} %bitcast.358, bf16[32,4,2,64,128]{4,3,2,1,0:T(8,128)(2,1)} %bitcast.341, s32[4,2,128,128]{3,2,1,0:T(8,128)S(1)} %broadcast_in_dim.158.st_ref, ...), custom_call_target="tpu_custom_call" | custom-call | flops 4000000 | bytes 8000 | tf_op jit(solution)/shard_map/attn_fwd/pallas_call | solution.py:633
  207.4 6.1 all-to-all-done.4
  225.5 18.5 %all_to_all.70 = bf16[4,144,1024]{2,1,0:T(8,128)(2,1)S(1)} all-to-all(bf16[4,144,1024]{2,1,0:T(8,128)(2,1)S(1)} %broadcast_in_dim.167), channel_id=1, replica_groups=mesh['ctx'=32,'fsdp'=4] {'fsdp'}, dimensions={0} | all-to-all | bytes 2359296 | tf_op jit(solution)/shard_map/all_to_all | solution.py:394
  250.6 16.4 %all_to_all.71 = bf16[4,128,1024]{2,1,0:T(8,128)(2,1)S(1)} all-to-all(bf16[4,128,1024]{2,1,0:T(8,128)(2,1)S(1)} %bitcast.397), channel_id=1, replica_groups=mesh['ctx'=32,'fsdp'=4] {'fsdp'}, dimensions={0} | all-to-all | bytes 2097152 | tf_op jit(solution)/shard_map/all_to_all | solution.py:394
  275.4 12.1 %all-to-all-done.7 = bf16[4,144,1024]{2,1,0:T(8,128)(2,1)} async-done(((bf16[4,144,1024]{2,1,0:T(8,128)(2,1)}), bf16[4,144,1024]{2,1,0:T(8,128)(2,1)}, u32[]{:S(2)}, u32[]{:S(2)}) %all-to-all-start.7) | async-done | bytes 1179680 | tf_op jit(solution)/shard_map/all_to_all | solution.py:394
  296.5 7.4 %all-to-all-start.8 = ((bf16[32,2,48,128]{3,2,1,0:T(8,128)(2,1)}), bf16[32,2,48,128]{3,2,1,0:T(8,128)(2,1)}, u32[]{:S(2)}, u32[]{:S(2)}) async-start(bf16[32,2,48,128]{3,2,1,0:T(8,128)(2,1)} %bitcast.354), calls=%async_computation.8 | async-start | bytes 1572864 | tf_op jit(solution)/shard_map/all_to_all | solution.py:394
  310.6 17.3 %attn_bwd.1 = (f32[4,2,128,64]{3,2,1,0:T(8,128)S(1)}, bf16[32,4,2,64,128]{4,3,2,1,0:T(8,128)(2,1)}) custom-call(s32[1]{0:T(128)} %bitcast.1.idx_ref, bf16[4,2,128,64]{3,2,1,0:T(8,128)(2,1)S(1)} %bitcast.359, bf16[32,4,2,64,128]{4,3,2,1,0:T(8,128)(2,1)} %bitcast.342, s32[4,2,128,128]{3,2,1,0:T(8,128)S(1)} %copy-done.11, f32[4,2,128,64]{3,2,1,0:T(8,128)S(1)} %copy-done.14, ...), custom_call_target="tpu_custom_call" | custom-call | flops 8000000 | bytes 16000 | tf_op jit(solution)/shard_map/attn_bwd/pallas_call | solution.py:750
  330.6 19.3 %all_to_all.72 = bf16[32,2,48,128]{3,2,1,0:T(8,128)(2,1)} all-to-all(bf16[32,2,48,128]{3,2,1,0:T(8,128)(2,1)S(1)} %chain.3), channel_id=1, replica_groups=mesh['ctx'=32,'fsdp'=4] {'ctx'}, dimensions={0} | all-to-all | bytes 1572864 | tf_op jit(solution)/shard_map/all_to_all | solution.py:394
  349.9 6.8 all-to-all-start.10
  377.3 14.2 %ssd_bwd.1 = (bf16[8,72,640]{2,1,0:T(8,128)(2,1)S(1)}, bf16[8,72,128]{2,1,0:T(8,128)(2,1)S(1)}, f32[8,8,640]{2,1,0:T(8,128)S(1)}) custom-call(s32[1]{0:T(128)} %bitcast.1.idx_ref, f32[8,72,640]{2,1,0:T(8,128)S(1)} %copy-done.8, f32[8,72,128]{2,1,0:T(8,128)S(1)} %copy-done.34, s32[8,64,128]{2,1,0:T(8,128)S(1)} %copy-done.36, ...), custom_call_target="tpu_custom_call" | custom-call | flops 4000000 | bytes 8000 | tf_op jit(solution)/shard_map/ssd_bwd/pallas_call | solution.py:780
  397.7 105.9 %all-reduce.15.cloned.1.call-done = (bf16[1024,1024]{1,0:T(8,128)(2,1)}, bf16[512,1024]{1,0:T(8,128)(2,1)}, bf16[384,1024]{1,0:T(8,128)(2,1)}, bf16[128,1024]{1,0:T(8,128)(2,1)}) async-done(((bf16[1024,1024]{1,0:T(8,128)(2,1)}, bf16[512,1024]{1,0:T(8,128)(2,1)}, bf16[384,1024]{1,0:T(8,128)(2,1)}, bf16[128,1024]{1,0:T(8,128)(2,1)}), (bf16[1024,1024]{1,0:T(8,128)(2,1)}, bf16[512,1024]{1,0:T(8,128)(2,1)}, ...) | async-done | bytes 4194320 | tf_op jit(solution)/shard_map/psum | solution.py:730
  555.1 18.1 %all-to-all-done.11.got_ref = bf16[32,4,8,1408]{3,2,1,0:T(8,128)(2,1)} async-done(((bf16[32,4,8,1408]{3,2,1,0:T(8,128)(2,1)}), bf16[32,4,8,1408]{3,2,1,0:T(8,128)(2,1)}, u32[]{:S(2)}, u32[]{:S(2)}) %all-to-all-start.11) | async-done | bytes 2883616 | tf_op jit(solution)/shard_map/all_to_all | solution.py:394
  595.8 7.3 %all-to-all-start.13 = ((bf16[32,8,4224]{2,1,0:T(8,128)(2,1)}), bf16[32,8,4224]{2,1,0:T(8,128)(2,1)}, u32[]{:S(2)}, u32[]{:S(2)}) async-start(bf16[32,8,4224]{2,1,0:T(8,128)(2,1)} %broadcast_in_dim.177), calls=%async_computation.13 | async-start | bytes 4325376 | tf_op jit(solution)/shard_map/all_to_all | solution.py:394
  610.6 19.8 %collective-permute-done.18 = bf16[3,1024]{1,0:T(4,128)(2,1)S(1)} collective-permute-done((bf16[3,1024]{1,0:T(4,128)(2,1)S(1)}, bf16[3,1024]{1,0:T(4,128)(2,1)S(1)}, u32[]{:S(2)}, u32[]{:S(2)}) %collective-permute-start.18) | collective-permute-done | bytes 6176 | tf_op jit(solution)/shard_map/ppermute | solution.py:813
  641.1 8.4 %collective-permute-done.20 = bf16[256,1024]{1,0:T(8,128)(2,1)} collective-permute-done((bf16[256,1024]{1,0:T(8,128)(2,1)}, bf16[256,1024]{1,0:T(8,128)(2,1)}, u32[]{:S(2)}, u32[]{:S(2)}) %collective-permute-start.20) | collective-permute-done | bytes 524320 | tf_op jit(solution)/shard_map/ppermute | solution.py:409
  656.8 6.9 %copy.104 = f32[4,256,2,512]{3,0,2,1:T(4,128)} copy(f32[4,256,2,512]{3,2,1,0:T(2,128)} %reshape.819) | data formatting | bytes 8388608 | tf_op jit(solution)/shard_map/convert_element_type | solution.py:909
  663.7 6.0 reshape.818
  (468 shorter events, 288.2 us)
Async XLA Ops:
  23.5 19.9 %all-to-all-start = ((bf16[4,2,72,1024]{3,2,1,0:T(8,128)(2,1)}), bf16[4,2,72,1024]{3,2,1,0:T(8,128)(2,1)}, u32[]{:S(2)}, u32[]{:S(2)}) async-start(bf16[4,2,72,1024]{3,2,1,0:T(8,128)(2,1)} %broadcast_in_dim.145), calls=%async_computation | async-start | bytes 2359296 | tf_op jit(solution)/shard_map/all_to_all | solution.py:394
  43.4 33.4 %all-to-all-start.1 = ((bf16[4,256,1280]{2,1,0:T(8,128)(2,1)}), bf16[4,256,1280]{2,1,0:T(8,128)(2,1)}, u32[]{:S(2)}, u32[]{:S(2)}) async-start(bf16[4,256,1280]{2,1,0:T(8,128)(2,1)} %copy-done.9), calls=%async_computation.1 | async-start | bytes 5242880 | tf_op jit(solution)/shard_map/all_to_all | solution.py:394
  48.0 92.2 %all-gather.3.cloned.1.call-start = ((), (), s32[]{:S(2)}) async-start(), calls=%async_computation.14 | async-start | bytes 4325376 | tf_op jit(solution)/shard_map/all_gather | solution.py:612
  85.6 31.1 %collective-permute-start.2 = (bf16[256,1024]{1,0:T(8,128)(2,1)}, bf16[256,1024]{1,0:T(8,128)(2,1)}, u32[]{:S(2)}, u32[]{:S(2)}) collective-permute-start(bf16[256,1024]{1,0:T(8,128)(2,1)} %dynamic-slice_bitcast_fusion.5), channel_id=1, source_target_pairs={{0,1},{1,2},{2,3},{3,0},{4,5},{5,6},{6,7},{7,4},{8,9},{9,10},{10,1... | collective-permute-start | bytes 1572872 | tf_op jit(solution)/shard_map/ppermute | solution.py:409
  103.5 36.7 %all-to-all-start.2 = ((bf16[32,2,64,128]{3,2,1,0:T(8,128)(2,1)}), bf16[32,2,64,128]{3,2,1,0:T(8,128)(2,1)S(1)}, u32[]{:S(2)}, u32[]{:S(2)}) async-start(bf16[32,2,64,128]{3,2,1,0:T(8,128)(2,1)} %bitcast.14), calls=%async_computation.2 | async-start | bytes 2097152 | tf_op jit(solution)/shard_map/all_to_all | solution.py:394
  112.9 26.1 %collective-permute-start.7 = (bf16[128,1024]{1,0:T(8,128)(2,1)S(1)}, bf16[128,1024]{1,0:T(8,128)(2,1)S(1)}, u32[]{:S(2)}, u32[]{:S(2)}) collective-permute-start(bf16[128,1024]{1,0:T(8,128)(2,1)S(1)} %bitcast.388), channel_id=1, source_target_pairs={{0,3},{1,0},{2,1},{3,2},{4,7},{5,4},{6,5},{7,6},{8,11},{9,8},{10,9... | collective-permute-start | bytes 786440 | tf_op jit(solution)/shard_map/ppermute | solution.py:417
  119.2 32.6 %collective-permute-start.3 = (bf16[256,1024]{1,0:T(8,128)(2,1)}, bf16[256,1024]{1,0:T(8,128)(2,1)}, u32[]{:S(2)}, u32[]{:S(2)}) collective-permute-start(bf16[256,1024]{1,0:T(8,128)(2,1)} %get-tuple-element.90), channel_id=1, source_target_pairs={{0,2},{1,3},{2,0},{3,1},{4,6},{5,7},{6,4},{7,5},{8,10},{9,11},{10,... | collective-permute-start | bytes 1572872 | tf_op jit(solution)/shard_map/ppermute | solution.py:409
  131.5 22.2 %collective-permute-start.4 = (bf16[256,1024]{1,0:T(8,128)(2,1)}, bf16[256,1024]{1,0:T(8,128)(2,1)}, u32[]{:S(2)}, u32[]{:S(2)}) collective-permute-start(bf16[256,1024]{1,0:T(8,128)(2,1)} %get-tuple-element.89), channel_id=1, source_target_pairs={{0,3},{1,0},{2,1},{3,2},{4,7},{5,4},{6,5},{7,6},{8,11},{9,8},{10,9... | collective-permute-start | bytes 1572872 | tf_op jit(solution)/shard_map/ppermute | solution.py:409
  144.0 34.7 %all-to-all-start.3 = ((bf16[32,2,48,128]{3,2,1,0:T(8,128)(2,1)}), bf16[32,2,48,128]{3,2,1,0:T(8,128)(2,1)S(1)}, u32[]{:S(2)}, u32[]{:S(2)}) async-start(bf16[32,2,48,128]{3,2,1,0:T(8,128)(2,1)} %copy-done.21), calls=%async_computation.3 | async-start | bytes 1572864 | tf_op jit(solution)/shard_map/all_to_all | solution.py:394
  190.3 23.2 %all-to-all-start.4 = ((bf16[4,144,1024]{2,1,0:T(8,128)(2,1)}), bf16[4,144,1024]{2,1,0:T(8,128)(2,1)}, u32[]{:S(2)}, u32[]{:S(2)}) async-start(bf16[4,144,1024]{2,1,0:T(8,128)(2,1)} %fusion.8), calls=%async_computation.4 | async-start | bytes 2359296 | tf_op jit(solution)/shard_map/all_to_all | solution.py:394
  296.5 32.2 %all-to-all-start.8 = ((bf16[32,2,48,128]{3,2,1,0:T(8,128)(2,1)}), bf16[32,2,48,128]{3,2,1,0:T(8,128)(2,1)}, u32[]{:S(2)}, u32[]{:S(2)}) async-start(bf16[32,2,48,128]{3,2,1,0:T(8,128)(2,1)} %bitcast.354), calls=%async_computation.8 | async-start | bytes 1572864 | tf_op jit(solution)/shard_map/all_to_all | solution.py:394
  349.9 153.8 %all-to-all-start.10 = ((bf16[32,4,2,64,128]{4,3,2,1,0:T(8,128)(2,1)}), bf16[32,4,2,64,128]{4,3,2,1,0:T(8,128)(2,1)}, u32[]{:S(2)}, u32[]{:S(2)}) async-start(bf16[32,4,2,64,128]{4,3,2,1,0:T(8,128)(2,1)} %get-tuple-element.39.dep_ref), calls=%async_computation.10 | async-start | bytes 8388608 | tf_op jit(solution)/shard_map/all_to_all | solution.py:394
  356.7 147.0 %all-reduce.15.cloned.1.call-start = ((), (), s32[]{:S(2)}) async-start(), calls=%async_computation.15 | async-start | bytes 8388608 | tf_op jit(solution)/shard_map/psum | solution.py:730
  532.8 40.4 %all-to-all-start.11 = ((bf16[32,4,8,1408]{3,2,1,0:T(8,128)(2,1)}), bf16[32,4,8,1408]{3,2,1,0:T(8,128)(2,1)}, u32[]{:S(2)}, u32[]{:S(2)}) async-start(bf16[32,4,8,1408]{3,2,1,0:T(8,128)(2,1)} %bitcast.366), calls=%async_computation.11 | async-start | bytes 5767168 | tf_op jit(solution)/shard_map/all_to_all | solution.py:394
  539.7 41.4 %collective-permute-start.14 = (bf16[144,1024]{1,0:T(8,128)(2,1)}, bf16[144,1024]{1,0:T(8,128)(2,1)}, u32[]{:S(2)}, u32[]{:S(2)}) collective-permute-start(bf16[144,1024]{1,0:T(8,128)(2,1)} %get-tuple-element.92), channel_id=1, source_target_pairs={{0,1},{1,2},{2,3},{3,0},{4,5},{5,6},{6,7},{7,4},{8,9},{9,10},{10,1... | collective-permute-start | bytes 884744 | tf_op jit(solution)/shard_map/ppermute | solution.py:427
  541.3 43.4 %collective-permute-start.16 = (bf16[144,1024]{1,0:T(8,128)(2,1)}, bf16[144,1024]{1,0:T(8,128)(2,1)}, u32[]{:S(2)}, u32[]{:S(2)}) collective-permute-start(bf16[144,1024]{1,0:T(8,128)(2,1)} %get-tuple-element.93), channel_id=1, source_target_pairs={{0,3},{1,0},{2,1},{3,2},{4,7},{5,4},{6,5},{7,6},{8,11},{9,8},{10,9... | collective-permute-start | bytes 884744 | tf_op jit(solution)/shard_map/ppermute | solution.py:427
  543.0 42.5 %collective-permute-start.15 = (bf16[144,1024]{1,0:T(8,128)(2,1)}, bf16[144,1024]{1,0:T(8,128)(2,1)}, u32[]{:S(2)}, u32[]{:S(2)}) collective-permute-start(bf16[144,1024]{1,0:T(8,128)(2,1)} %get-tuple-element.94), channel_id=1, source_target_pairs={{0,2},{1,3},{2,0},{3,1},{4,6},{5,7},{6,4},{7,5},{8,10},{9,11},{10,... | collective-permute-start | bytes 884744 | tf_op jit(solution)/shard_map/ppermute | solution.py:427
  546.6 91.6 %collective-permute-start.11 = (bf16[128,1024]{1,0:T(8,128)(2,1)}, bf16[128,1024]{1,0:T(8,128)(2,1)}, u32[]{:S(2)}, u32[]{:S(2)}) collective-permute-start(bf16[128,1024]{1,0:T(8,128)(2,1)} %get-tuple-element.95), channel_id=1, source_target_pairs={{0,1},{1,2},{2,3},{3,0},{4,5},{5,6},{6,7},{7,4},{8,9},{9,10},{10,1... | collective-permute-start | bytes 786440 | tf_op jit(solution)/shard_map/ppermute | solution.py:427
  547.2 90.9 %collective-permute-start.13 = (bf16[128,1024]{1,0:T(8,128)(2,1)}, bf16[128,1024]{1,0:T(8,128)(2,1)}, u32[]{:S(2)}, u32[]{:S(2)}) collective-permute-start(bf16[128,1024]{1,0:T(8,128)(2,1)} %get-tuple-element.96), channel_id=1, source_target_pairs={{0,3},{1,0},{2,1},{3,2},{4,7},{5,4},{6,5},{7,6},{8,11},{9,8},{10,9... | collective-permute-start | bytes 786440 | tf_op jit(solution)/shard_map/ppermute | solution.py:427
  581.2 57.0 %collective-permute-start.12 = (bf16[128,1024]{1,0:T(8,128)(2,1)}, bf16[128,1024]{1,0:T(8,128)(2,1)}, u32[]{:S(2)}, u32[]{:S(2)}) collective-permute-start(bf16[128,1024]{1,0:T(8,128)(2,1)} %get-tuple-element.97), channel_id=1, source_target_pairs={{0,2},{1,3},{2,0},{3,1},{4,6},{5,7},{6,4},{7,5},{8,10},{9,11},{10,... | collective-permute-start | bytes 786440 | tf_op jit(solution)/shard_map/ppermute | solution.py:427
  584.7 21.5 %collective-permute-start.19 = (bf16[256,1024]{1,0:T(8,128)(2,1)}, bf16[256,1024]{1,0:T(8,128)(2,1)}, u32[]{:S(2)}, u32[]{:S(2)}) collective-permute-start(bf16[256,1024]{1,0:T(8,128)(2,1)} %dynamic-slice_bitcast_fusion.2), channel_id=1, source_target_pairs={{0,1},{1,2},{2,3},{3,0},{4,5},{5,6},{6,7},{7,4},{8,9},{9,10},{10,1... | collective-permute-start | bytes 1572872 | tf_op jit(solution)/shard_map/ppermute | solution.py:409
  595.8 73.9 %all-to-all-start.13 = ((bf16[32,8,4224]{2,1,0:T(8,128)(2,1)}), bf16[32,8,4224]{2,1,0:T(8,128)(2,1)}, u32[]{:S(2)}, u32[]{:S(2)}) async-start(bf16[32,8,4224]{2,1,0:T(8,128)(2,1)} %broadcast_in_dim.177), calls=%async_computation.13 | async-start | bytes 4325376 | tf_op jit(solution)/shard_map/all_to_all | solution.py:394
  604.0 26.4 %collective-permute-start.18 = (bf16[3,1024]{1,0:T(4,128)(2,1)S(1)}, bf16[3,1024]{1,0:T(4,128)(2,1)S(1)}, u32[]{:S(2)}, u32[]{:S(2)}) collective-permute-start(bf16[3,1024]{1,0:T(4,128)(2,1)S(1)} %get-tuple-element.112), channel_id=1, source_target_pairs={{0,4},{4,8},{8,12},{12,16},{16,20},{20,24},{24,28},{28,32},{32,36}... | collective-permute-start | bytes 18440 | tf_op jit(solution)/shard_map/ppermute | solution.py:813
  608.4 42.2 %collective-permute-start.21 = (bf16[256,1024]{1,0:T(8,128)(2,1)}, bf16[256,1024]{1,0:T(8,128)(2,1)}, u32[]{:S(2)}, u32[]{:S(2)}) collective-permute-start(bf16[256,1024]{1,0:T(8,128)(2,1)} %get-tuple-element.85), channel_id=1, source_target_pairs={{0,3},{1,0},{2,1},{3,2},{4,7},{5,4},{6,5},{7,6},{8,11},{9,8},{10,9... | collective-permute-start | bytes 1572872 | tf_op jit(solution)/shard_map/ppermute | solution.py:409
  (108 other events, 1032.9 us)
Sparse Core Ops, SparseCore 0:
  83.0 55.3 all-gather.2
  366.8 136.8 all-reduce.14

commit v2 on v1

--- a/solution.py
+++ b/solution.py
@@ -163,13 +163,78 @@
         out_ref[zz, :, 512:] = w_ref[:, FF + 512 * zz : FF + 512 * zz + 512]
 
 
-def total_kernel(n, got_ref, *refs):
-    out_ref = refs[-1]
-
+def total_kernel(n, got_ref, dep_ref, out_ref):
     def step(j, acc):
         return acc + got_ref[j].astype(F32)
 
     out_ref[...] = lax.fori_loop(1, n, step, got_ref[0].astype(F32))
+
+
+def pack_kernel(nj, rj, kin_ref, gin_ref, kex_ref, gex_ref, gu_ref, o_ref, out_ref):
+    for a in range(4):
+        part = (kin_ref[a].astype(F32) + gin_ref[a].astype(F32)).astype(BF16)
+        out_ref[:, a, :, :LPROJ] = part.reshape(nj, rj, LPROJ)
+        part = (kex_ref[a].astype(F32) + gex_ref[a].astype(F32)).astype(BF16)
+        out_ref[:, a, :, LPROJ:1408] = part.reshape(nj, rj, 128)
+        out_ref[:, a, :, 1408:2432] = gu_ref[a].reshape(nj, rj, 1024)
+    out_ref[:, :, :, 2432:] = o_ref[...].reshape(nj, 4, rj, 1024)
+
+
+def assemble_kernel(owned_ref, o_ref, out_ref):
+    def put(lo, value):
+        out_ref[:, lo : lo + value.shape[1]] = value.astype(BF16)
+
+    shared = owned_ref[0, :, 768:1024]
+    for zz in range(4):
+        put(LX * zz, owned_ref[zz, :, :LX])
+        put(1536 + LX * zz, owned_ref[zz, :, LX : 2 * LX])
+        put(3328 + 128 * zz, owned_ref[zz, :, 1024:1152])
+        put(4096 + 512 * zz, owned_ref[zz, :, 1408:1920])
+        put(6144 + 512 * zz, owned_ref[zz, :, 1920:2432])
+        put(8320 + 1024 * zz, o_ref[zz])
+        if zz > 0:
+            shared = shared + owned_ref[zz, :, 768:1024]
+    put(3072, shared)
+    first = owned_ref[0, :, 1152:1280] + owned_ref[1, :, 1152:1280]
+    second = owned_ref[2, :, 1152:1280] + owned_ref[3, :, 1152:1280]
+    put(3840, jnp.concatenate([first[:, :HDIM], second[:, :HDIM]], axis=1))
+    put(3968, jnp.concatenate([first[:, HDIM:], second[:, HDIM:]], axis=1))
+    extras = [owned_ref[zz, :, 1280:1304] for zz in range(4)]
+    extras.append(jnp.zeros((extras[0].shape[0], 32), F32))
+    put(8192, jnp.concatenate(extras, axis=1))
+
+
+def unpack_kernel(nj, rj, core_ref, mine_ref, other_ref, in_ref, gu_ref, ex_ref, down_ref, mo_ref, ao_ref):
+    half = pl.program_id(0)
+    core = core_ref[0]
+
+    def write(src):
+        in_ref[...] = src[:, :, :4096].reshape(128, 4096).astype(F32)
+        gu_ref[...] = src[:, :, 4096:8192].reshape(128, 4096).astype(F32)
+        ex_ref[...] = src[:, :, 8192:8320].reshape(128, 128).astype(F32)
+        for j in range(nj):
+            for a in range(4):
+                row = j * 4 * rj + a * rj
+                part = src[j, :, 8320 + 1024 * a : 9344 + 1024 * a].astype(F32)
+
+                @pl.when(half == 0)
+                def _():
+                    down_ref[row : row + rj] = part
+
+                @pl.when(half == 1)
+                def _():
+                    if row < 384:
+                        mo_ref[row : row + rj] = part
+                    else:
+                        ao_ref[row - 384 : row - 384 + rj] = part
+
+    @pl.when(half == core)
+    def _():
+        write(mine_ref)
+
+    @pl.when(half != core)
+    def _():
+        write(other_ref)
 
 
 def leak_kernel(nk, pr, dy_ref, swx_ref, c_ref, out_ref):
@@ -271,7 +336,8 @@
     misc_ref[0] = jnp.concatenate(rows, axis=0)
 
 
-def scan_kernel(reverse, n, pr, st_ref, dec_ref, dep_ref, out_ref):
+def scan_kernel(reverse, n, pr, st_ref, dec_ref, *refs):
+    out_ref = refs[-1]
     rows = LOCAL_HEADS * pr
 
     def step(j, half, s):
@@ -525,7 +591,7 @@
         ]
     )
     flat = jnp.pad(flat, (0, 10 * D - flat.shape[0])).reshape(2, 5, D)
-    wide = spread(jnp.concatenate([flat, halo, tok], axis=1), "fsdp")
+    wide = ring_spread(jnp.concatenate([flat, halo, tok], axis=1), z)
     own_in = exchange(send_in, "fsdp").reshape(D, LPROJ)
     own_gu = ring_exchange(send_gu, z).reshape(D, 1024)
     grad_own = cotangent[0].reshape(128, D)
@@ -611,18 +677,18 @@
     got = exchange(state_out.reshape(nctx, 2, srows + 16, 128), "ctx")
     kv_all = lax.all_gather(kv_own, "ctx")
 
-    def chain(reverse, terms, after):
+    def chain(reverse, terms, *after):
         return pl.pallas_call(
             functools.partial(scan_kernel, reverse, nctx, pr),
-            in_specs=[VMEM, VMEM, ANY],
+            in_specs=[VMEM, VMEM] + [ANY] * len(after),
             out_specs=VMEM,
             out_shape=sds((nctx, 2, srows, 128), BF16),
             compiler_params=PARAMS,
             cost_estimate=cost(10**7, 3 * 10**6),
             name="chain",
-        )(terms, got, after)
-
-    entry = exchange(chain(False, got, kv_all), "ctx").reshape(4, nk, 2, srows, 128)
+        )(terms, got, *after)
+
+    entry = exchange(chain(False, got), "ctx").reshape(4, nk, 2, srows, 128)
 
     st_rows = jnp.broadcast_to(
         starts.reshape(4, 2, 1, BLK, 1), (4, 2, 2, BLK, 128)
@@ -727,10 +793,21 @@
     )
     grad_mamba_out = matmul(act_mamba, grad_mix, TN).astype(BF16)
     grad_attn_out = matmul(act_attn, grad_mix, TN).astype(BF16)
-    totals = lax.psum((grad_gate_up, grad_down, grad_mamba_out, grad_attn_out), "ctx")
-    total_gate_up, total_down, total_mamba_out, total_attn_out = totals
-    total_gate_up = ring_exchange(total_gate_up.reshape(4, 256, 1024), z)
-    total_gate_up = total_gate_up.reshape(4, 256, 2, 512).transpose(1, 2, 0, 3).reshape(256, 4096)
+    core = i % 2
+    pair = [(a, a ^ 1) for a in range(nctx)]
+
+    def halves(v):
+        v = v.reshape(4, 2, 128, v.shape[-1])
+        keep = lax.dynamic_index_in_dim(v, core, 1, keepdims=False)
+        give = lax.dynamic_index_in_dim(v, 1 - core, 1, keepdims=False)
+        return keep, lax.ppermute(give, "ctx", pair)
+
+    kept, taken = halves(grad_gate_up)
+    pair_gu = (kept.astype(F32) + taken.astype(F32)).astype(BF16)
+    out_grads = jnp.concatenate([grad_mamba_out, grad_attn_out], axis=0)
+    kept = jnp.where(core == 0, grad_down, out_grads)
+    taken = lax.ppermute(jnp.where(core == 0, out_grads, grad_down), "ctx", pair)
+    pair_o = (kept.astype(F32) + taken.astype(F32)).astype(BF16)
     grad_inner_gain = jnp.sum(grad_m * norm_in, axis=0)
     grad_u = inner_r * (grad_n - norm_in * dots)
     grad_y = (grad_u * z_silu).reshape(8, BLK, LX)
@@ -761,16 +838,16 @@
         cost_estimate=cost(8 * 10**9, 16 * 10**6, 2 * 10**6),
         name="attn_bwd",
     )(idx, query, kv_all, st_rows, attn_o, lse, grad_attn)
-    grad_exit = exchange(chain(True, got_leak, grad_kv), "ctx").reshape(4, nk, 2, srows, 128)
+    grad_exit = exchange(chain(True, got_leak, grad_kv, pair_gu, pair_o), "ctx").reshape(4, nk, 2, srows, 128)
     grad_kv = pl.pallas_call(
         functools.partial(total_kernel, nctx),
-        in_specs=[VMEM] + [ANY] * 4,
+        in_specs=[VMEM, ANY],
         out_specs=VMEM,
         out_shape=sds((4, 2, BLK, 128), F32),
         compiler_params=PARAMS,
         cost_estimate=cost(2 * 10**6, 4 * 10**6),
         name="total_kv",
-    )(exchange(grad_kv, "ctx"), *totals)
+    )(exchange(grad_kv, "ctx"), mixed)
     back = (tables[0], -tables[1])
     grad_key = turn(grad_kv[..., :HDIM].reshape(4, 2, BLK, 1, HDIM), *back).reshape(8, BLK, HDIM)
     grad_value = grad_kv[..., HDIM:].reshape(8, BLK, HDIM)
@@ -818,9 +895,6 @@
     grad_tokens = grad_middle + rms_back(hidden, rms_of(hidden), own_act * mixer_scale)
     grad_tokens = grad_tokens.reshape(1, 2, BLK, D)
 
-    def permuted(v):
-        return v.reshape(4, nctx, rpc, -1).swapaxes(0, 1)
-
     grad_in = matmul(act_one, grad_proj, TN).astype(BF16)
     grad_dtw = matmul(act_one, grad_dt, TN)
     misc = jnp.sum(misc, axis=0)
@@ -841,42 +915,70 @@
         ],
         axis=1,
     ).astype(BF16)
-    sent = permuted(jnp.concatenate([grad_in, extras], axis=1))
+    nj = nctx // 2
+    rj = 128 // nj
+    groups = [[2 * j + c for j in range(nj)] for c in range(2)]
+    kept_in, taken_in = halves(grad_in)
+    kept_ex, taken_ex = halves(extras)
+    sent = pl.pallas_call(
+        functools.partial(pack_kernel, nj, rj),
+        in_specs=[VMEM] * 6,
+        out_specs=VMEM,
+        out_shape=sds((nj, 4, rj, 3456), BF16),
+        compiler_params=PARAMS,
+        cost_estimate=cost(0, 7 * 10**6),
+        name="pack",
+    )(kept_in, taken_in, kept_ex, taken_ex, pair_gu, pair_o)
     summed = pl.pallas_call(
-        functools.partial(total_kernel, nctx),
-        in_specs=[VMEM],
+        functools.partial(total_kernel, nj),
+        in_specs=[VMEM, ANY],
         out_specs=VMEM,
-        out_shape=sds((4, rpc, LPROJ + 128), F32),
+        out_shape=sds((4, rj, 3456), F32),
         compiler_params=PARAMS,
         cost_estimate=cost(2 * 10**6, 4 * 10**6),
         name="total",
-    )(exchange(sent, "ctx"))
-    owned = exchange(summed, "fsdp")
-
-    def side(lo, hi):
-        return jnp.concatenate([owned[zz, :, lo:hi] for zz in range(4)], axis=1)
-
-    def shared(lo, hi):
-        return jnp.concatenate(
-            [owned[0, :, lo:hi] + owned[1, :, lo:hi], owned[2, :, lo:hi] + owned[3, :, lo:hi]], axis=1
-        )
-
-    final = jnp.concatenate(
-        [
-            side(0, 384),
-            side(384, 768),
-            jnp.sum(owned[:, :, 768:1024], axis=0),
-            side(1024, 1152),
-            shared(1152, 1216),
-            shared(1216, 1280),
-            side(1280, 1304),
-            jnp.zeros((rpc, 32), F32),
-        ],
-        axis=1,
-    ).astype(BF16)
-    final = spread(final, "ctx").reshape(256, 4224).astype(F32)
-    total_in = final[:, :4096]
-    extra = final[:, 4096:4192].reshape(256, 4, 24)
+    )(lax.all_to_all(sent, "ctx", 0, 0, axis_index_groups=groups, tiled=True), got_act)
+    owned = exchange(summed[:, :, :2432], "fsdp")
+    final = pl.pallas_call(
+        assemble_kernel,
+        in_specs=[VMEM] * 2,
+        out_specs=VMEM,
+        out_shape=sds((rj, 12416), BF16),
+        compiler_params=PARAMS,
+        cost_estimate=cost(0, 10**6),
+        name="assemble",
+    )(owned, summed[:, :, 2432:])
+    mine_all = lax.all_to_all(
+        jnp.broadcast_to(final[None], (nj, rj, 12416)),
+        "ctx", 0, 0, axis_index_groups=groups, tiled=True,
+    )
+    other_all = lax.ppermute(mine_all, "ctx", pair)
+    half_spec = pl.BlockSpec((128, 4096), lambda h: (h, 0))
+    total_in, total_gate_up, extra, total_down, total_mamba_out, total_attn_out = pl.pallas_call(
+        functools.partial(unpack_kernel, nj, rj),
+        grid=(2,),
+        in_specs=[SMEM, whole((nj, rj, 12416)), whole((nj, rj, 12416))],
+        out_specs=[
+            half_spec,
+            half_spec,
+            pl.BlockSpec((128, 128), lambda h: (h, 0)),
+            whole((512, 1024)),
+            whole((384, 1024)),
+            whole((128, 1024)),
+        ],
+        out_shape=[
+            sds((256, 4096), F32),
+            sds((256, 4096), F32),
+            sds((256, 128), F32),
+            sds((512, 1024), F32),
+            sds((384, 1024), F32),
+            sds((128, 1024), F32),
+        ],
+        compiler_params=PARAMS,
+        cost_estimate=cost(0, 10**7),
+        name="unpack",
+    )(core.astype(jnp.int32).reshape(1), mine_all, other_all)
+    extra = extra[:, :96].reshape(256, 4, 24)
     total_dt = extra[:, :, :6].reshape(256, 24)
     total_mixer = jnp.sum(extra[:, :, 6], axis=1)
     total_ffn = jnp.sum(extra[:, :, 7], axis=1)
@@ -902,12 +1004,12 @@
         mine[3206:3212],
         mine[3212:3218],
         mine[3218:3602],
-        total_mamba_out.astype(F32),
-        total_attn_out.astype(F32),
+        total_mamba_out,
+        total_attn_out,
         total_mixer,
         total_ffn,
-        total_gate_up.astype(F32),
-        total_down.astype(F32),
+        total_gate_up,
+        total_down,
     )
 
 

time: 697 us -> 627 us (0.90)
  the two profiles are of different devices: /device:TPU:6 before, /device:TPU:1 now
where the time goes in v2:
time: 627 us; the launch traced here: 615 us
  waiting for transfers between devices  163 us (26%)
  starting transfers between devices  110 us (18%)
  blocking collectives  94.8 us (15%)
  local copies, waits for them, and re-layouts  83.1 us (13%)
  Pallas kernels  79.9 us (13%)
  other arithmetic  35.9 us (6%)
  matrix products  31.8 us (5%)
  between operations  16.4 us (3%)
    all_to_all x9, starting transfers between devices, exchange(): return lax.all_to_all(parts, axis, 0, 0, tiled=True)  57.6 us
    all_to_all x1, blocking collectives, per_device(): lax.all_to_all(jnp.broadcast_to(final[None], (nj, rj, 12416)), 'ctx', 0,...  54.2 us
    all_to_all x9, waiting for transfers between devices, exchange(): return lax.all_to_all(parts, axis, 0, 0, tiled=True)  46.6 us
    ppermute x6, waiting for transfers between devices, ring_spread(): got = lax.ppermute(part, 'fsdp', perm)  44.4 us
    all_to_all x2, blocking collectives, exchange(): return lax.all_to_all(parts, axis, 0, 0, tiled=True)  40.6 us
    unnamed x256, local copies, waits for them, and re-layouts  36.6 us
    dot_general x18, matrix products, matmul(): return lax.dot_general(a, b, (dims, ((), ())), preferred_element_type=F32)  31.8 us
    all_to_all x1, waiting for transfers between devices, per_device(): lax.all_to_all(sent, 'ctx', 0, 0, axis_index_groups=groups, tiled=True)  31.3 us
  transfers between devices with their start and end apart: 38, of which 22 were waited for; matrix products, arithmetic and copies ran while one was open for 14% of the time, Pallas kernels for 9%

profile of v2, /device:TPU:1, one launch (start us, length us, event | category | flops | bytes accessed | tf_op | source)
XLA Modules:
  0.0 614.8 jit_solution(10397854561375492502)
XLA Ops:
  18.0 5.2 all-to-all-start
  30.4 31.2 %collective-permute-done.2 = bf16[2,72,1024]{2,1,0:T(8,128)(2,1)S(1)} collective-permute-done((bf16[2,72,1024]{2,1,0:T(8,128)(2,1)S(1)}, bf16[2,72,1024]{2,1,0:T(8,128)(2,1)S(1)}, u32[]{:S(2)}, u32[]{:S(2)}) %collective-permute-start.2) | collective-permute-done | bytes 294944 | tf_op jit(solution)/shard_map/ppermute | solution.py:483
  61.7 6.6 %collective-permute-done.3 = bf16[2,72,1024]{2,1,0:T(8,128)(2,1)S(1)} collective-permute-done((bf16[2,72,1024]{2,1,0:T(8,128)(2,1)S(1)}, bf16[2,72,1024]{2,1,0:T(8,128)(2,1)S(1)}, u32[]{:S(2)}, u32[]{:S(2)}) %collective-permute-start.3) | collective-permute-done | bytes 294944 | tf_op jit(solution)/shard_map/ppermute | solution.py:483
  86.5 8.9 %ssd_fwd.1 = (f32[8,64,384]{2,1,0:T(8,128)S(1)}, f32[8,64,384]{2,1,0:T(8,128)S(1)}, bf16[8,64,128]{2,1,0:T(8,128)(2,1)S(1)}, bf16[4,8,2,64,128]{4,3,2,1,0:T(8,128)(2,1)}) custom-call(s32[1]{0:T(128)} %bitcast.1.idx_ref, f32[8,72,640]{2,1,0:T(8,128)S(1)} %slice.301.ext_ref, f32[8,72,128]{2,1,0:T(8,128)S(1)} %fusion.41.dtr_ref, ...), custom_call_target="tpu_custom_call" | custom-call | flops 2000000 | bytes 6000 | tf_op jit(solution)/shard_map/ssd_fwd/pallas_call | solution.py:657
  98.3 7.6 %all-to-all-start.1 = ((bf16[32,2,64,128]{3,2,1,0:T(8,128)(2,1)}), bf16[32,2,64,128]{3,2,1,0:T(8,128)(2,1)S(1)}, u32[]{:S(2)}, u32[]{:S(2)}) async-start(bf16[32,2,64,128]{3,2,1,0:T(8,128)(2,1)} %bitcast.17), calls=%async_computation.1 | async-start | bytes 2097152 | tf_op jit(solution)/shard_map/all_to_all | solution.py:460
  117.0 5.0 collective-permute-done.9
  123.3 5.1 all-to-all-done.1.st_ref.dec_ref
  130.0 6.0 all-to-all-start.2
  137.9 6.3 %collective-permute-done.7 = bf16[256,1024]{1,0:T(8,128)(2,1)} collective-permute-done((bf16[256,1024]{1,0:T(8,128)(2,1)}, bf16[256,1024]{1,0:T(8,128)(2,1)}, u32[]{:S(2)}, u32[]{:S(2)}) %collective-permute-start.7) | collective-permute-done | bytes 524320 | tf_op jit(solution)/shard_map/ppermute | solution.py:475
  158.2 13.4 %attn_fwd.1 = (f32[4,2,128,64]{3,2,1,0:T(8,128)S(1)}, f32[4,2,128,128]{3,2,1,0:T(8,128)S(1)}) custom-call(s32[1]{0:T(128)} %bitcast.1.idx_ref, bf16[4,2,128,64]{3,2,1,0:T(8,128)(2,1)S(1)} %bitcast.325, bf16[32,4,2,64,128]{4,3,2,1,0:T(8,128)(2,1)} %bitcast.335, s32[4,2,128,128]{3,2,1,0:T(8,128)S(1)} %broadcast_in_dim.153.st_ref, ...), custom_call_target="tpu_custom_call" | custom-call | flops 4000000 | bytes 8000 | tf_op jit(solution)/shard_map/attn_fwd/pallas_call | solution.py:699
  218.1 19.0 %all_to_all.65 = bf16[4,144,1024]{2,1,0:T(8,128)(2,1)S(1)} all-to-all(bf16[4,144,1024]{2,1,0:T(8,128)(2,1)S(1)} %broadcast_in_dim.162), channel_id=1, replica_groups=mesh['ctx'=32,'fsdp'=4] {'fsdp'}, dimensions={0} | all-to-all | bytes 2359296 | tf_op jit(solution)/shard_map/all_to_all | solution.py:460
  244.6 14.5 %all-to-all-start.5 = ((bf16[4,128,1024]{2,1,0:T(8,128)(2,1)}), bf16[4,128,1024]{2,1,0:T(8,128)(2,1)}, u32[]{:S(2)}, u32[]{:S(2)}) async-start(bf16[4,128,1024]{2,1,0:T(8,128)(2,1)} %bitcast.368), calls=%async_computation.5 | async-start | bytes 2097152 | tf_op jit(solution)/shard_map/all_to_all | solution.py:460
  320.5 7.1 %all-to-all-start.7 = ((bf16[32,2,48,128]{3,2,1,0:T(8,128)(2,1)}), bf16[32,2,48,128]{3,2,1,0:T(8,128)(2,1)}, u32[]{:S(2)}, u32[]{:S(2)}) async-start(bf16[32,2,48,128]{3,2,1,0:T(8,128)(2,1)} %bitcast.321), calls=%async_computation.7 | async-start | bytes 1572864 | tf_op jit(solution)/shard_map/all_to_all | solution.py:460
  331.4 17.5 %attn_bwd.1 = (f32[4,2,128,64]{3,2,1,0:T(8,128)S(1)}, bf16[32,4,2,64,128]{4,3,2,1,0:T(8,128)(2,1)}) custom-call(s32[1]{0:T(128)} %bitcast.1.idx_ref, bf16[4,2,128,64]{3,2,1,0:T(8,128)(2,1)S(1)} %bitcast.326, bf16[32,4,2,64,128]{4,3,2,1,0:T(8,128)(2,1)} %bitcast.336, s32[4,2,128,128]{3,2,1,0:T(8,128)S(1)} %broadcast_in_dim.153.st_ref, ...), custom_call_target="tpu_custom_call" | custom-call | flops 8000000 | bytes 16000 | tf_op jit(solution)/shard_map/attn_bwd/pallas_call | solution.py:827
  353.9 21.5 %all_to_all.66 = bf16[32,2,48,128]{3,2,1,0:T(8,128)(2,1)} all-to-all(bf16[32,2,48,128]{3,2,1,0:T(8,128)(2,1)S(1)} %chain.3), channel_id=1, replica_groups=mesh['ctx'=32,'fsdp'=4] {'ctx'}, dimensions={0} | all-to-all | bytes 1572864 | tf_op jit(solution)/shard_map/all_to_all | solution.py:460
  389.8 14.0 %ssd_bwd.1 = (bf16[8,72,640]{2,1,0:T(8,128)(2,1)S(1)}, bf16[8,72,128]{2,1,0:T(8,128)(2,1)S(1)}, f32[8,8,640]{2,1,0:T(8,128)S(1)}) custom-call(s32[1]{0:T(128)} %bitcast.1.idx_ref, f32[8,72,640]{2,1,0:T(8,128)S(1)} %copy-done.6, f32[8,72,128]{2,1,0:T(8,128)S(1)} %copy-done.32, s32[8,64,128]{2,1,0:T(8,128)S(1)} %copy-done.36, f32[8,640]{1,0:T(8,128)S(1)} %copy-done.52, ...), custom_call_target="tpu_custom_call" | custom-call | flops 4000000 | bytes 8000 | tf_op jit(solution)/shard_map/ssd_bwd/pallas_call | solution.py:857
  407.6 24.8 %all-to-all-done.9.got_ref = bf16[32,4,2,64,128]{4,3,2,1,0:T(8,128)(2,1)} async-done(((bf16[32,4,2,64,128]{4,3,2,1,0:T(8,128)(2,1)}), bf16[32,4,2,64,128]{4,3,2,1,0:T(8,128)(2,1)}, u32[]{:S(2)}, u32[]{:S(2)}) %all-to-all-start.9) | async-done | bytes 4194336 | tf_op jit(solution)/shard_map/all_to_all | solution.py:460
  460.6 6.1 all-to-all-start.10
  470.2 6.8 %collective-permute-done.19 = bf16[144,1024]{1,0:T(8,128)(2,1)S(1)} collective-permute-done((bf16[144,1024]{1,0:T(8,128)(2,1)S(1)}, bf16[144,1024]{1,0:T(8,128)(2,1)S(1)}, u32[]{:S(2)}, u32[]{:S(2)}) %collective-permute-start.19) | collective-permute-done | bytes 294944 | tf_op jit(solution)/shard_map/ppermute | solution.py:493
  476.9 5.2 collective-permute-done.20
  483.1 31.3 %all-to-all-done.10.got_ref = bf16[16,4,8,3456]{3,2,1,0:T(8,128)(2,1)} async-done(((bf16[16,4,8,3456]{3,2,1,0:T(8,128)(2,1)}), bf16[16,4,8,3456]{3,2,1,0:T(8,128)(2,1)}, u32[]{:S(2)}, u32[]{:S(2)}) %all-to-all-start.10) | async-done | bytes 3538976 | tf_op jit(solution)/shard_map/all_to_all | solution.py:940
  521.9 5.9 all-to-all-done.11.owned_ref
  528.2 54.2 %all_to_all.67.mine_ref = bf16[16,8,12416]{2,1,0:T(8,128)(2,1)} all-to-all(bf16[16,8,12416]{2,1,0:T(8,128)(2,1)S(1)} %broadcast_in_dim.169), channel_id=1, replica_groups={{0,8,16,24,32,40,48,56,64,72,80,88,96,104,112,120},{4,12,20,28,36,44,52..., dimensions={0} | all-to-all | bytes 6356992 | tf_op jit(solution)/shard_map/all_to_all | solution.py:951
  594.8 8.3 %unpack.1 = (f32[256,4096]{1,0:T(8,128)}, f32[256,4096]{1,0:T(8,128)}, f32[256,128]{1,0:T(8,128)S(1)}, f32[512,1024]{1,0:T(8,128)}, f32[384,1024]{1,0:T(8,128)}, /*index=5*/f32[128,1024]{1,0:T(8,128)}) custom-call(s32[1]{0:T(128)} %bitcast.93.core_ref, bf16[16,8,12416]{2,1,0:T(8,128)(2,1)} %all_to_all.67.mine_ref, ...), custom_call_target="tpu_custom_call" | custom-call | bytes 10000 | tf_op jit(solution)/shard_map/unpack/pallas_call | solution.py:957
  (528 shorter events, 267.1 us)
Async XLA Ops:
  8.0 15.9 %collective-permute-start.1 = (bf16[3,1024]{1,0:T(4,128)(2,1)S(1)}, bf16[3,1024]{1,0:T(4,128)(2,1)S(1)}, u32[]{:S(2)}, u32[]{:S(2)}) collective-permute-start(bf16[3,1024]{1,0:T(4,128)(2,1)S(1)} %get-tuple-element.106), channel_id=1, source_target_pairs={{4,0},{8,4},{12,8},{16,12},{20,16},{24,20},{28,24},{32,28},{36,32}... | collective-permute-start | bytes 18440 | tf_op jit(solution)/shard_map/ppermute | solution.py:579
  18.0 52.1 %all-to-all-start = ((bf16[4,256,1280]{2,1,0:T(8,128)(2,1)}), bf16[4,256,1280]{2,1,0:T(8,128)(2,1)}, u32[]{:S(2)}, u32[]{:S(2)}) async-start(bf16[4,256,1280]{2,1,0:T(8,128)(2,1)} %copy-done.7), calls=%async_computation | async-start | bytes 5242880 | tf_op jit(solution)/shard_map/all_to_all | solution.py:460
  23.2 131.1 %all-gather.3.cloned.1.call-start = ((), (), s32[]{:S(2)}) async-start(), calls=%async_computation.13 | async-start | bytes 4325376 | tf_op jit(solution)/shard_map/all_gather | solution.py:678
  24.0 37.5 %collective-permute-start.2 = (bf16[2,72,1024]{2,1,0:T(8,128)(2,1)S(1)}, bf16[2,72,1024]{2,1,0:T(8,128)(2,1)S(1)}, u32[]{:S(2)}, u32[]{:S(2)}) collective-permute-start(bf16[2,72,1024]{2,1,0:T(8,128)(2,1)S(1)} %pad_maximum_fusion.4), channel_id=1, source_target_pairs={{0,1},{1,2},{2,3},{3,0},{4,5},{5,6},{6,7},{7,4},{8,9},{9,10},{10,1... | collective-permute-start | bytes 884744 | tf_op jit(solution)/shard_map/ppermute | solution.py:483
  25.6 42.7 %collective-permute-start.3 = (bf16[2,72,1024]{2,1,0:T(8,128)(2,1)S(1)}, bf16[2,72,1024]{2,1,0:T(8,128)(2,1)S(1)}, u32[]{:S(2)}, u32[]{:S(2)}) collective-permute-start(bf16[2,72,1024]{2,1,0:T(8,128)(2,1)S(1)} %pad_maximum_fusion.4), channel_id=1, source_target_pairs={{0,2},{1,3},{2,0},{3,1},{4,6},{5,7},{6,4},{7,5},{8,10},{9,11},{10,... | collective-permute-start | bytes 884744 | tf_op jit(solution)/shard_map/ppermute | solution.py:483
  29.6 38.7 %collective-permute-start.4 = (bf16[2,72,1024]{2,1,0:T(8,128)(2,1)S(1)}, bf16[2,72,1024]{2,1,0:T(8,128)(2,1)S(1)}, u32[]{:S(2)}, u32[]{:S(2)}) collective-permute-start(bf16[2,72,1024]{2,1,0:T(8,128)(2,1)S(1)} %pad_maximum_fusion.4), channel_id=1, source_target_pairs={{0,3},{1,0},{2,1},{3,2},{4,7},{5,4},{6,5},{7,6},{8,11},{9,8},{10,9... | collective-permute-start | bytes 884744 | tf_op jit(solution)/shard_map/ppermute | solution.py:483
  79.4 30.8 %collective-permute-start.5 = (bf16[256,1024]{1,0:T(8,128)(2,1)}, bf16[256,1024]{1,0:T(8,128)(2,1)}, u32[]{:S(2)}, u32[]{:S(2)}) collective-permute-start(bf16[256,1024]{1,0:T(8,128)(2,1)} %dynamic-slice_bitcast_fusion.5), channel_id=1, source_target_pairs={{0,1},{1,2},{2,3},{3,0},{4,5},{5,6},{6,7},{7,4},{8,9},{9,10},{10,1... | collective-permute-start | bytes 1572872 | tf_op jit(solution)/shard_map/ppermute | solution.py:475
  98.3 30.1 %all-to-all-start.1 = ((bf16[32,2,64,128]{3,2,1,0:T(8,128)(2,1)}), bf16[32,2,64,128]{3,2,1,0:T(8,128)(2,1)S(1)}, u32[]{:S(2)}, u32[]{:S(2)}) async-start(bf16[32,2,64,128]{3,2,1,0:T(8,128)(2,1)} %bitcast.17), calls=%async_computation.1 | async-start | bytes 2097152 | tf_op jit(solution)/shard_map/all_to_all | solution.py:460
  112.7 23.2 %collective-permute-start.6 = (bf16[256,1024]{1,0:T(8,128)(2,1)}, bf16[256,1024]{1,0:T(8,128)(2,1)}, u32[]{:S(2)}, u32[]{:S(2)}) collective-permute-start(bf16[256,1024]{1,0:T(8,128)(2,1)} %get-tuple-element.81), channel_id=1, source_target_pairs={{0,2},{1,3},{2,0},{3,1},{4,6},{5,7},{6,4},{7,5},{8,10},{9,11},{10,... | collective-permute-start | bytes 1572872 | tf_op jit(solution)/shard_map/ppermute | solution.py:475
  115.8 28.4 %collective-permute-start.7 = (bf16[256,1024]{1,0:T(8,128)(2,1)}, bf16[256,1024]{1,0:T(8,128)(2,1)}, u32[]{:S(2)}, u32[]{:S(2)}) collective-permute-start(bf16[256,1024]{1,0:T(8,128)(2,1)} %get-tuple-element.80), channel_id=1, source_target_pairs={{0,3},{1,0},{2,1},{3,2},{4,7},{5,4},{6,5},{7,6},{8,11},{9,8},{10,9... | collective-permute-start | bytes 1572872 | tf_op jit(solution)/shard_map/ppermute | solution.py:475
  130.0 43.2 %all-to-all-start.2 = ((bf16[32,2,48,128]{3,2,1,0:T(8,128)(2,1)}), bf16[32,2,48,128]{3,2,1,0:T(8,128)(2,1)S(1)}, u32[]{:S(2)}, u32[]{:S(2)}) async-start(bf16[32,2,48,128]{3,2,1,0:T(8,128)(2,1)} %copy-done.27), calls=%async_computation.2 | async-start | bytes 1572864 | tf_op jit(solution)/shard_map/all_to_all | solution.py:460
  185.1 19.9 %all-to-all-start.3 = ((bf16[4,144,1024]{2,1,0:T(8,128)(2,1)}), bf16[4,144,1024]{2,1,0:T(8,128)(2,1)}, u32[]{:S(2)}, u32[]{:S(2)}) async-start(bf16[4,144,1024]{2,1,0:T(8,128)(2,1)} %fusion.9), calls=%async_computation.3 | async-start | bytes 2359296 | tf_op jit(solution)/shard_map/all_to_all | solution.py:460
  195.6 16.4 %collective-permute-start.11 = (bf16[128,1024]{1,0:T(8,128)(2,1)}, bf16[128,1024]{1,0:T(8,128)(2,1)}, u32[]{:S(2)}, u32[]{:S(2)}) collective-permute-start(bf16[128,1024]{1,0:T(8,128)(2,1)} %get-tuple-element.89), channel_id=1, source_target_pairs={{0,1},{1,2},{2,3},{3,0},{4,5},{5,6},{6,7},{7,4},{8,9},{9,10},{10,1... | collective-permute-start | bytes 786440 | tf_op jit(solution)/shard_map/ppermute | solution.py:493
  197.0 19.3 %collective-permute-start.12 = (bf16[128,1024]{1,0:T(8,128)(2,1)}, bf16[128,1024]{1,0:T(8,128)(2,1)}, u32[]{:S(2)}, u32[]{:S(2)}) collective-permute-start(bf16[128,1024]{1,0:T(8,128)(2,1)} %get-tuple-element.91), channel_id=1, source_target_pairs={{0,2},{1,3},{2,0},{3,1},{4,6},{5,7},{6,4},{7,5},{8,10},{9,11},{10,... | collective-permute-start | bytes 786440 | tf_op jit(solution)/shard_map/ppermute | solution.py:493
  199.6 16.6 %collective-permute-start.13 = (bf16[128,1024]{1,0:T(8,128)(2,1)}, bf16[128,1024]{1,0:T(8,128)(2,1)}, u32[]{:S(2)}, u32[]{:S(2)}) collective-permute-start(bf16[128,1024]{1,0:T(8,128)(2,1)} %get-tuple-element.90), channel_id=1, source_target_pairs={{0,3},{1,0},{2,1},{3,2},{4,7},{5,4},{6,5},{7,6},{8,11},{9,8},{10,9... | collective-permute-start | bytes 786440 | tf_op jit(solution)/shard_map/ppermute | solution.py:493
  244.6 27.5 %all-to-all-start.5 = ((bf16[4,128,1024]{2,1,0:T(8,128)(2,1)}), bf16[4,128,1024]{2,1,0:T(8,128)(2,1)}, u32[]{:S(2)}, u32[]{:S(2)}) async-start(bf16[4,128,1024]{2,1,0:T(8,128)(2,1)} %bitcast.368), calls=%async_computation.5 | async-start | bytes 2097152 | tf_op jit(solution)/shard_map/all_to_all | solution.py:460
  264.6 18.8 %collective-permute-start.15 = (bf16[128,1024]{1,0:T(8,128)(2,1)}, bf16[128,1024]{1,0:T(8,128)(2,1)}, u32[]{:S(2)}, u32[]{:S(2)}) collective-permute-start(bf16[128,1024]{1,0:T(8,128)(2,1)} %get-tuple-element.88), channel_id=1, source_target_pairs={{0,2},{1,3},{2,0},{3,1},{4,6},{5,7},{6,4},{7,5},{8,10},{9,11},{10,... | collective-permute-start | bytes 786440 | tf_op jit(solution)/shard_map/ppermute | solution.py:493
  267.0 16.4 %collective-permute-start.16 = (bf16[128,1024]{1,0:T(8,128)(2,1)}, bf16[128,1024]{1,0:T(8,128)(2,1)}, u32[]{:S(2)}, u32[]{:S(2)}) collective-permute-start(bf16[128,1024]{1,0:T(8,128)(2,1)} %get-tuple-element.87), channel_id=1, source_target_pairs={{0,3},{1,0},{2,1},{3,2},{4,7},{5,4},{6,5},{7,6},{8,11},{9,8},{10,9... | collective-permute-start | bytes 786440 | tf_op jit(solution)/shard_map/ppermute | solution.py:493
  287.1 18.6 %all-to-all-start.6 = ((bf16[4,144,1024]{2,1,0:T(8,128)(2,1)}), bf16[4,144,1024]{2,1,0:T(8,128)(2,1)}, u32[]{:S(2)}, u32[]{:S(2)}) async-start(bf16[4,144,1024]{2,1,0:T(8,128)(2,1)} %broadcast_in_dim.163), calls=%async_computation.6 | async-start | bytes 2359296 | tf_op jit(solution)/shard_map/all_to_all | solution.py:460
  297.9 29.7 %collective-permute-start.17 = (bf16[4,128,1024]{2,1,0:T(8,128)(2,1)}, bf16[4,128,1024]{2,1,0:T(8,128)(2,1)}, u32[]{:S(2)}, u32[]{:S(2)}) collective-permute-start(bf16[4,128,1024]{2,1,0:T(8,128)(2,1)} %dynamic-slice_bitcast_fusion.2), channel_id=1, source_target_pairs={{0,4},{4,0},{8,12},{12,8},{16,20},{20,16},{24,28},{28,24},{32,36},... | collective-permute-start | bytes 3145736 | tf_op jit(solution)/shard_map/ppermute | solution.py:803
  311.0 38.7 %collective-permute-start.18 = (bf16[512,1024]{1,0:T(8,128)(2,1)}, bf16[512,1024]{1,0:T(8,128)(2,1)}, u32[]{:S(2)}, u32[]{:S(2)}) collective-permute-start(bf16[512,1024]{1,0:T(8,128)(2,1)} %get-tuple-element.123), channel_id=1, source_target_pairs={{0,4},{4,0},{8,12},{12,8},{16,20},{20,16},{24,28},{28,24},{32,36},... | collective-permute-start | bytes 3145736 | tf_op jit(solution)/shard_map/ppermute | solution.py:809
  320.5 31.1 %all-to-all-start.7 = ((bf16[32,2,48,128]{3,2,1,0:T(8,128)(2,1)}), bf16[32,2,48,128]{3,2,1,0:T(8,128)(2,1)}, u32[]{:S(2)}, u32[]{:S(2)}) async-start(bf16[32,2,48,128]{3,2,1,0:T(8,128)(2,1)} %bitcast.321), calls=%async_computation.7 | async-start | bytes 1572864 | tf_op jit(solution)/shard_map/all_to_all | solution.py:460
  375.5 56.9 %all-to-all-start.9 = ((bf16[32,4,2,64,128]{4,3,2,1,0:T(8,128)(2,1)}), bf16[32,4,2,64,128]{4,3,2,1,0:T(8,128)(2,1)}, u32[]{:S(2)}, u32[]{:S(2)}) async-start(bf16[32,4,2,64,128]{4,3,2,1,0:T(8,128)(2,1)} %get-tuple-element.45.refs_0_), calls=%async_computation.9 | async-start | bytes 8388608 | tf_op jit(solution)/shard_map/all_to_all | solution.py:460
  460.6 53.8 %all-to-all-start.10 = ((bf16[16,4,8,3456]{3,2,1,0:T(8,128)(2,1)}), bf16[16,4,8,3456]{3,2,1,0:T(8,128)(2,1)}, u32[]{:S(2)}, u32[]{:S(2)}) async-start(bf16[16,4,8,3456]{3,2,1,0:T(8,128)(2,1)} %pack.1), calls=%async_computation.10 | async-start | bytes 7077888 | tf_op jit(solution)/shard_map/all_to_all | solution.py:940
  (143 other events, 1259.3 us)
Sparse Core Ops, SparseCore 0:
  76.8 55.7 all-gather.2

commit v3 on v2

--- a/solution.py
+++ b/solution.py
@@ -106,6 +106,52 @@
     half = pl.program_id(0) % 2
     i = idx_ref[0]
     return jnp.where(half == 0, i, 2 * nctx - 1 - i) * BLK
+
+
+def proj_kernel(x_ref, w_ref, wdt_ref, gain_ref, *refs):
+    z_ref, ext_ref, dtr_ref, qkv_ref, act_ref = refs[-5:]
+    x = x_ref[...].astype(F32)
+    r = lax.rsqrt(jnp.mean(x * x, axis=1, keepdims=True) + EPS)
+    act_ref[...] = (x * r * gain_ref[...]).astype(BF16)
+    a = act_ref[...]
+
+    def columns(lo, width):
+        p = lax.dot_general(a, w_ref[:, lo : lo + width], (NN, ((), ())), preferred_element_type=F32)
+        return p.reshape(8, EXT, width)
+
+    z_ref[:, :, :256] = columns(0, 256)[:, 8:]
+    both = columns(256, 256)
+    z_ref[:, :, 256:] = both[:, 8:, :128]
+    ext_ref[:, :, :128] = both[:, :, 128:]
+    ext_ref[:, :, 128:384] = columns(512, 256)
+    ext_ref[:, :, 384:] = columns(768, 256)
+    qkv_ref[...] = columns(1024, 256)[:, 8:]
+    p = lax.dot_general(a, wdt_ref[...], (NN, ((), ())), preferred_element_type=F32)
+    dtr_ref[...] = p.reshape(8, EXT, 128)
+
+
+def mid_kernel(u_ref, w_ref, ss_ref, dep_ref, out_ref):
+    eye = iota((128, 128), 0) == iota((128, 128), 1)
+    for a in range(4):
+        part = lax.dot_general(
+            u_ref[128 * a : 128 * a + 128], w_ref[...], (NN, ((), ())), preferred_element_type=F32
+        )
+        out_ref[a, :128] = part.astype(BF16)
+        row = jnp.sum(jnp.where(eye, ss_ref[128 * a : 128 * a + 128], 0.0), axis=0, keepdims=True)
+        high = row.astype(BF16).astype(F32)
+        pair = jnp.concatenate([high, row - high, jnp.zeros((14, 128), F32)], axis=0)
+        pair = jnp.concatenate([pair, jnp.zeros((16, D - 128), F32)], axis=1)
+        out_ref[a, 128:] = pair.astype(BF16)
+
+
+def hold_kernel(value_ref, dep_ref, out_ref):
+    out_ref[...] = value_ref[...]
+
+
+def down_kernel(inner_ref, w_ref, dep_ref, out_ref):
+    out_ref[...] = lax.dot_general(
+        inner_ref[...], w_ref[...], (NN, ((), ())), preferred_element_type=F32
+    ).astype(BF16)
 
 
 def ssd_fwd_kernel(nctx, nk, pr, idx_ref, ext_ref, dtr_ref, st_ref, pv_ref, y_ref, swx_ref, c_ref, s_ref):
@@ -163,21 +209,38 @@
         out_ref[zz, :, 512:] = w_ref[:, FF + 512 * zz : FF + 512 * zz + 512]
 
 
-def total_kernel(n, got_ref, dep_ref, out_ref):
+def total_kernel(n, got_ref, *refs):
+    out_ref = refs[-1]
+
     def step(j, acc):
         return acc + got_ref[j].astype(F32)
 
     out_ref[...] = lax.fori_loop(1, n, step, got_ref[0].astype(F32))
 
 
-def pack_kernel(nj, rj, kin_ref, gin_ref, kex_ref, gex_ref, gu_ref, o_ref, out_ref):
+def pack_kernel(nj, rj, kin_ref, gin_ref, kex_ref, gex_ref, dep_ref, out_ref):
     for a in range(4):
         part = (kin_ref[a].astype(F32) + gin_ref[a].astype(F32)).astype(BF16)
         out_ref[:, a, :, :LPROJ] = part.reshape(nj, rj, LPROJ)
         part = (kex_ref[a].astype(F32) + gex_ref[a].astype(F32)).astype(BF16)
-        out_ref[:, a, :, LPROJ:1408] = part.reshape(nj, rj, 128)
-        out_ref[:, a, :, 1408:2432] = gu_ref[a].reshape(nj, rj, 1024)
-    out_ref[:, :, :, 2432:] = o_ref[...].reshape(nj, 4, rj, 1024)
+        out_ref[:, a, :, LPROJ:] = part.reshape(nj, rj, 128)
+
+
+def pack_early_kernel(nj, rj, gu_ref, o_ref, out_ref):
+    for a in range(4):
+        out_ref[:, a, :, :1024] = gu_ref[a].reshape(nj, rj, 1024)
+    out_ref[:, :, :, 1024:] = o_ref[...].reshape(nj, 4, rj, 1024)
+
+
+def totals_kernel(n, got_ref, early_ref, dep_ref, out_ref, o_ref):
+    def step(j, acc):
+        return acc[0] + got_ref[j].astype(F32), acc[1] + early_ref[j].astype(F32)
+
+    first = (got_ref[0].astype(F32), early_ref[0].astype(F32))
+    late, early = lax.fori_loop(1, n, step, first)
+    out_ref[:, :, :1408] = late
+    out_ref[:, :, 1408:] = early[:, :, :1024]
+    o_ref[...] = early[:, :, 1024:]
 
 
 def assemble_kernel(owned_ref, o_ref, out_ref):
@@ -199,17 +262,20 @@
     second = owned_ref[2, :, 1152:1280] + owned_ref[3, :, 1152:1280]
     put(3840, jnp.concatenate([first[:, :HDIM], second[:, :HDIM]], axis=1))
     put(3968, jnp.concatenate([first[:, HDIM:], second[:, HDIM:]], axis=1))
-    extras = [owned_ref[zz, :, 1280:1304] for zz in range(4)]
-    extras.append(jnp.zeros((extras[0].shape[0], 32), F32))
+    extras = [owned_ref[zz, :, 1280:1302] for zz in range(4)]
+    extras.append(jnp.zeros((extras[0].shape[0], 40), F32))
     put(8192, jnp.concatenate(extras, axis=1))
 
 
-def unpack_kernel(nj, rj, core_ref, mine_ref, other_ref, in_ref, gu_ref, ex_ref, down_ref, mo_ref, ao_ref):
+def unpack_kernel(nj, rj, core_ref, mine_ref, other_ref, w_ref, in_ref, mix_ref, gu_ref, ex_ref, down_ref, mo_ref, ao_ref):
     half = pl.program_id(0)
     core = core_ref[0]
 
     def write(src):
-        in_ref[...] = src[:, :, :4096].reshape(128, 4096).astype(F32)
+        total = src[:, :, :4096].reshape(128, 4096).astype(F32)
+        in_ref[...] = total
+        mix = jnp.sum(total * w_ref[...].astype(F32), axis=1, keepdims=True)
+        mix_ref[...] = jnp.broadcast_to(mix, (128, 128))
         gu_ref[...] = src[:, :, 4096:8192].reshape(128, 4096).astype(F32)
         ex_ref[...] = src[:, :, 8192:8320].reshape(128, 128).astype(F32)
         for j in range(nj):
@@ -397,8 +463,9 @@
 
 
 def attn_bwd_kernel(
-    nctx, gs, idx_ref, q_ref, kv_ref, st_ref, o_ref, lse_ref, do_ref, dq_ref, dkv_ref, del_ref, acc_ref
+    nctx, gs, idx_ref, q_ref, kv_ref, st_ref, o_ref, lse_ref, do_ref, *refs
 ):
+    dq_ref, keep_ref, give_ref, del_ref, acc_ref = refs[-5:]
     i = idx_ref[0]
     gi = i // gs
     acc_ref[...] = jnp.zeros(acc_ref.shape, F32)
@@ -419,11 +486,21 @@
         acc_ref[half, g] = acc_ref[half, g] + dkv
         dq_ref[0, rowset] = dq_ref[0, rowset] + dotb(ds, kv[:, :HDIM], NN)
     dq_ref[...] = dq_ref[...] * (HDIM**-0.5)
-    for g in range(4):
-        for half in range(2):
-            dkv_ref[g * gs : (g + 1) * gs, 0, half] = (
-                acc_ref[half, g].astype(BF16).reshape(gs, BLK, 128)
-            )
+
+    def write(even_ref, odd_ref):
+        for src in range(4 * gs):
+            g, at = src // gs, (src % gs) * BLK
+            ref = odd_ref if src % 2 else even_ref
+            for half in range(2):
+                ref[src // 2, 0, half] = acc_ref[half, g, at : at + BLK].astype(BF16)
+
+    @pl.when(i % 2 == 0)
+    def _():
+        write(keep_ref, give_ref)
+
+    @pl.when(i % 2 == 1)
+    def _():
+        write(give_ref, keep_ref)
 
 
 def spec(shape, index):
@@ -620,13 +697,22 @@
     inner_scale = inner_gain.astype(F32)
 
     rows = 8 * EXT
-    hidden_all = wide.reshape(rows, D).astype(F32)
-    norm_one = hidden_all * rms_of(hidden_all)
-    act_one = (norm_one * mixer_scale).astype(BF16)
-    projected = matmul(act_one, own_in).reshape(8, EXT, LPROJ)
-    raw_dt = matmul(act_one, own_dt).reshape(8, EXT, 128)
-    gate_z = projected[:, 8:, :LX]
-    conv_ext = projected[:, :, LX : LX + LCONV]
+    st_wide = jnp.broadcast_to(starts[:, :, None], (8, BLK, 128))
+    gate_z, conv_ext, raw_dt, qkv, act_one = pl.pallas_call(
+        proj_kernel,
+        in_specs=[VMEM] * 4 + [ANY] * 2,
+        out_specs=[VMEM] * 5,
+        out_shape=[
+            sds((8, BLK, LX), F32),
+            sds((8, EXT, LCONV), F32),
+            sds((8, EXT, 128), F32),
+            sds((8, BLK, 256), F32),
+            sds((rows, D), BF16),
+        ],
+        compiler_params=PARAMS,
+        cost_estimate=cost(2 * 10**9, 8 * 10**6),
+        name="proj",
+    )(wide.reshape(rows, D), own_in, own_dt, mixer_scale[None], pv, st_wide)
 
     blocks = jnp.stack([i, 2 * nctx - 1 - i])
     positions = blocks[:, None] * BLK + jnp.arange(BLK, dtype=jnp.int32)[None, :]
@@ -636,15 +722,14 @@
     angle = positions.astype(F32)[:, :, None] * freq
     cosine, sine = jnp.cos(angle), jnp.sin(angle)
     tables = (cosine[None, :, :, None, :], sine[None, :, :, None, :])
-    query = projected[:, 8:, 1024:1152].reshape(4, 2, BLK, 2, HDIM)
+    query = qkv[:, :, :128].reshape(4, 2, BLK, 2, HDIM)
     query = turn(query, *tables).astype(BF16) * jnp.asarray(HDIM**-0.5, BF16)
     query = query.transpose(0, 1, 3, 2, 4).reshape(4, 2, 2 * BLK, HDIM)
-    key = projected[:, 8:, 1152:1216].reshape(4, 2, BLK, 1, HDIM)
+    key = qkv[:, :, 128:192].reshape(4, 2, BLK, 1, HDIM)
     key = turn(key, *tables).astype(BF16).reshape(4, 2, BLK, HDIM)
-    value = projected[:, 8:, 1216:1280].astype(BF16).reshape(4, 2, BLK, HDIM)
+    value = qkv[:, :, 192:].astype(BF16).reshape(4, 2, BLK, HDIM)
     kv_own = jnp.concatenate([key, value], axis=-1)
 
-    st_wide = jnp.broadcast_to(starts[:, :, None], (8, BLK, 128))
     srows = LOCAL_HEADS * pr
     ssd_in = (idx, conv_ext, raw_dt, st_wide, pv)
     ssd_in_specs = [
@@ -677,6 +762,9 @@
     got = exchange(state_out.reshape(nctx, 2, srows + 16, 128), "ctx")
     kv_all = lax.all_gather(kv_own, "ctx")
 
+    st_rows = jnp.broadcast_to(
+        starts.reshape(4, 2, 1, BLK, 1), (4, 2, 2, BLK, 128)
+    ).reshape(4, 2, 2 * BLK, 128)
     def chain(reverse, terms, *after):
         return pl.pallas_call(
             functools.partial(scan_kernel, reverse, nctx, pr),
@@ -688,11 +776,8 @@
             name="chain",
         )(terms, got, *after)
 
-    entry = exchange(chain(False, got), "ctx").reshape(4, nk, 2, srows, 128)
-
-    st_rows = jnp.broadcast_to(
-        starts.reshape(4, 2, 1, BLK, 1), (4, 2, 2, BLK, 128)
-    ).reshape(4, 2, 2 * BLK, 128)
+    entry = exchange(chain(False, got, own_gu, grad_all, query, st_rows), "ctx").reshape(4, nk, 2, srows, 128)
+
     row_spec = pl.BlockSpec((1, 2, 2 * BLK, HDIM), lambda s: (s, 0, 0, 0))
     wide_spec = pl.BlockSpec((1, 2, 2 * BLK, 128), lambda s: (s, 0, 0, 0))
     kv_spec = pl.BlockSpec((nctx, 1, 2, BLK, 128), lambda s: (0, s, 0, 0, 0))
@@ -744,9 +829,16 @@
         return jnp.sum(got_rows.astype(F32), axis=0)
 
     attn_mid = ring_sum(matmul(act_attn, attn_out), z)
-    scaled_part = matmul(scaled_u.reshape(512, LX), mamba_out).astype(BF16).reshape(4, 128, D)
-    square_rows = as_rows(squares[:, :, 0].reshape(4, 128))
-    got_part = exchange(jnp.concatenate([scaled_part, square_rows], axis=1), "fsdp")
+    part_rows = pl.pallas_call(
+        mid_kernel,
+        in_specs=[VMEM] * 3 + [ANY],
+        out_specs=VMEM,
+        out_shape=sds((4, 144, D), BF16),
+        compiler_params=PARAMS,
+        cost_estimate=cost(4 * 10**8, 3 * 10**6),
+        name="mid_part",
+    )(scaled_u.reshape(512, LX), mamba_out, squares.reshape(512, 128), attn_mid)
+    got_part = exchange(part_rows, "fsdp")
     scaled_mid = jnp.sum(got_part[:, :128].astype(F32), axis=0)
     square_sum = jnp.sum(from_rows(got_part[:, 128:]), axis=0)
     own_r = lax.rsqrt(square_sum.reshape(128, 1) * (1.0 / 1536) + EPS)
@@ -776,7 +868,6 @@
     grad_gate = grad_inner * up_val * (gate_sig * (1.0 + gate_val * (1.0 - gate_sig)))
     grad_gu = jnp.concatenate([grad_gate, grad_inner * gate_silu], axis=1).astype(BF16)
     grad_act_two = gather_sum(matmul(grad_gu, own_gu, NT))
-    mixed = (middle + ring_sum(matmul(inner, w_down), z)).astype(BF16).reshape(1, 2, BLK, D)
     grad_down = matmul(inner, grad_all, TN).astype(BF16)
     grad_gate_up = matmul(act_two, grad_gu, TN).astype(BF16)
     grad_ffn_gain = jnp.sum(grad_act_two * norm_two, axis=0)
@@ -784,6 +875,17 @@
     own_mix = grad_middle.astype(BF16)
     own_dots = jnp.sum(own_mix.astype(F32) * mamba_mid, axis=1) * (1.0 / 1536)
     grad_mix, dots = spread_rows(own_mix, own_dots)
+
+    down_part = pl.pallas_call(
+        down_kernel,
+        in_specs=[VMEM, VMEM, ANY],
+        out_specs=VMEM,
+        out_shape=sds((512, D), BF16),
+        compiler_params=PARAMS,
+        cost_estimate=cost(5 * 10**8, 3 * 10**6),
+        name="down",
+    )(inner, w_down, grad_mix)
+    mixed = (middle + ring_sum(down_part, z)).astype(BF16).reshape(1, 2, BLK, D)
 
     grad_m = matmul(grad_mix, mamba_out, NT)
     grad_n = grad_m * inner_scale
@@ -824,12 +926,17 @@
         name="leak",
     )(grad_y, swx, c_mat)
     got_leak = exchange(leak.reshape(nctx, 2, srows, 128), "ctx")
-    grad_query, grad_kv = pl.pallas_call(
+    half_kv_spec = pl.BlockSpec((nctx // 2, 1, 2, BLK, 128), lambda s: (0, s, 0, 0, 0))
+    grad_query, keep_kv, give_kv = pl.pallas_call(
         functools.partial(attn_bwd_kernel, nctx, gs),
         grid=(4,),
-        in_specs=[SMEM, row_spec, kv_spec, wide_spec, row_spec, wide_spec, row_spec],
-        out_specs=[row_spec, kv_spec],
-        out_shape=[sds((4, 2, 2 * BLK, HDIM), F32), sds((nctx, 4, 2, BLK, 128), BF16)],
+        in_specs=[SMEM, row_spec, kv_spec, wide_spec, row_spec, wide_spec, row_spec] + [ANY] * 5,
+        out_specs=[row_spec, half_kv_spec, half_kv_spec],
+        out_shape=[
+            sds((4, 2, 2 * BLK, HDIM), F32),
+            sds((nctx // 2, 4, 2, BLK, 128), BF16),
+            sds((nctx // 2, 4, 2, BLK, 128), BF16),
+        ],
         scratch_shapes=[
             pltpu.VMEM((2, 2 * BLK, 128), F32),
             pltpu.VMEM((2, 4, gs * BLK, 128), F32),
@@ -837,23 +944,26 @@
         compiler_params=PARAMS,
         cost_estimate=cost(8 * 10**9, 16 * 10**6, 2 * 10**6),
         name="attn_bwd",
-    )(idx, query, kv_all, st_rows, attn_o, lse, grad_attn)
-    grad_exit = exchange(chain(True, got_leak, grad_kv, pair_gu, pair_o), "ctx").reshape(4, nk, 2, srows, 128)
-    grad_kv = pl.pallas_call(
-        functools.partial(total_kernel, nctx),
+    )(
+        idx, query, kv_all, st_rows, attn_o, lse, grad_attn,
+        leak, grad_gate_up, grad_down, grad_mamba_out, grad_attn_out,
+    )
+    chained = chain(True, got_leak, give_kv)
+    grad_exit = exchange(chained, "ctx").reshape(4, nk, 2, srows, 128)
+    give_kv = pl.pallas_call(
+        hold_kernel,
         in_specs=[VMEM, ANY],
         out_specs=VMEM,
-        out_shape=sds((4, 2, BLK, 128), F32),
-        compiler_params=PARAMS,
-        cost_estimate=cost(2 * 10**6, 4 * 10**6),
-        name="total_kv",
-    )(exchange(grad_kv, "ctx"), mixed)
-    back = (tables[0], -tables[1])
-    grad_key = turn(grad_kv[..., :HDIM].reshape(4, 2, BLK, 1, HDIM), *back).reshape(8, BLK, HDIM)
-    grad_value = grad_kv[..., HDIM:].reshape(8, BLK, HDIM)
-    grad_query = grad_query.reshape(4, 2, 2, BLK, HDIM).transpose(0, 1, 3, 2, 4)
-    grad_query = turn(grad_query, *back).reshape(8, BLK, 128)
-
+        out_shape=sds(give_kv.shape, BF16),
+        compiler_params=PARAMS,
+        cost_estimate=cost(0, 4 * 10**6),
+        name="hold",
+    )(give_kv, chained)
+    taken_kv = lax.ppermute(give_kv, "ctx", pair)
+    pair_kv = (keep_kv.astype(F32) + taken_kv.astype(F32)).astype(BF16)
+    nj = nctx // 2
+    rj = 128 // nj
+    groups = [[2 * j + c for j in range(nj)] for c in range(2)]
     grad_ext, grad_dt, misc = pl.pallas_call(
         functools.partial(ssd_bwd_kernel, nctx, nk, pr),
         grid=(8,),
@@ -870,6 +980,53 @@
         name="ssd_bwd",
     )(*ssd_in, grad_y, entry, grad_exit)
 
+    grad_dt = grad_dt.reshape(rows, 128)
+    grad_dtw = matmul(act_one, grad_dt, TN)
+    misc = jnp.sum(misc, axis=0)
+    grad_skip = jnp.sum(misc[5, :LX].reshape(LOCAL_HEADS, HDIM), axis=1)
+    small = jnp.concatenate(
+        [misc[:5].reshape(-1), misc[6, :6], misc[7, :6], grad_skip, grad_inner_gain]
+    )
+    small = jnp.pad(small, (0, 3840 - small.shape[0])).reshape(1, 256, 15)
+    small = jnp.broadcast_to(small, (4, 256, 15)).reshape(D, 15)
+    extras = jnp.concatenate(
+        [
+            grad_dtw[:, :6],
+            grad_ffn_gain[:, None],
+            small,
+            jnp.zeros((D, 106), F32),
+        ],
+        axis=1,
+    ).astype(BF16)
+    early = pl.pallas_call(
+        functools.partial(pack_early_kernel, nj, rj),
+        in_specs=[VMEM] * 2,
+        out_specs=VMEM,
+        out_shape=sds((nj, 4, rj, 2048), BF16),
+        compiler_params=PARAMS,
+        cost_estimate=cost(0, 4 * 10**6),
+        name="pack_early",
+    )(pair_gu, pair_o)
+
+    def core_exchange(parts):
+        return lax.all_to_all(parts, "ctx", 0, 0, axis_index_groups=groups, tiled=True)
+
+    grad_kv = pl.pallas_call(
+        functools.partial(total_kernel, nj),
+        in_specs=[VMEM] + [ANY] * 3,
+        out_specs=VMEM,
+        out_shape=sds((4, 2, BLK, 128), F32),
+        compiler_params=PARAMS,
+        cost_estimate=cost(2 * 10**6, 4 * 10**6),
+        name="total_kv",
+    )(core_exchange(pair_kv), mixed, early, extras)
+    got_early = core_exchange(early)
+    back = (tables[0], -tables[1])
+    grad_key = turn(grad_kv[..., :HDIM].reshape(4, 2, BLK, 1, HDIM), *back).reshape(8, BLK, HDIM)
+    grad_value = grad_kv[..., HDIM:].reshape(8, BLK, HDIM)
+    grad_query = grad_query.reshape(4, 2, 2, BLK, HDIM).transpose(0, 1, 3, 2, 4)
+    grad_query = turn(grad_query, *back).reshape(8, BLK, 128)
+
     def lead(v):
         return jnp.pad(v.astype(BF16), ((0, 0), (8, 0), (0, 0)))
 
@@ -881,7 +1038,6 @@
         ],
         axis=-1,
     ).reshape(rows, LPROJ)
-    grad_dt = grad_dt.reshape(rows, 128)
     grad_act = matmul(grad_proj, own_in, NT) + matmul(grad_dt, own_dt, NT)
 
     got_act = ring_sum(grad_act, z).reshape(2, EXT, D)
@@ -896,49 +1052,27 @@
     grad_tokens = grad_tokens.reshape(1, 2, BLK, D)
 
     grad_in = matmul(act_one, grad_proj, TN).astype(BF16)
-    grad_dtw = matmul(act_one, grad_dt, TN)
-    misc = jnp.sum(misc, axis=0)
-    grad_skip = jnp.sum(misc[5, :LX].reshape(LOCAL_HEADS, HDIM), axis=1)
-    small = jnp.concatenate(
-        [misc[:5].reshape(-1), misc[6, :6], misc[7, :6], grad_skip, grad_inner_gain]
-    )
-    small = jnp.pad(small, (0, 3840 - small.shape[0])).reshape(1, 256, 15)
-    small = jnp.broadcast_to(small, (4, 256, 15)).reshape(D, 15)
-    grad_mixer_gain = jnp.sum(grad_act * norm_one, axis=0)
-    extras = jnp.concatenate(
-        [
-            grad_dtw[:, :6],
-            grad_mixer_gain[:, None],
-            grad_ffn_gain[:, None],
-            small,
-            jnp.zeros((D, 105), F32),
-        ],
-        axis=1,
-    ).astype(BF16)
-    nj = nctx // 2
-    rj = 128 // nj
-    groups = [[2 * j + c for j in range(nj)] for c in range(2)]
     kept_in, taken_in = halves(grad_in)
     kept_ex, taken_ex = halves(extras)
     sent = pl.pallas_call(
         functools.partial(pack_kernel, nj, rj),
-        in_specs=[VMEM] * 6,
+        in_specs=[VMEM] * 4 + [ANY],
         out_specs=VMEM,
-        out_shape=sds((nj, 4, rj, 3456), BF16),
+        out_shape=sds((nj, 4, rj, 1408), BF16),
         compiler_params=PARAMS,
         cost_estimate=cost(0, 7 * 10**6),
         name="pack",
-    )(kept_in, taken_in, kept_ex, taken_ex, pair_gu, pair_o)
-    summed = pl.pallas_call(
-        functools.partial(total_kernel, nj),
-        in_specs=[VMEM, ANY],
-        out_specs=VMEM,
-        out_shape=sds((4, rj, 3456), F32),
+    )(kept_in, taken_in, kept_ex, taken_ex, got_early)
+    summed, summed_o = pl.pallas_call(
+        functools.partial(totals_kernel, nj),
+        in_specs=[VMEM, VMEM, ANY],
+        out_specs=[VMEM, VMEM],
+        out_shape=[sds((4, rj, 2432), F32), sds((4, rj, 1024), F32)],
         compiler_params=PARAMS,
         cost_estimate=cost(2 * 10**6, 4 * 10**6),
-        name="total",
-    )(lax.all_to_all(sent, "ctx", 0, 0, axis_index_groups=groups, tiled=True), got_act)
-    owned = exchange(summed[:, :, :2432], "fsdp")
+        name="totals",
+    )(core_exchange(sent), got_early, got_act)
+    owned = exchange(summed, "fsdp")
     final = pl.pallas_call(
         assemble_kernel,
         in_specs=[VMEM] * 2,
@@ -947,19 +1081,17 @@
         compiler_params=PARAMS,
         cost_estimate=cost(0, 10**6),
         name="assemble",
-    )(owned, summed[:, :, 2432:])
-    mine_all = lax.all_to_all(
-        jnp.broadcast_to(final[None], (nj, rj, 12416)),
-        "ctx", 0, 0, axis_index_groups=groups, tiled=True,
-    )
+    )(owned, summed_o)
+    mine_all = core_exchange(jnp.broadcast_to(final[None], (nj, rj, 12416)))
     other_all = lax.ppermute(mine_all, "ctx", pair)
     half_spec = pl.BlockSpec((128, 4096), lambda h: (h, 0))
-    total_in, total_gate_up, extra, total_down, total_mamba_out, total_attn_out = pl.pallas_call(
+    total_in, mixer_dot, total_gate_up, extra, total_down, total_mamba_out, total_attn_out = pl.pallas_call(
         functools.partial(unpack_kernel, nj, rj),
         grid=(2,),
-        in_specs=[SMEM, whole((nj, rj, 12416)), whole((nj, rj, 12416))],
+        in_specs=[SMEM, whole((nj, rj, 12416)), whole((nj, rj, 12416)), half_spec],
         out_specs=[
             half_spec,
+            pl.BlockSpec((128, 128), lambda h: (h, 0)),
             half_spec,
             pl.BlockSpec((128, 128), lambda h: (h, 0)),
             whole((512, 1024)),
@@ -968,6 +1100,7 @@
         ],
         out_shape=[
             sds((256, 4096), F32),
+            sds((256, 128), F32),
             sds((256, 4096), F32),
             sds((256, 128), F32),
             sds((512, 1024), F32),
@@ -977,12 +1110,13 @@
         compiler_params=PARAMS,
         cost_estimate=cost(0, 10**7),
         name="unpack",
-    )(core.astype(jnp.int32).reshape(1), mine_all, other_all)
-    extra = extra[:, :96].reshape(256, 4, 24)
+    )(core.astype(jnp.int32).reshape(1), mine_all, other_all, w_in)
+    extra = extra[:, :88].reshape(256, 4, 22)
     total_dt = extra[:, :, :6].reshape(256, 24)
-    total_mixer = jnp.sum(extra[:, :, 6], axis=1)
-    total_ffn = jnp.sum(extra[:, :, 7], axis=1)
-    small = extra[:, :, 8:23].transpose(1, 0, 2).reshape(4, 3840)
+    mixer_dot = mixer_dot[:, 0] + jnp.sum(total_dt * w_dt.astype(F32), axis=1)
+    total_mixer = mixer_dot / mixer_gain.astype(F32)
+    total_ffn = jnp.sum(extra[:, :, 6], axis=1)
+    small = extra[:, :, 7:22].transpose(1, 0, 2).reshape(4, 3840)
     taps = small[:, :3200].reshape(4, 5, LCONV)
     taps = jnp.concatenate(
         [

time: 627 us -> 605 us (0.965)
  blocking collectives: 94.8 us -> 69.6 us
  starting transfers between devices: 110 us -> 101 us
  local copies, waits for them, and re-layouts: 83.1 us -> 91.1 us
  other arithmetic: 35.9 us -> 42.5 us
  Pallas kernels: 79.9 us -> 86.2 us
    all_to_all x1 -> x3, waiting for transfers between devices: 31.3 us -> 15.1 us  [core_exchange(): lax.all_to_all(parts, 'ctx', 0, 0, axis_index_groups=groups, tiled=True)]
    ppermute x6, waiting for transfers between devices: 44.4 us -> 59 us  [ring_spread(): got = lax.ppermute(part, 'fsdp', perm)]
    all_to_all x2, blocking collectives: 40.6 us -> 26 us  [exchange(): return lax.all_to_all(parts, axis, 0, 0, tiled=True)]
    unnamed x256 -> x274, local copies, waits for them, and re-layouts: 36.6 us -> 50.1 us
    all_to_all x1, blocking collectives: 54.2 us -> 43.6 us  [core_exchange(): lax.all_to_all(parts, 'ctx', 0, 0, axis_index_groups=groups, tiled=True)]
    all_to_all x1 -> x3, starting transfers between devices: 6.1 us -> 16.5 us  [core_exchange(): lax.all_to_all(parts, 'ctx', 0, 0, axis_index_groups=groups, tiled=True)]
    all_to_all x9 -> x8, starting transfers between devices: 57.6 us -> 50.9 us  [exchange(): return lax.all_to_all(parts, axis, 0, 0, tiled=True)]
    all_to_all x9 -> x8, waiting for transfers between devices: 46.6 us -> 41.4 us  [exchange(): return lax.all_to_all(parts, axis, 0, 0, tiled=True)]
  transfers between devices with their start and end apart: 38 -> 40, of which waited for: 22 -> 19; matrix products, arithmetic and copies ran while one was open for 14% -> 14% of each run, Pallas kernels for 9% -> 11%
where the time goes in v3:
time: 605 us; the launch traced here: 593 us
  waiting for transfers between devices  157 us (26%)
  starting transfers between devices  101 us (17%)
  local copies, waits for them, and re-layouts  91.1 us (15%)
  Pallas kernels  86.2 us (14%)
  blocking collectives  69.6 us (12%)
  other arithmetic  42.5 us (7%)
  matrix products  29.5 us (5%)
  between operations  16.5 us (3%)
    ppermute x6, waiting for transfers between devices, ring_spread(): got = lax.ppermute(part, 'fsdp', perm)  59 us
    all_to_all x8, starting transfers between devices, exchange(): return lax.all_to_all(parts, axis, 0, 0, tiled=True)  50.9 us
    unnamed x274, local copies, waits for them, and re-layouts  50.1 us
    all_to_all x1, blocking collectives, core_exchange(): lax.all_to_all(parts, 'ctx', 0, 0, axis_index_groups=groups, tiled=True)  43.6 us
    all_to_all x8, waiting for transfers between devices, exchange(): return lax.all_to_all(parts, axis, 0, 0, tiled=True)  41.4 us
    dot_general x14, matrix products, matmul(): return lax.dot_general(a, b, (dims, ((), ())), preferred_element_type=F32)  29.5 us
    ppermute x9, waiting for transfers between devices, ring_sum(): total = total + lax.ppermute(sent, 'fsdp', perm).astype(F32)  26.7 us
    all_to_all x2, blocking collectives, exchange(): return lax.all_to_all(parts, axis, 0, 0, tiled=True)  26 us
  transfers between devices with their start and end apart: 40, of which 19 were waited for; matrix products, arithmetic and copies ran while one was open for 14% of the time, Pallas kernels for 11%

profile of v3, /device:TPU:1, one launch (start us, length us, event | category | flops | bytes accessed | tf_op | source)
XLA Modules:
  0.0 593.4 jit_solution(11421140711445188839)
XLA Ops:
  18.0 5.2 all-to-all-start
  30.7 30.8 %collective-permute-done.2 = bf16[2,72,1024]{2,1,0:T(8,128)(2,1)S(1)} collective-permute-done((bf16[2,72,1024]{2,1,0:T(8,128)(2,1)S(1)}, bf16[2,72,1024]{2,1,0:T(8,128)(2,1)S(1)}, u32[]{:S(2)}, u32[]{:S(2)}) %collective-permute-start.2) | collective-permute-done | bytes 294944 | tf_op jit(solution)/shard_map/ppermute | solution.py:560
  61.7 6.7 %collective-permute-done.3 = bf16[2,72,1024]{2,1,0:T(8,128)(2,1)S(1)} collective-permute-done((bf16[2,72,1024]{2,1,0:T(8,128)(2,1)S(1)}, bf16[2,72,1024]{2,1,0:T(8,128)(2,1)S(1)}, u32[]{:S(2)}, u32[]{:S(2)}) %collective-permute-start.3) | collective-permute-done | bytes 294944 | tf_op jit(solution)/shard_map/ppermute | solution.py:560
  86.1 10.4 %collective-permute-done.5 = bf16[256,1024]{1,0:T(8,128)(2,1)S(1)} collective-permute-done((bf16[256,1024]{1,0:T(8,128)(2,1)S(1)}, bf16[256,1024]{1,0:T(8,128)(2,1)S(1)}, u32[]{:S(2)}, u32[]{:S(2)}) %collective-permute-start.5) | collective-permute-done | bytes 524320 | tf_op jit(solution)/shard_map/ppermute | solution.py:552
  97.6 21.5 %collective-permute-done.8 = bf16[128,1024]{1,0:T(8,128)(2,1)} collective-permute-done((bf16[128,1024]{1,0:T(8,128)(2,1)}, bf16[128,1024]{1,0:T(8,128)(2,1)}, u32[]{:S(2)}, u32[]{:S(2)}) %collective-permute-start.8) | collective-permute-done | bytes 262176 | tf_op jit(solution)/shard_map/ppermute | solution.py:560
  124.6 8.3 %ssd_fwd.1 = (f32[8,64,384]{2,1,0:T(8,128)S(1)}, f32[8,64,384]{2,1,0:T(8,128)S(1)}, bf16[8,64,128]{2,1,0:T(8,128)(2,1)S(1)}, bf16[4,8,2,64,128]{4,3,2,1,0:T(8,128)(2,1)S(1)}) custom-call(s32[1]{0:T(128)} %bitcast.1.idx_ref, f32[8,72,640]{2,1,0:T(8,128)S(1)} %copy-done.17, f32[8,72,128]{2,1,0:T(8,128)S(1)} %copy-done.54, s32[8,64,128]{2,1,0:T(8,128)S(1)} %copy-done.30, ...), custom_call_target="tpu_custom_call" | custom-call | flops 2000000 | bytes 6000 | tf_op jit(solution)/shard_map/ssd_fwd/pallas_call | solution.py:742
  135.6 8.6 %all-to-all-start.1 = ((bf16[32,2,64,128]{3,2,1,0:T(8,128)(2,1)}), bf16[32,2,64,128]{3,2,1,0:T(8,128)(2,1)S(1)}, u32[]{:S(2)}, u32[]{:S(2)}) async-start(bf16[32,2,64,128]{3,2,1,0:T(8,128)(2,1)} %bitcast.308), calls=%async_computation.1 | async-start | bytes 2097152 | tf_op jit(solution)/shard_map/all_to_all | solution.py:537
  154.6 6.4 %all-to-all-done.1.st_ref.dec_ref = bf16[32,2,64,128]{3,2,1,0:T(8,128)(2,1)S(1)} async-done(((bf16[32,2,64,128]{3,2,1,0:T(8,128)(2,1)}), bf16[32,2,64,128]{3,2,1,0:T(8,128)(2,1)S(1)}, u32[]{:S(2)}, u32[]{:S(2)}) %all-to-all-start.1) | async-done | bytes 1048608 | tf_op jit(solution)/shard_map/all_to_all | solution.py:537
  171.0 13.4 %attn_fwd.1 = (f32[4,2,128,64]{3,2,1,0:T(8,128)S(1)}, f32[4,2,128,128]{3,2,1,0:T(8,128)S(1)}) custom-call(s32[1]{0:T(128)} %bitcast.1.idx_ref, bf16[4,2,128,64]{3,2,1,0:T(8,128)(2,1)S(1)} %bitcast.302, bf16[32,4,2,64,128]{4,3,2,1,0:T(8,128)(2,1)} %bitcast.318, s32[4,2,128,128]{3,2,1,0:T(8,128)S(1)} %copy-done.12, bf16[1024,1024]{1,0:T(8,128)(2,1)S(1)} %bitcast.286, ...), custom_call_target="tpu_custom_call" | custom-call | flops 4000000 | bytes 8000 | tf_op jit(solution)/shard_map/attn_fwd/pallas_call | solution.py:784
  216.5 16.2 %all-to-all-done.3 = bf16[4,144,1024]{2,1,0:T(8,128)(2,1)} async-done(((bf16[4,144,1024]{2,1,0:T(8,128)(2,1)}), bf16[4,144,1024]{2,1,0:T(8,128)(2,1)}, u32[]{:S(2)}, u32[]{:S(2)}) %all-to-all-start.3) | async-done | bytes 1179680 | tf_op jit(solution)/shard_map/all_to_all | solution.py:537
  237.5 17.7 %all_to_all.70 = bf16[4,144,1024]{2,1,0:T(8,128)(2,1)S(1)} all-to-all(bf16[4,144,1024]{2,1,0:T(8,128)(2,1)S(1)} %broadcast_in_dim.169), channel_id=1, replica_groups=mesh['ctx'=32,'fsdp'=4] {'fsdp'}, dimensions={0} | all-to-all | bytes 2359296 | tf_op jit(solution)/shard_map/all_to_all | solution.py:537
  268.5 12.3 %all-to-all-done.5 = bf16[4,128,1024]{2,1,0:T(8,128)(2,1)} async-done(((bf16[4,128,1024]{2,1,0:T(8,128)(2,1)}), bf16[4,128,1024]{2,1,0:T(8,128)(2,1)}, u32[]{:S(2)}, u32[]{:S(2)}) %all-to-all-start.5) | async-done | bytes 1048608 | tf_op jit(solution)/shard_map/all_to_all | solution.py:537
  312.9 12.4 %all-to-all-start.7 = ((bf16[32,2,48,128]{3,2,1,0:T(8,128)(2,1)}), bf16[32,2,48,128]{3,2,1,0:T(8,128)(2,1)S(1)}, u32[]{:S(2)}, u32[]{:S(2)}) async-start(bf16[32,2,48,128]{3,2,1,0:T(8,128)(2,1)} %bitcast.61), calls=%async_computation.7 | async-start | bytes 1572864 | tf_op jit(solution)/shard_map/all_to_all | solution.py:537
  330.7 16.6 %attn_bwd.1 = (f32[4,2,128,64]{3,2,1,0:T(8,128)S(1)}, bf16[16,4,2,64,128]{4,3,2,1,0:T(8,128)(2,1)}, bf16[16,4,2,64,128]{4,3,2,1,0:T(8,128)(2,1)}) custom-call(s32[1]{0:T(128)} %bitcast.1.idx_ref, bf16[4,2,128,64]{3,2,1,0:T(8,128)(2,1)S(1)} %bitcast.303, bf16[32,4,2,64,128]{4,3,2,1,0:T(8,128)(2,1)} %bitcast.319, s32[4,2,128,128]{3,2,1,0:T(8,128)S(1)} %copy-done.13, ...), custom_call_target="tpu_custom_call" | custom-call | flops 8000000 | bytes 16000 | tf_op jit(solution)/shard_map/attn_bwd/pallas_call | solution.py:930
  355.7 7.4 %all-to-all-start.8 = ((bf16[32,2,48,128]{3,2,1,0:T(8,128)(2,1)}), bf16[32,2,48,128]{3,2,1,0:T(8,128)(2,1)S(1)}, u32[]{:S(2)}, u32[]{:S(2)}) async-start(bf16[32,2,48,128]{3,2,1,0:T(8,128)(2,1)} %chain.3.dep_ref), calls=%async_computation.8 | async-start | bytes 1572864 | tf_op jit(solution)/shard_map/all_to_all | solution.py:537
  378.2 5.0 all-to-all-start.9
  393.8 6.9 %collective-permute-done.14 = bf16[128,1024]{1,0:T(8,128)(2,1)} collective-permute-done((bf16[128,1024]{1,0:T(8,128)(2,1)}, bf16[128,1024]{1,0:T(8,128)(2,1)}, u32[]{:S(2)}, u32[]{:S(2)}) %collective-permute-start.14) | collective-permute-done | bytes 262176 | tf_op jit(solution)/shard_map/ppermute | solution.py:570
  407.6 15.0 %ssd_bwd.1 = (bf16[8,72,640]{2,1,0:T(8,128)(2,1)S(1)}, bf16[8,72,128]{2,1,0:T(8,128)(2,1)S(1)}, f32[8,8,640]{2,1,0:T(8,128)S(1)}) custom-call(s32[1]{0:T(128)} %bitcast.1.idx_ref, f32[8,72,640]{2,1,0:T(8,128)S(1)} %copy-done.18, f32[8,72,128]{2,1,0:T(8,128)S(1)} %copy-done.55, s32[8,64,128]{2,1,0:T(8,128)S(1)} %copy-done.31, f32[8,640]{1,0:T(8,128)S(1)} %copy-done.79, ...), custom_call_target="tpu_custom_call" | custom-call | flops 4000000 | bytes 8000 | tf_op jit(solution)/shard_map/ssd_bwd/pallas_call | solution.py:967
  433.3 6.7 %all-to-all-start.10 = ((bf16[16,4,8,2048]{3,2,1,0:T(8,128)(2,1)}), bf16[16,4,8,2048]{3,2,1,0:T(8,128)(2,1)S(1)}, u32[]{:S(2)}, u32[]{:S(2)}) async-start(bf16[16,4,8,2048]{3,2,1,0:T(8,128)(2,1)} %copy-done.4), calls=%async_computation.10 | async-start | bytes 4194304 | tf_op jit(solution)/shard_map/all_to_all | solution.py:1012
  453.9 15.1 %all-to-all-done.10.dep_ref.early_ref = bf16[16,4,8,2048]{3,2,1,0:T(8,128)(2,1)S(1)} async-done(((bf16[16,4,8,2048]{3,2,1,0:T(8,128)(2,1)}), bf16[16,4,8,2048]{3,2,1,0:T(8,128)(2,1)S(1)}, u32[]{:S(2)}, u32[]{:S(2)}) %all-to-all-start.10) | async-done | bytes 2097184 | tf_op jit(solution)/shard_map/all_to_all | solution.py:1012
  491.2 8.8 %collective-permute-done.20 = bf16[144,1024]{1,0:T(8,128)(2,1)S(1)} collective-permute-done((bf16[144,1024]{1,0:T(8,128)(2,1)S(1)}, bf16[144,1024]{1,0:T(8,128)(2,1)S(1)}, u32[]{:S(2)}, u32[]{:S(2)}) %collective-permute-start.20) | collective-permute-done | bytes 294944 | tf_op jit(solution)/shard_map/ppermute | solution.py:570
  503.1 8.3 %all_to_all.71.owned_ref = f32[4,8,2432]{2,1,0:T(8,128)S(1)} all-to-all(f32[4,8,2432]{2,1,0:T(8,128)S(1)} %get-tuple-element.65), channel_id=1, replica_groups=mesh['ctx'=32,'fsdp'=4] {'fsdp'}, dimensions={0} | all-to-all | bytes 622592 | tf_op jit(solution)/shard_map/all_to_all | solution.py:537
  511.7 43.6 %all_to_all.72.mine_ref = bf16[16,8,12416]{2,1,0:T(8,128)(2,1)S(1)} all-to-all(bf16[16,8,12416]{2,1,0:T(8,128)(2,1)S(1)} %broadcast_in_dim.180), channel_id=1, replica_groups={{0,8,16,24,32,40,48,56,64,72,80,88,96,104,112,120},{4,12,20,28,36,44,52..., dimensions={0} | all-to-all | bytes 6356992 | tf_op jit(solution)/shard_map/all_to_all | solution.py:1012
  571.7 7.5 %unpack.1 = (f32[256,4096]{1,0:T(8,128)}, f32[256,128]{1,0:T(8,128)S(1)}, f32[256,4096]{1,0:T(8,128)}, f32[256,128]{1,0:T(8,128)S(1)}, f32[512,1024]{1,0:T(8,128...) custom-call(s32[1]{0:T(128)} %bitcast.92.core_ref, bf16[16,8,12416]{2,1,0:T(8,128)(2,1)S(1)} %all_to_all.72.mine_ref, ...), custom_call_target="tpu_custom_call" | custom-call | bytes 10000 | tf_op jit(solution)/shard_map/unpack/pallas_call | solution.py:1088
  (543 shorter events, 266.3 us)
Async XLA Ops:
  18.0 52.4 %all-to-all-start = ((bf16[4,256,1280]{2,1,0:T(8,128)(2,1)}), bf16[4,256,1280]{2,1,0:T(8,128)(2,1)}, u32[]{:S(2)}, u32[]{:S(2)}) async-start(bf16[4,256,1280]{2,1,0:T(8,128)(2,1)} %split_in.1), calls=%async_computation | async-start | bytes 5242880 | tf_op jit(solution)/shard_map/all_to_all | solution.py:537
  23.2 145.9 %all-gather.3.cloned.1.call-start = ((), (), s32[]{:S(2)}) async-start(), calls=%async_computation.14 | async-start | bytes 4325376 | tf_op jit(solution)/shard_map/all_gather | solution.py:763
  24.0 37.4 %collective-permute-start.2 = (bf16[2,72,1024]{2,1,0:T(8,128)(2,1)S(1)}, bf16[2,72,1024]{2,1,0:T(8,128)(2,1)S(1)}, u32[]{:S(2)}, u32[]{:S(2)}) collective-permute-start(bf16[2,72,1024]{2,1,0:T(8,128)(2,1)S(1)} %pad_maximum_fusion.4), channel_id=1, source_target_pairs={{0,1},{1,2},{2,3},{3,0},{4,5},{5,6},{6,7},{7,4},{8,9},{9,10},{10,1... | collective-permute-start | bytes 884744 | tf_op jit(solution)/shard_map/ppermute | solution.py:560
  26.5 41.8 %collective-permute-start.3 = (bf16[2,72,1024]{2,1,0:T(8,128)(2,1)S(1)}, bf16[2,72,1024]{2,1,0:T(8,128)(2,1)S(1)}, u32[]{:S(2)}, u32[]{:S(2)}) collective-permute-start(bf16[2,72,1024]{2,1,0:T(8,128)(2,1)S(1)} %pad_maximum_fusion.4), channel_id=1, source_target_pairs={{0,2},{1,3},{2,0},{3,1},{4,6},{5,7},{6,4},{7,5},{8,10},{9,11},{10,... | collective-permute-start | bytes 884744 | tf_op jit(solution)/shard_map/ppermute | solution.py:560
  29.9 38.5 %collective-permute-start.4 = (bf16[2,72,1024]{2,1,0:T(8,128)(2,1)S(1)}, bf16[2,72,1024]{2,1,0:T(8,128)(2,1)S(1)}, u32[]{:S(2)}, u32[]{:S(2)}) collective-permute-start(bf16[2,72,1024]{2,1,0:T(8,128)(2,1)S(1)} %pad_maximum_fusion.4), channel_id=1, source_target_pairs={{0,3},{1,0},{2,1},{3,2},{4,7},{5,4},{6,5},{7,6},{8,11},{9,8},{10,9... | collective-permute-start | bytes 884744 | tf_op jit(solution)/shard_map/ppermute | solution.py:560
  82.2 36.9 %collective-permute-start.8 = (bf16[128,1024]{1,0:T(8,128)(2,1)}, bf16[128,1024]{1,0:T(8,128)(2,1)}, u32[]{:S(2)}, u32[]{:S(2)}) collective-permute-start(bf16[128,1024]{1,0:T(8,128)(2,1)} %bitcast.21), channel_id=1, source_target_pairs={{0,1},{1,2},{2,3},{3,0},{4,5},{5,6},{6,7},{7,4},{8,9},{9,10},{10,1... | collective-permute-start | bytes 786440 | tf_op jit(solution)/shard_map/ppermute | solution.py:560
  82.5 40.3 %collective-permute-start.9 = (bf16[128,1024]{1,0:T(8,128)(2,1)}, bf16[128,1024]{1,0:T(8,128)(2,1)}, u32[]{:S(2)}, u32[]{:S(2)}) collective-permute-start(bf16[128,1024]{1,0:T(8,128)(2,1)} %bitcast.21), channel_id=1, source_target_pairs={{0,2},{1,3},{2,0},{3,1},{4,6},{5,7},{6,4},{7,5},{8,10},{9,11},{10,... | collective-permute-start | bytes 786440 | tf_op jit(solution)/shard_map/ppermute | solution.py:560
  86.1 58.1 %collective-permute-start.10 = (bf16[128,1024]{1,0:T(8,128)(2,1)}, bf16[128,1024]{1,0:T(8,128)(2,1)}, u32[]{:S(2)}, u32[]{:S(2)}) collective-permute-start(bf16[128,1024]{1,0:T(8,128)(2,1)} %bitcast.21), channel_id=1, source_target_pairs={{0,3},{1,0},{2,1},{3,2},{4,7},{5,4},{6,5},{7,6},{8,11},{9,8},{10,9... | collective-permute-start | bytes 786440 | tf_op jit(solution)/shard_map/ppermute | solution.py:560
  97.6 48.5 %collective-permute-start.6 = (bf16[256,1024]{1,0:T(8,128)(2,1)}, bf16[256,1024]{1,0:T(8,128)(2,1)}, u32[]{:S(2)}, u32[]{:S(2)}) collective-permute-start(bf16[256,1024]{1,0:T(8,128)(2,1)} %get-tuple-element.95), channel_id=1, source_target_pairs={{0,2},{1,3},{2,0},{3,1},{4,6},{5,7},{6,4},{7,5},{8,10},{9,11},{10,... | collective-permute-start | bytes 1572872 | tf_op jit(solution)/shard_map/ppermute | solution.py:552
  122.9 24.3 %collective-permute-start.7 = (bf16[256,1024]{1,0:T(8,128)(2,1)}, bf16[256,1024]{1,0:T(8,128)(2,1)}, u32[]{:S(2)}, u32[]{:S(2)}) collective-permute-start(bf16[256,1024]{1,0:T(8,128)(2,1)} %get-tuple-element.94), channel_id=1, source_target_pairs={{0,3},{1,0},{2,1},{3,2},{4,7},{5,4},{6,5},{7,6},{8,11},{9,8},{10,9... | collective-permute-start | bytes 1572872 | tf_op jit(solution)/shard_map/ppermute | solution.py:552
  135.6 25.4 %all-to-all-start.1 = ((bf16[32,2,64,128]{3,2,1,0:T(8,128)(2,1)}), bf16[32,2,64,128]{3,2,1,0:T(8,128)(2,1)S(1)}, u32[]{:S(2)}, u32[]{:S(2)}) async-start(bf16[32,2,64,128]{3,2,1,0:T(8,128)(2,1)} %bitcast.308), calls=%async_computation.1 | async-start | bytes 2097152 | tf_op jit(solution)/shard_map/all_to_all | solution.py:537
  164.6 31.0 %all-to-all-start.2 = ((bf16[32,2,48,128]{3,2,1,0:T(8,128)(2,1)}), bf16[32,2,48,128]{3,2,1,0:T(8,128)(2,1)}, u32[]{:S(2)}, u32[]{:S(2)}) async-start(bf16[32,2,48,128]{3,2,1,0:T(8,128)(2,1)} %copy-done.47), calls=%async_computation.2 | async-start | bytes 1572864 | tf_op jit(solution)/shard_map/all_to_all | solution.py:537
  212.2 20.5 %all-to-all-start.3 = ((bf16[4,144,1024]{2,1,0:T(8,128)(2,1)}), bf16[4,144,1024]{2,1,0:T(8,128)(2,1)}, u32[]{:S(2)}, u32[]{:S(2)}) async-start(bf16[4,144,1024]{2,1,0:T(8,128)(2,1)} %copy-done.21), calls=%async_computation.3 | async-start | bytes 2359296 | tf_op jit(solution)/shard_map/all_to_all | solution.py:537
  264.0 16.8 %all-to-all-start.5 = ((bf16[4,128,1024]{2,1,0:T(8,128)(2,1)}), bf16[4,128,1024]{2,1,0:T(8,128)(2,1)}, u32[]{:S(2)}, u32[]{:S(2)}) async-start(bf16[4,128,1024]{2,1,0:T(8,128)(2,1)} %bitcast.338), calls=%async_computation.5 | async-start | bytes 2097152 | tf_op jit(solution)/shard_map/all_to_all | solution.py:537
  285.1 16.8 %all-to-all-start.6 = ((bf16[4,144,1024]{2,1,0:T(8,128)(2,1)}), bf16[4,144,1024]{2,1,0:T(8,128)(2,1)}, u32[]{:S(2)}, u32[]{:S(2)}) async-start(bf16[4,144,1024]{2,1,0:T(8,128)(2,1)} %broadcast_in_dim.170), calls=%async_computation.6 | async-start | bytes 2359296 | tf_op jit(solution)/shard_map/all_to_all | solution.py:537
  312.9 36.3 %all-to-all-start.7 = ((bf16[32,2,48,128]{3,2,1,0:T(8,128)(2,1)}), bf16[32,2,48,128]{3,2,1,0:T(8,128)(2,1)S(1)}, u32[]{:S(2)}, u32[]{:S(2)}) async-start(bf16[32,2,48,128]{3,2,1,0:T(8,128)(2,1)} %bitcast.61), calls=%async_computation.7 | async-start | bytes 1572864 | tf_op jit(solution)/shard_map/all_to_all | solution.py:537
  353.8 17.0 %collective-permute-start.17 = (bf16[16,4,2,64,128]{4,3,2,1,0:T(8,128)(2,1)}, bf16[16,4,2,64,128]{4,3,2,1,0:T(8,128)(2,1)}, u32[]{:S(2)}, u32[]{:S(2)}) collective-permute-start(bf16[16,4,2,64,128]{4,3,2,1,0:T(8,128)(2,1)} %hold.1), channel_id=1, source_target_pairs={{0,4},{4,0},{8,12},{12,8},{16,20},{20,16},{24,28},{28,24},{32,36},... | collective-permute-start | bytes 6291464 | tf_op jit(solution)/shard_map/ppermute | solution.py:962
  355.7 21.6 %all-to-all-start.8 = ((bf16[32,2,48,128]{3,2,1,0:T(8,128)(2,1)}), bf16[32,2,48,128]{3,2,1,0:T(8,128)(2,1)S(1)}, u32[]{:S(2)}, u32[]{:S(2)}) async-start(bf16[32,2,48,128]{3,2,1,0:T(8,128)(2,1)} %chain.3.dep_ref), calls=%async_computation.8 | async-start | bytes 1572864 | tf_op jit(solution)/shard_map/all_to_all | solution.py:537
  370.6 32.4 %collective-permute-start.19 = (bf16[512,1024]{1,0:T(8,128)(2,1)}, bf16[512,1024]{1,0:T(8,128)(2,1)}, u32[]{:S(2)}, u32[]{:S(2)}) collective-permute-start(bf16[512,1024]{1,0:T(8,128)(2,1)} %get-tuple-element.135), channel_id=1, source_target_pairs={{0,4},{4,0},{8,12},{12,8},{16,20},{20,16},{24,28},{28,24},{32,36},... | collective-permute-start | bytes 3145736 | tf_op jit(solution)/shard_map/ppermute | solution.py:911
  378.2 53.8 %all-to-all-start.9 = ((bf16[16,4,2,64,128]{4,3,2,1,0:T(8,128)(2,1)}), bf16[16,4,2,64,128]{4,3,2,1,0:T(8,128)(2,1)S(1)}, u32[]{:S(2)}, u32[]{:S(2)}) async-start(bf16[16,4,2,64,128]{4,3,2,1,0:T(8,128)(2,1)} %add_convert_fusion), calls=%async_computation.9 | async-start | bytes 4194304 | tf_op jit(solution)/shard_map/all_to_all | solution.py:1012
  433.3 35.6 %all-to-all-start.10 = ((bf16[16,4,8,2048]{3,2,1,0:T(8,128)(2,1)}), bf16[16,4,8,2048]{3,2,1,0:T(8,128)(2,1)S(1)}, u32[]{:S(2)}, u32[]{:S(2)}) async-start(bf16[16,4,8,2048]{3,2,1,0:T(8,128)(2,1)} %copy-done.4), calls=%async_computation.10 | async-start | bytes 4194304 | tf_op jit(solution)/shard_map/all_to_all | solution.py:1012
  450.3 18.7 %collective-permute-start.25 = (bf16[4,128,1280]{2,1,0:T(8,128)(2,1)}, bf16[4,128,1280]{2,1,0:T(8,128)(2,1)}, u32[]{:S(2)}, u32[]{:S(2)}) collective-permute-start(bf16[4,128,1280]{2,1,0:T(8,128)(2,1)} %get-tuple-element.88), channel_id=1, source_target_pairs={{0,4},{4,0},{8,12},{12,8},{16,20},{20,16},{24,28},{28,24},{32,36},... | collective-permute-start | bytes 3932168 | tf_op jit(solution)/shard_map/ppermute | solution.py:905
  474.4 25.8 %all-to-all-start.11 = ((bf16[16,4,8,1408]{3,2,1,0:T(8,128)(2,1)}), bf16[16,4,8,1408]{3,2,1,0:T(8,128)(2,1)}, u32[]{:S(2)}, u32[]{:S(2)}) async-start(bf16[16,4,8,1408]{3,2,1,0:T(8,128)(2,1)} %copy-done.19), calls=%async_computation.11 | async-start | bytes 2883584 | tf_op jit(solution)/shard_map/all_to_all | solution.py:1012
  555.3 16.4 %collective-permute-start.27 = (bf16[16,8,12416]{2,1,0:T(8,128)(2,1)S(1)}, bf16[16,8,12416]{2,1,0:T(8,128)(2,1)}, u32[]{:S(2)}, u32[]{:S(2)}) collective-permute-start(bf16[16,8,12416]{2,1,0:T(8,128)(2,1)S(1)} %all_to_all.72.mine_ref), channel_id=1, source_target_pairs={{0,4},{4,0},{8,12},{12,8},{16,20},{20,16},{24,28},{28,24},{32,36},... | collective-permute-start | bytes 9535496 | tf_op jit(solution)/shard_map/ppermute | solution.py:1086
  (151 other events, 1296.4 us)
Sparse Core Ops, SparseCore 0:
  80.4 45.3 all-gather.2

commit v4 on v3

--- a/solution.py
+++ b/solution.py
@@ -108,26 +108,72 @@
     return jnp.where(half == 0, i, 2 * nctx - 1 - i) * BLK
 
 
-def proj_kernel(x_ref, w_ref, wdt_ref, gain_ref, *refs):
-    z_ref, ext_ref, dtr_ref, qkv_ref, act_ref = refs[-5:]
+def turned(v, cosine, sine):
+    a, b = v[:, : HDIM // 2], v[:, HDIM // 2 :]
+    return jnp.concatenate([a * cosine - b * sine, b * cosine + a * sine], axis=1)
+
+
+def proj_kernel(core_ref, x_ref, mine_ref, other_ref, wdt_ref, gain_ref, cos_ref, sin_ref, *refs):
+    z_ref, ext_ref, dtr_ref, q_ref, kv_ref, act_ref, w_ref = refs[-7:]
     x = x_ref[...].astype(F32)
     r = lax.rsqrt(jnp.mean(x * x, axis=1, keepdims=True) + EPS)
     act_ref[...] = (x * r * gain_ref[...]).astype(BF16)
+
+    def place(even_ref, odd_ref):
+        for src in range(4):
+            w_ref[256 * src : 256 * src + 128] = even_ref[src]
+            w_ref[256 * src + 128 : 256 * src + 256] = odd_ref[src]
+
+    @pl.when(core_ref[0] == 0)
+    def _():
+        place(mine_ref, other_ref)
+
+    @pl.when(core_ref[0] == 1)
+    def _():
+        place(other_ref, mine_ref)
+
     a = act_ref[...]
 
     def columns(lo, width):
         p = lax.dot_general(a, w_ref[:, lo : lo + width], (NN, ((), ())), preferred_element_type=F32)
         return p.reshape(8, EXT, width)
 
+    p = columns(1024, 256)
+    for j in range(8):
+        seq, half = j // 2, j % 2
+        own = p[j, 8:]
+        cosine, sine = cos_ref[half], sin_ref[half]
+        for e in range(2):
+            q = turned(own[:, HDIM * e : HDIM * e + HDIM], cosine, sine).astype(BF16)
+            q = (q.astype(F32) * HDIM**-0.5).astype(BF16)
+            q_ref[seq, half, BLK * e : BLK * e + BLK] = q
+        k = turned(own[:, 128:192], cosine, sine)
+        kv_ref[seq, half] = jnp.concatenate([k, own[:, 192:]], axis=1).astype(BF16)
     z_ref[:, :, :256] = columns(0, 256)[:, 8:]
     both = columns(256, 256)
     z_ref[:, :, 256:] = both[:, 8:, :128]
     ext_ref[:, :, :128] = both[:, :, 128:]
     ext_ref[:, :, 128:384] = columns(512, 256)
     ext_ref[:, :, 384:] = columns(768, 256)
-    qkv_ref[...] = columns(1024, 256)[:, 8:]
     p = lax.dot_general(a, wdt_ref[...], (NN, ((), ())), preferred_element_type=F32)
     dtr_ref[...] = p.reshape(8, EXT, 128)
+
+
+def dproj_kernel(n, got_ref, z_ref, ext_ref, q_ref, cos_ref, sin_ref, *refs):
+    out_ref = refs[-1]
+
+    def step(j, acc):
+        return acc + got_ref[j].astype(F32)
+
+    kv = lax.fori_loop(1, n, step, got_ref[0].astype(F32))
+    out_ref[:, :8] = jnp.zeros((8, 8, LPROJ), BF16)
+    out_ref[:, :, LX : LX + LCONV] = ext_ref[...]
+    for j in range(8):
+        own = kv[j // 2, j % 2]
+        k = turned(own[:, :HDIM], cos_ref[j % 2], -sin_ref[j % 2])
+        out_ref[j, 8:, :LX] = z_ref[j].astype(BF16)
+        out_ref[j, 8:, 1024:1152] = q_ref[j // 2, j % 2]
+        out_ref[j, 8:, 1152:] = jnp.concatenate([k, own[:, HDIM:]], axis=1).astype(BF16)
 
 
 def mid_kernel(u_ref, w_ref, ss_ref, dep_ref, out_ref):
@@ -181,7 +227,8 @@
     to_chunks(state, s_ref, nk, pr, [high, dec - high])
 
 
-def ssd_out_kernel(nk, pr, y_ref, swx_ref, c_ref, s_ref, z_ref, gain_ref, dep_ref, out_ref, u_ref, ss_ref):
+def ssd_out_kernel(nk, pr, y_ref, swx_ref, c_ref, s_ref, z_ref, gain_ref, *refs):
+    out_ref, u_ref, ss_ref = refs[-3:]
     s_in = from_chunks(s_ref, nk, pr)
     y = y_ref[0] + swx_ref[0] * dotb(c_ref[0], s_in, NT)
     z = z_ref[0]
@@ -191,7 +238,8 @@
     ss_ref[0] = jnp.broadcast_to(jnp.sum(u * u, axis=1, keepdims=True), (BLK, 128))
 
 
-def split_in_kernel(w_ref, out_ref):
+def split_in_kernel(core_ref, full_ref, out_ref):
+    w_ref = full_ref.at[pl.ds(pl.multiple_of(core_ref[0] * 128, 128), 128)]
     for zz in range(4):
         kv = HDIM * (zz // 2)
         out_ref[zz, :, :LX] = w_ref[:, LX * zz : LX * zz + LX]
@@ -209,15 +257,6 @@
         out_ref[zz, :, 512:] = w_ref[:, FF + 512 * zz : FF + 512 * zz + 512]
 
 
-def total_kernel(n, got_ref, *refs):
-    out_ref = refs[-1]
-
-    def step(j, acc):
-        return acc + got_ref[j].astype(F32)
-
-    out_ref[...] = lax.fori_loop(1, n, step, got_ref[0].astype(F32))
-
-
 def pack_kernel(nj, rj, kin_ref, gin_ref, kex_ref, gex_ref, dep_ref, out_ref):
     for a in range(4):
         part = (kin_ref[a].astype(F32) + gin_ref[a].astype(F32)).astype(BF16)
@@ -232,7 +271,7 @@
     out_ref[:, :, :, 1024:] = o_ref[...].reshape(nj, 4, rj, 1024)
 
 
-def totals_kernel(n, got_ref, early_ref, dep_ref, out_ref, o_ref):
+def totals_kernel(n, got_ref, early_ref, dep_a, dep_b, out_ref, o_ref):
     def step(j, acc):
         return acc[0] + got_ref[j].astype(F32), acc[1] + early_ref[j].astype(F32)
 
@@ -438,7 +477,7 @@
     return (kpos <= qpos) & (kpos >= st)
 
 
-def attn_fwd_kernel(nctx, gs, idx_ref, q_ref, kv_ref, st_ref, dep_a, dep_b, o_ref, lse_ref, s_ref, m_ref, l_ref, acc_ref):
+def attn_fwd_kernel(nctx, gs, idx_ref, q_ref, kv_ref, st_ref, o_ref, lse_ref, s_ref, m_ref, l_ref, acc_ref):
     i = idx_ref[0]
     gi = i // gs
     m_ref[...] = jnp.full(m_ref.shape, NEG, F32)
@@ -463,9 +502,9 @@
 
 
 def attn_bwd_kernel(
-    nctx, gs, idx_ref, q_ref, kv_ref, st_ref, o_ref, lse_ref, do_ref, *refs
+    nctx, gs, idx_ref, q_ref, kv_ref, st_ref, o_ref, lse_ref, do_ref, cos_ref, sin_ref, *refs
 ):
-    dq_ref, keep_ref, give_ref, del_ref, acc_ref = refs[-5:]
+    out_ref, keep_ref, give_ref, del_ref, acc_ref, dq_ref = refs[-6:]
     i = idx_ref[0]
     gi = i // gs
     acc_ref[...] = jnp.zeros(acc_ref.shape, F32)
@@ -484,8 +523,13 @@
         ds = (prob * (dp - del_ref[rowset, :, :1])).astype(BF16)
         dkv = jnp.concatenate([dotb(ds, q, TN), dotb(prob, do, TN)], axis=1)
         acc_ref[half, g] = acc_ref[half, g] + dkv
-        dq_ref[0, rowset] = dq_ref[0, rowset] + dotb(ds, kv[:, :HDIM], NN)
-    dq_ref[...] = dq_ref[...] * (HDIM**-0.5)
+        dq_ref[rowset] = dq_ref[rowset] + dotb(ds, kv[:, :HDIM], NN)
+    for half in range(2):
+        parts = []
+        for e in range(2):
+            part = dq_ref[half, BLK * e : BLK * e + BLK] * HDIM**-0.5
+            parts.append(turned(part, cos_ref[half], -sin_ref[half]))
+        out_ref[0, half] = jnp.concatenate(parts, axis=1).astype(BF16)
 
     def write(even_ref, odd_ref):
         for src in range(4 * gs):
@@ -522,7 +566,9 @@
 ANY = pl.BlockSpec(memory_space=pl.ANY)
 VMEM = pl.BlockSpec(memory_space=pltpu.VMEM)
 SMEM = pl.BlockSpec(memory_space=pltpu.SMEM)
-PARAMS = pltpu.CompilerParams(vmem_limit_bytes=48 * 1024 * 1024)
+PARAMS = pltpu.CompilerParams(vmem_limit_bytes=16 * 1024 * 1024)
+WIDER = pltpu.CompilerParams(vmem_limit_bytes=28 * 1024 * 1024)
+WIDEST = pltpu.CompilerParams(vmem_limit_bytes=48 * 1024 * 1024)
 
 
 def cost(flops, moved, trans=0):
@@ -590,11 +636,6 @@
 def rms_back(v, r, dn):
     n = v * r
     return r * (dn - n * jnp.mean(dn * n, axis=-1, keepdims=True))
-
-
-def turn(values, cosine, sine):
-    a, b = values[..., : HDIM // 2], values[..., HDIM // 2 :]
-    return jnp.concatenate([a * cosine - b * sine, b * cosine + a * sine], axis=-1)
 
 
 def matmul(a, b, dims=NN):
@@ -632,15 +673,18 @@
     up = [(a, a + 1) for a in range(nctx - 1)]
     down = [(b, a) for a, b in up]
 
+    core = i % 2
+    core_idx = core.astype(jnp.int32).reshape(1)
+    pair = [(a, a ^ 1) for a in range(nctx)]
     send_in = pl.pallas_call(
         split_in_kernel,
-        in_specs=[VMEM],
+        in_specs=[SMEM, VMEM],
         out_specs=VMEM,
-        out_shape=sds((4, 256, LPROJ), BF16),
+        out_shape=sds((4, 128, LPROJ), BF16),
         compiler_params=PARAMS,
         cost_estimate=cost(0, 5 * 10**6),
         name="split_in",
-    )(w_in)
+    )(core_idx, w_in)
     send_gu = pl.pallas_call(
         split_gate_up_kernel,
         in_specs=[VMEM],
@@ -669,7 +713,8 @@
     )
     flat = jnp.pad(flat, (0, 10 * D - flat.shape[0])).reshape(2, 5, D)
     wide = ring_spread(jnp.concatenate([flat, halo, tok], axis=1), z)
-    own_in = exchange(send_in, "fsdp").reshape(D, LPROJ)
+    mine_in = exchange(send_in, "fsdp")
+    other_in = lax.ppermute(mine_in, "ctx", pair)
     own_gu = ring_exchange(send_gu, z).reshape(D, 1024)
     grad_own = cotangent[0].reshape(128, D)
     grad_all = ring_spread(grad_own, z).reshape(512, D)
@@ -698,37 +743,33 @@
 
     rows = 8 * EXT
     st_wide = jnp.broadcast_to(starts[:, :, None], (8, BLK, 128))
-    gate_z, conv_ext, raw_dt, qkv, act_one = pl.pallas_call(
+    blocks = jnp.stack([i, 2 * nctx - 1 - i])
+    positions = blocks[:, None] * BLK + jnp.arange(BLK, dtype=jnp.int32)[None, :]
+    freq = jnp.exp(
+        jnp.arange(HDIM // 2, dtype=F32) * (-2.0 * math.log(ROPE_BASE) / HDIM)
+    )
+    angle = positions.astype(F32)[:, :, None] * freq
+    cosine, sine = jnp.cos(angle), jnp.sin(angle)
+    gate_z, conv_ext, raw_dt, query, kv_own, act_one, own_in = pl.pallas_call(
         proj_kernel,
-        in_specs=[VMEM] * 4 + [ANY] * 2,
-        out_specs=[VMEM] * 5,
+        in_specs=[SMEM] + [VMEM] * 7 + [ANY] * 2,
+        out_specs=[VMEM] * 7,
         out_shape=[
             sds((8, BLK, LX), F32),
             sds((8, EXT, LCONV), F32),
             sds((8, EXT, 128), F32),
-            sds((8, BLK, 256), F32),
+            sds((4, 2, 2 * BLK, HDIM), BF16),
+            sds((4, 2, BLK, 128), BF16),
             sds((rows, D), BF16),
-        ],
-        compiler_params=PARAMS,
+            sds((D, LPROJ), BF16),
+        ],
+        compiler_params=WIDER,
         cost_estimate=cost(2 * 10**9, 8 * 10**6),
         name="proj",
-    )(wide.reshape(rows, D), own_in, own_dt, mixer_scale[None], pv, st_wide)
-
-    blocks = jnp.stack([i, 2 * nctx - 1 - i])
-    positions = blocks[:, None] * BLK + jnp.arange(BLK, dtype=jnp.int32)[None, :]
-    freq = jnp.exp(
-        jnp.arange(HDIM // 2, dtype=F32) * (-2.0 * math.log(ROPE_BASE) / HDIM)
-    )
-    angle = positions.astype(F32)[:, :, None] * freq
-    cosine, sine = jnp.cos(angle), jnp.sin(angle)
-    tables = (cosine[None, :, :, None, :], sine[None, :, :, None, :])
-    query = qkv[:, :, :128].reshape(4, 2, BLK, 2, HDIM)
-    query = turn(query, *tables).astype(BF16) * jnp.asarray(HDIM**-0.5, BF16)
-    query = query.transpose(0, 1, 3, 2, 4).reshape(4, 2, 2 * BLK, HDIM)
-    key = qkv[:, :, 128:192].reshape(4, 2, BLK, 1, HDIM)
-    key = turn(key, *tables).astype(BF16).reshape(4, 2, BLK, HDIM)
-    value = qkv[:, :, 192:].astype(BF16).reshape(4, 2, BLK, HDIM)
-    kv_own = jnp.concatenate([key, value], axis=-1)
+    )(
+        core_idx, wide.reshape(rows, D), mine_in, other_in, own_dt, mixer_scale[None],
+        cosine, sine, pv, st_wide,
+    )
 
     srows = LOCAL_HEADS * pr
     ssd_in = (idx, conv_ext, raw_dt, st_wide, pv)
@@ -776,7 +817,7 @@
             name="chain",
         )(terms, got, *after)
 
-    entry = exchange(chain(False, got, own_gu, grad_all, query, st_rows), "ctx").reshape(4, nk, 2, srows, 128)
+    entry = exchange(chain(False, got, st_rows), "ctx").reshape(4, nk, 2, srows, 128)
 
     row_spec = pl.BlockSpec((1, 2, 2 * BLK, HDIM), lambda s: (s, 0, 0, 0))
     wide_spec = pl.BlockSpec((1, 2, 2 * BLK, 128), lambda s: (s, 0, 0, 0))
@@ -784,7 +825,7 @@
     attn_o, lse = pl.pallas_call(
         functools.partial(attn_fwd_kernel, nctx, gs),
         grid=(4,),
-        in_specs=[SMEM, row_spec, kv_spec, wide_spec, ANY, ANY],
+        in_specs=[SMEM, row_spec, kv_spec, wide_spec],
         out_specs=[row_spec, wide_spec],
         out_shape=[sds((4, 2, 2 * BLK, HDIM), F32), sds((4, 2, 2 * BLK, 128), F32)],
         scratch_shapes=[
@@ -796,7 +837,7 @@
         compiler_params=PARAMS,
         cost_estimate=cost(4 * 10**9, 8 * 10**6, 2 * 10**6),
         name="attn_fwd",
-    )(idx, query, kv_all, st_rows, own_gu, grad_all)
+    )(idx, query, kv_all, st_rows)
     act_attn = (
         attn_o.reshape(4, 2, 2, BLK, HDIM).transpose(0, 1, 3, 2, 4).reshape(512, 128).astype(BF16)
     )
@@ -811,8 +852,8 @@
             chunk_spec(nk, srows),
             per_pair((BLK, LX)),
             whole((1, LX)),
-            ANY,
-        ],
+        ]
+        + [ANY] * 3,
         out_specs=[per_pair((BLK, LX)), per_pair((BLK, LX)), per_pair((BLK, 128))],
         out_shape=[
             sds((8, BLK, LX), F32),
@@ -822,7 +863,7 @@
         compiler_params=PARAMS,
         cost_estimate=cost(10**9, 6 * 10**6),
         name="ssd_out",
-    )(y_local, swx, c_mat, entry, gate_z, inner_scale[None], attn_o)
+    )(y_local, swx, c_mat, entry, gate_z, inner_scale[None], attn_o, own_gu, grad_all)
 
     def gather_sum(part_rows):
         got_rows = exchange(part_rows.astype(BF16).reshape((4, -1) + part_rows.shape[1:]), "fsdp")
@@ -895,9 +936,6 @@
     )
     grad_mamba_out = matmul(act_mamba, grad_mix, TN).astype(BF16)
     grad_attn_out = matmul(act_attn, grad_mix, TN).astype(BF16)
-    core = i % 2
-    pair = [(a, a ^ 1) for a in range(nctx)]
-
     def halves(v):
         v = v.reshape(4, 2, 128, v.shape[-1])
         keep = lax.dynamic_index_in_dim(v, core, 1, keepdims=False)
@@ -930,22 +968,29 @@
     grad_query, keep_kv, give_kv = pl.pallas_call(
         functools.partial(attn_bwd_kernel, nctx, gs),
         grid=(4,),
-        in_specs=[SMEM, row_spec, kv_spec, wide_spec, row_spec, wide_spec, row_spec] + [ANY] * 5,
-        out_specs=[row_spec, half_kv_spec, half_kv_spec],
+        in_specs=[SMEM, row_spec, kv_spec, wide_spec, row_spec, wide_spec, row_spec]
+        + [whole((2, BLK, HDIM // 2))] * 2
+        + [ANY] * 5,
+        out_specs=[
+            pl.BlockSpec((1, 2, BLK, 128), lambda s: (s, 0, 0, 0)),
+            half_kv_spec,
+            half_kv_spec,
+        ],
         out_shape=[
-            sds((4, 2, 2 * BLK, HDIM), F32),
+            sds((4, 2, BLK, 128), BF16),
             sds((nctx // 2, 4, 2, BLK, 128), BF16),
             sds((nctx // 2, 4, 2, BLK, 128), BF16),
         ],
         scratch_shapes=[
             pltpu.VMEM((2, 2 * BLK, 128), F32),
             pltpu.VMEM((2, 4, gs * BLK, 128), F32),
+            pltpu.VMEM((2, 2 * BLK, HDIM), F32),
         ],
         compiler_params=PARAMS,
         cost_estimate=cost(8 * 10**9, 16 * 10**6, 2 * 10**6),
         name="attn_bwd",
     )(
-        idx, query, kv_all, st_rows, attn_o, lse, grad_attn,
+        idx, query, kv_all, st_rows, attn_o, lse, grad_attn, cosine, sine,
         leak, grad_gate_up, grad_down, grad_mamba_out, grad_attn_out,
     )
     chained = chain(True, got_leak, give_kv)
@@ -1011,33 +1056,19 @@
     def core_exchange(parts):
         return lax.all_to_all(parts, "ctx", 0, 0, axis_index_groups=groups, tiled=True)
 
-    grad_kv = pl.pallas_call(
-        functools.partial(total_kernel, nj),
-        in_specs=[VMEM] + [ANY] * 3,
+    grad_proj = pl.pallas_call(
+        functools.partial(dproj_kernel, nj),
+        in_specs=[VMEM] * 6 + [ANY] * 2,
         out_specs=VMEM,
-        out_shape=sds((4, 2, BLK, 128), F32),
+        out_shape=sds((8, EXT, LPROJ), BF16),
         compiler_params=PARAMS,
         cost_estimate=cost(2 * 10**6, 4 * 10**6),
-        name="total_kv",
-    )(core_exchange(pair_kv), mixed, early, extras)
+        name="dproj",
+    )(
+        core_exchange(pair_kv), grad_z.reshape(8, BLK, LX), grad_ext, grad_query, cosine, sine,
+        early, extras,
+    ).reshape(rows, LPROJ)
     got_early = core_exchange(early)
-    back = (tables[0], -tables[1])
-    grad_key = turn(grad_kv[..., :HDIM].reshape(4, 2, BLK, 1, HDIM), *back).reshape(8, BLK, HDIM)
-    grad_value = grad_kv[..., HDIM:].reshape(8, BLK, HDIM)
-    grad_query = grad_query.reshape(4, 2, 2, BLK, HDIM).transpose(0, 1, 3, 2, 4)
-    grad_query = turn(grad_query, *back).reshape(8, BLK, 128)
-
-    def lead(v):
-        return jnp.pad(v.astype(BF16), ((0, 0), (8, 0), (0, 0)))
-
-    grad_proj = jnp.concatenate(
-        [
-            lead(grad_z.reshape(8, BLK, LX)),
-            grad_ext,
-            lead(jnp.concatenate([grad_query, grad_key, grad_value], axis=-1)),
-        ],
-        axis=-1,
-    ).reshape(rows, LPROJ)
     grad_act = matmul(grad_proj, own_in, NT) + matmul(grad_dt, own_dt, NT)
 
     got_act = ring_sum(grad_act, z).reshape(2, EXT, D)
@@ -1065,13 +1096,13 @@
     )(kept_in, taken_in, kept_ex, taken_ex, got_early)
     summed, summed_o = pl.pallas_call(
         functools.partial(totals_kernel, nj),
-        in_specs=[VMEM, VMEM, ANY],
+        in_specs=[VMEM, VMEM, ANY, ANY],
         out_specs=[VMEM, VMEM],
         out_shape=[sds((4, rj, 2432), F32), sds((4, rj, 1024), F32)],
         compiler_params=PARAMS,
         cost_estimate=cost(2 * 10**6, 4 * 10**6),
         name="totals",
-    )(core_exchange(sent), got_early, got_act)
+    )(core_exchange(sent), got_early, got_act, mixed)
     owned = exchange(summed, "fsdp")
     final = pl.pallas_call(
         assemble_kernel,
@@ -1107,10 +1138,10 @@
             sds((384, 1024), F32),
             sds((128, 1024), F32),
         ],
-        compiler_params=PARAMS,
+        compiler_params=WIDEST,
         cost_estimate=cost(0, 10**7),
         name="unpack",
-    )(core.astype(jnp.int32).reshape(1), mine_all, other_all, w_in)
+    )(core_idx, mine_all, other_all, w_in)
     extra = extra[:, :88].reshape(256, 4, 22)
     total_dt = extra[:, :, :6].reshape(256, 24)
     mixer_dot = mixer_dot[:, 0] + jnp.sum(total_dt * w_dt.astype(F32), axis=1)

time: 605 us -> 550 us (0.909)
  waiting for transfers between devices: 157 us -> 100 us
  other arithmetic: 42.5 us -> 30.5 us
  starting transfers between devices: 101 us -> 110 us
    ppermute x6, waiting for transfers between devices: 59 us -> 27.9 us  [ring_spread(): got = lax.ppermute(part, 'fsdp', perm)]
    all_to_all x3, waiting for transfers between devices: 15.1 us -> 1.35 us  [core_exchange(): lax.all_to_all(parts, 'ctx', 0, 0, axis_index_groups=groups, tiled=True)]
    ppermute x3, waiting for transfers between devices: 10.4 us -> 0.01 us  [ring_exchange(): got = lax.ppermute(sent, 'fsdp', perm)]
    ppermute x9, waiting for transfers between devices: 26.7 us -> 17.6 us  [ring_sum(): total = total + lax.ppermute(sent, 'fsdp', perm).astype(F32)]
    ppermute x3, starting transfers between devices: 0.08 us -> 6.29 us  [ring_exchange(): got = lax.ppermute(sent, 'fsdp', perm)]
    unnamed x274 -> x294, local copies, waits for them, and re-layouts: 50.1 us -> 56 us
  transfers between devices with their start and end apart: 40 -> 41, of which waited for: 19 -> 16; matrix products, arithmetic and copies ran while one was open for 14% -> 12% of each run, Pallas kernels for 11% -> 12%
where the time goes in v4:
time: 550 us; the launch traced here: 539 us
  starting transfers between devices  110 us (20%)
  waiting for transfers between devices  100 us (18%)
  local copies, waits for them, and re-layouts  95.5 us (17%)
  Pallas kernels  82.6 us (15%)
  blocking collectives  75.2 us (14%)
  other arithmetic  30.5 us (6%)
  matrix products  29 us (5%)
  between operations  16.5 us (3%)
    unnamed x294, local copies, waits for them, and re-layouts  56 us
    all_to_all x8, starting transfers between devices, exchange(): return lax.all_to_all(parts, axis, 0, 0, tiled=True)  50.8 us
    all_to_all x1, blocking collectives, core_exchange(): lax.all_to_all(parts, 'ctx', 0, 0, axis_index_groups=groups, tiled=True)  48.5 us
    all_to_all x8, waiting for transfers between devices, exchange(): return lax.all_to_all(parts, axis, 0, 0, tiled=True)  43.9 us
    dot_general x14, matrix products, matmul(): return lax.dot_general(a, b, (dims, ((), ())), preferred_element_type=F32)  29 us
    ppermute x6, waiting for transfers between devices, ring_spread(): got = lax.ppermute(part, 'fsdp', perm)  27.9 us
    all_to_all x2, blocking collectives, exchange(): return lax.all_to_all(parts, axis, 0, 0, tiled=True)  26.7 us
    all_to_all x3, starting transfers between devices, core_exchange(): lax.all_to_all(parts, 'ctx', 0, 0, axis_index_groups=groups, tiled=True)  17.7 us
  transfers between devices with their start and end apart: 41, of which 16 were waited for; matrix products, arithmetic and copies ran while one was open for 12% of the time, Pallas kernels for 12%

profile of v4, /device:TPU:1, one launch (start us, length us, event | category | flops | bytes accessed | tf_op | source)
XLA Modules:
  0.0 539.4 jit_solution(9728725204723777338)
XLA Ops:
  17.4 5.2 all-to-all-start
  29.8 17.3 %collective-permute-done.2 = bf16[2,72,1024]{2,1,0:T(8,128)(2,1)} collective-permute-done((bf16[2,72,1024]{2,1,0:T(8,128)(2,1)S(1)}, bf16[2,72,1024]{2,1,0:T(8,128)(2,1)}, u32[]{:S(2)}, u32[]{:S(2)}) %collective-permute-start.2) | collective-permute-done | bytes 294944 | tf_op jit(solution)/shard_map/ppermute | solution.py:606
  79.7 8.3 %ssd_fwd.1 = (f32[8,64,384]{2,1,0:T(8,128)S(1)}, f32[8,64,384]{2,1,0:T(8,128)S(1)}, bf16[8,64,128]{2,1,0:T(8,128)(2,1)S(1)}, bf16[4,8,2,64,128]{4,3,2,1,0:T(8,128)(2,1)S(1)}) custom-call(s32[1]{0:T(128)} %bitcast.1.idx_ref, f32[8,72,640]{2,1,0:T(8,128)S(1)} %get-tuple-element.47.ext_ref, f32[8,72,128]{2,1,0:T(8,128)S(1)} %get-tuple-element.48.dtr_ref, ...), custom_call_target="tpu_custom_call" | custom-call | flops 2000000 | bytes 6000 | tf_op jit(solution)/shard_map/ssd_fwd/pallas_call | solution.py:783
  90.8 7.9 %all-to-all-start.1 = ((bf16[32,2,64,128]{3,2,1,0:T(8,128)(2,1)}), bf16[32,2,64,128]{3,2,1,0:T(8,128)(2,1)S(1)}, u32[]{:S(2)}, u32[]{:S(2)}) async-start(bf16[32,2,64,128]{3,2,1,0:T(8,128)(2,1)} %bitcast.292), calls=%async_computation.1 | async-start | bytes 2097152 | tf_op jit(solution)/shard_map/all_to_all | solution.py:583
  102.6 5.6 %collective-permute-done.10 = bf16[128,1024]{1,0:T(8,128)(2,1)S(1)} collective-permute-done((bf16[128,1024]{1,0:T(8,128)(2,1)}, bf16[128,1024]{1,0:T(8,128)(2,1)S(1)}, u32[]{:S(2)}, u32[]{:S(2)}) %collective-permute-start.10) | collective-permute-done | bytes 262176 | tf_op jit(solution)/shard_map/ppermute | solution.py:606
  122.1 6.2 %all-to-all-start.2 = ((bf16[32,2,48,128]{3,2,1,0:T(8,128)(2,1)}), bf16[32,2,48,128]{3,2,1,0:T(8,128)(2,1)S(1)}, u32[]{:S(2)}, u32[]{:S(2)}) async-start(bf16[32,2,48,128]{3,2,1,0:T(8,128)(2,1)} %copy-done.44), calls=%async_computation.2 | async-start | bytes 1572864 | tf_op jit(solution)/shard_map/all_to_all | solution.py:583
  130.6 12.5 %attn_fwd.1 = (f32[4,2,128,64]{3,2,1,0:T(8,128)S(1)}, f32[4,2,128,128]{3,2,1,0:T(8,128)S(1)}) custom-call(s32[1]{0:T(128)} %bitcast.1.idx_ref, bf16[4,2,128,64]{3,2,1,0:T(8,128)(2,1)S(1)} %copy-done.61, bf16[32,4,2,64,128]{4,3,2,1,0:T(8,128)(2,1)S(1)} %bitcast.265, s32[4,2,128,128]{3,2,1,0:T(8,128)S(1)} %broadcast_in_dim.157.refs_0_.st_ref), custom_call_target="tpu_custom_call" | custom-call | flops 4000000 | bytes 8000 | tf_op jit(solution)/shard_map/attn_fwd/pallas_call | solution.py:825
  171.0 15.6 %all-to-all-done.3 = bf16[4,144,1024]{2,1,0:T(8,128)(2,1)} async-done(((bf16[4,144,1024]{2,1,0:T(8,128)(2,1)}), bf16[4,144,1024]{2,1,0:T(8,128)(2,1)}, u32[]{:S(2)}, u32[]{:S(2)}) %all-to-all-start.3) | async-done | bytes 1179680 | tf_op jit(solution)/shard_map/all_to_all | solution.py:583
  190.5 17.4 %all_to_all.70 = bf16[4,144,1024]{2,1,0:T(8,128)(2,1)S(1)} all-to-all(bf16[4,144,1024]{2,1,0:T(8,128)(2,1)S(1)} %broadcast_in_dim.167), channel_id=1, replica_groups=mesh['ctx'=32,'fsdp'=4] {'fsdp'}, dimensions={0} | all-to-all | bytes 2359296 | tf_op jit(solution)/shard_map/all_to_all | solution.py:583
  223.7 12.1 %all-to-all-done.5 = bf16[4,128,1024]{2,1,0:T(8,128)(2,1)} async-done(((bf16[4,128,1024]{2,1,0:T(8,128)(2,1)}), bf16[4,128,1024]{2,1,0:T(8,128)(2,1)}, u32[]{:S(2)}, u32[]{:S(2)}) %all-to-all-start.5) | async-done | bytes 1048608 | tf_op jit(solution)/shard_map/all_to_all | solution.py:583
  269.7 11.0 %all-to-all-start.7 = ((bf16[32,2,48,128]{3,2,1,0:T(8,128)(2,1)}), bf16[32,2,48,128]{3,2,1,0:T(8,128)(2,1)}, u32[]{:S(2)}, u32[]{:S(2)}) async-start(bf16[32,2,48,128]{3,2,1,0:T(8,128)(2,1)} %bitcast.278), calls=%async_computation.7 | async-start | bytes 1572864 | tf_op jit(solution)/shard_map/all_to_all | solution.py:583
  286.1 15.8 %attn_bwd.1 = (bf16[4,2,64,128]{3,2,1,0:T(8,128)(2,1)S(1)}, bf16[16,4,2,64,128]{4,3,2,1,0:T(8,128)(2,1)S(1)}, bf16[16,4,2,64,128]{4,3,2,1,0:T(8,128)(2,1)S(1)}) custom-call(s32[1]{0:T(128)} %bitcast.1.idx_ref, bf16[4,2,128,64]{3,2,1,0:T(8,128)(2,1)S(1)} %copy-done.62, bf16[32,4,2,64,128]{4,3,2,1,0:T(8,128)(2,1)S(1)} %bitcast.266, ...), custom_call_target="tpu_custom_call" | custom-call | flops 8000000 | bytes 16000 | tf_op jit(solution)/shard_map/attn_bwd/pallas_call | solution.py:968
  313.6 7.4 %all-to-all-start.9 = ((bf16[32,2,48,128]{3,2,1,0:T(8,128)(2,1)}), bf16[32,2,48,128]{3,2,1,0:T(8,128)(2,1)}, u32[]{:S(2)}, u32[]{:S(2)}) async-start(bf16[32,2,48,128]{3,2,1,0:T(8,128)(2,1)} %copy-done.12), calls=%async_computation.9 | async-start | bytes 1572864 | tf_op jit(solution)/shard_map/all_to_all | solution.py:583
  326.3 8.9 %all-to-all-done.9 = bf16[32,2,48,128]{3,2,1,0:T(8,128)(2,1)} async-done(((bf16[32,2,48,128]{3,2,1,0:T(8,128)(2,1)}), bf16[32,2,48,128]{3,2,1,0:T(8,128)(2,1)}, u32[]{:S(2)}, u32[]{:S(2)}) %all-to-all-start.9) | async-done | bytes 786464 | tf_op jit(solution)/shard_map/all_to_all | solution.py:583
  351.7 15.0 %ssd_bwd.1 = (bf16[8,72,640]{2,1,0:T(8,128)(2,1)S(1)}, bf16[8,72,128]{2,1,0:T(8,128)(2,1)S(1)}, f32[8,8,640]{2,1,0:T(8,128)S(1)}) custom-call(s32[1]{0:T(128)} %bitcast.1.idx_ref, f32[8,72,640]{2,1,0:T(8,128)S(1)} %copy-done.18, f32[8,72,128]{2,1,0:T(8,128)S(1)} %copy-done.52, s32[8,64,128]{2,1,0:T(8,128)S(1)} %copy-done.32, f32[8,640]{1,0:T(8,128)S(1)} %copy-done.84, ...), custom_call_target="tpu_custom_call" | custom-call | flops 4000000 | bytes 8000 | tf_op jit(solution)/shard_map/ssd_bwd/pallas_call | solution.py:1012
  371.9 6.7 %all-to-all-start.10 = ((bf16[16,4,8,2048]{3,2,1,0:T(8,128)(2,1)}), bf16[16,4,8,2048]{3,2,1,0:T(8,128)(2,1)S(1)}, u32[]{:S(2)}, u32[]{:S(2)}) async-start(bf16[16,4,8,2048]{3,2,1,0:T(8,128)(2,1)} %copy-done.2), calls=%async_computation.10 | async-start | bytes 4194304 | tf_op jit(solution)/shard_map/all_to_all | solution.py:1057
  399.7 5.7 %collective-permute-done.21 = bf16[144,1024]{1,0:T(8,128)(2,1)S(1)} collective-permute-done((bf16[144,1024]{1,0:T(8,128)(2,1)S(1)}, bf16[144,1024]{1,0:T(8,128)(2,1)S(1)}, u32[]{:S(2)}, u32[]{:S(2)}) %collective-permute-start.21) | collective-permute-done | bytes 294944 | tf_op jit(solution)/shard_map/ppermute | solution.py:616
  405.4 5.2 collective-permute-done.22
  420.8 6.4 %all-to-all-start.11 = ((bf16[16,4,8,1408]{3,2,1,0:T(8,128)(2,1)}), bf16[16,4,8,1408]{3,2,1,0:T(8,128)(2,1)}, u32[]{:S(2)}, u32[]{:S(2)}) async-start(bf16[16,4,8,1408]{3,2,1,0:T(8,128)(2,1)} %copy-done.19), calls=%async_computation.11 | async-start | bytes 2883584 | tf_op jit(solution)/shard_map/all_to_all | solution.py:1057
  439.8 5.6 %collective-permute-done.16 = bf16[128,1024]{1,0:T(8,128)(2,1)} collective-permute-done((bf16[128,1024]{1,0:T(8,128)(2,1)}, bf16[128,1024]{1,0:T(8,128)(2,1)}, u32[]{:S(2)}, u32[]{:S(2)}) %collective-permute-start.16) | collective-permute-done | bytes 262176 | tf_op jit(solution)/shard_map/ppermute | solution.py:616
  452.4 9.3 %all_to_all.71.owned_ref = f32[4,8,2432]{2,1,0:T(8,128)S(1)} all-to-all(f32[4,8,2432]{2,1,0:T(8,128)S(1)} %get-tuple-element.69), channel_id=1, replica_groups=mesh['ctx'=32,'fsdp'=4] {'fsdp'}, dimensions={0} | all-to-all | bytes 622592 | tf_op jit(solution)/shard_map/all_to_all | solution.py:583
  462.0 48.5 %all_to_all.72.mine_ref = bf16[16,8,12416]{2,1,0:T(8,128)(2,1)S(1)} all-to-all(bf16[16,8,12416]{2,1,0:T(8,128)(2,1)S(1)} %broadcast_in_dim.178), channel_id=1, replica_groups={{0,8,16,24,32,40,48,56,64,72,80,88,96,104,112,120},{4,12,20,28,36,44,52..., dimensions={0} | all-to-all | bytes 6356992 | tf_op jit(solution)/shard_map/all_to_all | solution.py:1057
  510.7 5.5 %collective-permute-done.28.other_ref = bf16[16,8,12416]{2,1,0:T(8,128)(2,1)} collective-permute-done((bf16[16,8,12416]{2,1,0:T(8,128)(2,1)S(1)}, bf16[16,8,12416]{2,1,0:T(8,128)(2,1)}, u32[]{:S(2)}, u32[]{:S(2)}) %collective-permute-start.28) | collective-permute-done | bytes 3178528 | tf_op jit(solution)/shard_map/ppermute | solution.py:1117
  517.9 7.4 %unpack.1 = (f32[256,4096]{1,0:T(8,128)}, f32[256,128]{1,0:T(8,128)S(1)}, f32[256,4096]{1,0:T(8,128)}, f32[256,128]{1,0:T(8,128)S(1)}, f32[512,1024]{1,0:T(8,128...) custom-call(s32[1]{0:T(128)} %bitcast.2.core_ref, bf16[16,8,12416]{2,1,0:T(8,128)(2,1)S(1)} %all_to_all.72.mine_ref, ...), custom_call_target="tpu_custom_call" | custom-call | bytes 10000 | tf_op jit(solution)/shard_map/unpack/pallas_call | solution.py:1119
  (545 shorter events, 256.6 us)
Async XLA Ops:
  17.4 30.8 %all-to-all-start = ((bf16[4,128,1280]{2,1,0:T(8,128)(2,1)}), bf16[4,128,1280]{2,1,0:T(8,128)(2,1)S(1)}, u32[]{:S(2)}, u32[]{:S(2)}) async-start(bf16[4,128,1280]{2,1,0:T(8,128)(2,1)} %split_in.1), calls=%async_computation | async-start | bytes 2621440 | tf_op jit(solution)/shard_map/all_to_all | solution.py:583
  22.6 105.8 %all-gather.3.cloned.1.call-start = ((), (), s32[]{:S(2)}) async-start(), calls=%async_computation.14 | async-start | bytes 4325376 | tf_op jit(solution)/shard_map/all_gather | solution.py:804
  23.5 23.7 %collective-permute-start.2 = (bf16[2,72,1024]{2,1,0:T(8,128)(2,1)S(1)}, bf16[2,72,1024]{2,1,0:T(8,128)(2,1)}, u32[]{:S(2)}, u32[]{:S(2)}) collective-permute-start(bf16[2,72,1024]{2,1,0:T(8,128)(2,1)S(1)} %pad_maximum_fusion.4), channel_id=1, source_target_pairs={{0,1},{1,2},{2,3},{3,0},{4,5},{5,6},{6,7},{7,4},{8,9},{9,10},{10,1... | collective-permute-start | bytes 884744 | tf_op jit(solution)/shard_map/ppermute | solution.py:606
  25.9 27.8 %collective-permute-start.3 = (bf16[2,72,1024]{2,1,0:T(8,128)(2,1)S(1)}, bf16[2,72,1024]{2,1,0:T(8,128)(2,1)}, u32[]{:S(2)}, u32[]{:S(2)}) collective-permute-start(bf16[2,72,1024]{2,1,0:T(8,128)(2,1)S(1)} %pad_maximum_fusion.4), channel_id=1, source_target_pairs={{0,2},{1,3},{2,0},{3,1},{4,6},{5,7},{6,4},{7,5},{8,10},{9,11},{10,... | collective-permute-start | bytes 884744 | tf_op jit(solution)/shard_map/ppermute | solution.py:606
  28.5 26.2 %collective-permute-start.4 = (bf16[2,72,1024]{2,1,0:T(8,128)(2,1)S(1)}, bf16[2,72,1024]{2,1,0:T(8,128)(2,1)}, u32[]{:S(2)}, u32[]{:S(2)}) collective-permute-start(bf16[2,72,1024]{2,1,0:T(8,128)(2,1)S(1)} %pad_maximum_fusion.4), channel_id=1, source_target_pairs={{0,3},{1,0},{2,1},{3,2},{4,7},{5,4},{6,5},{7,6},{8,11},{9,8},{10,9... | collective-permute-start | bytes 884744 | tf_op jit(solution)/shard_map/ppermute | solution.py:606
  72.4 29.1 %collective-permute-start.9 = (bf16[128,1024]{1,0:T(8,128)(2,1)}, bf16[128,1024]{1,0:T(8,128)(2,1)}, u32[]{:S(2)}, u32[]{:S(2)}) collective-permute-start(bf16[128,1024]{1,0:T(8,128)(2,1)} %bitcast.309), channel_id=1, source_target_pairs={{0,1},{1,2},{2,3},{3,0},{4,5},{5,6},{6,7},{7,4},{8,9},{9,10},{10,1... | collective-permute-start | bytes 786440 | tf_op jit(solution)/shard_map/ppermute | solution.py:606
  78.0 30.3 %collective-permute-start.6 = (bf16[256,1024]{1,0:T(8,128)(2,1)}, bf16[256,1024]{1,0:T(8,128)(2,1)}, u32[]{:S(2)}, u32[]{:S(2)}) collective-permute-start(bf16[256,1024]{1,0:T(8,128)(2,1)} %dynamic-slice_bitcast_fusion.5), channel_id=1, source_target_pairs={{0,1},{1,2},{2,3},{3,0},{4,5},{5,6},{6,7},{7,4},{8,9},{9,10},{10,1... | collective-permute-start | bytes 1572872 | tf_op jit(solution)/shard_map/ppermute | solution.py:598
  90.8 29.5 %all-to-all-start.1 = ((bf16[32,2,64,128]{3,2,1,0:T(8,128)(2,1)}), bf16[32,2,64,128]{3,2,1,0:T(8,128)(2,1)S(1)}, u32[]{:S(2)}, u32[]{:S(2)}) async-start(bf16[32,2,64,128]{3,2,1,0:T(8,128)(2,1)} %bitcast.292), calls=%async_computation.1 | async-start | bytes 2097152 | tf_op jit(solution)/shard_map/all_to_all | solution.py:583
  110.8 41.4 %collective-permute-start.7 = (bf16[256,1024]{1,0:T(8,128)(2,1)}, bf16[256,1024]{1,0:T(8,128)(2,1)}, u32[]{:S(2)}, u32[]{:S(2)}) collective-permute-start(bf16[256,1024]{1,0:T(8,128)(2,1)} %get-tuple-element.99), channel_id=1, source_target_pairs={{0,2},{1,3},{2,0},{3,1},{4,6},{5,7},{6,4},{7,5},{8,10},{9,11},{10,... | collective-permute-start | bytes 1572872 | tf_op jit(solution)/shard_map/ppermute | solution.py:598
  114.5 39.6 %collective-permute-start.8 = (bf16[256,1024]{1,0:T(8,128)(2,1)}, bf16[256,1024]{1,0:T(8,128)(2,1)}, u32[]{:S(2)}, u32[]{:S(2)}) collective-permute-start(bf16[256,1024]{1,0:T(8,128)(2,1)} %get-tuple-element.98), channel_id=1, source_target_pairs={{0,3},{1,0},{2,1},{3,2},{4,7},{5,4},{6,5},{7,6},{8,11},{9,8},{10,9... | collective-permute-start | bytes 1572872 | tf_op jit(solution)/shard_map/ppermute | solution.py:598
  122.1 33.8 %all-to-all-start.2 = ((bf16[32,2,48,128]{3,2,1,0:T(8,128)(2,1)}), bf16[32,2,48,128]{3,2,1,0:T(8,128)(2,1)S(1)}, u32[]{:S(2)}, u32[]{:S(2)}) async-start(bf16[32,2,48,128]{3,2,1,0:T(8,128)(2,1)} %copy-done.44), calls=%async_computation.2 | async-start | bytes 1572864 | tf_op jit(solution)/shard_map/all_to_all | solution.py:583
  166.6 19.9 %all-to-all-start.3 = ((bf16[4,144,1024]{2,1,0:T(8,128)(2,1)}), bf16[4,144,1024]{2,1,0:T(8,128)(2,1)}, u32[]{:S(2)}, u32[]{:S(2)}) async-start(bf16[4,144,1024]{2,1,0:T(8,128)(2,1)} %copy-done.23), calls=%async_computation.3 | async-start | bytes 2359296 | tf_op jit(solution)/shard_map/all_to_all | solution.py:583
  219.3 16.6 %all-to-all-start.5 = ((bf16[4,128,1024]{2,1,0:T(8,128)(2,1)}), bf16[4,128,1024]{2,1,0:T(8,128)(2,1)}, u32[]{:S(2)}, u32[]{:S(2)}) async-start(bf16[4,128,1024]{2,1,0:T(8,128)(2,1)} %bitcast.318), calls=%async_computation.5 | async-start | bytes 2097152 | tf_op jit(solution)/shard_map/all_to_all | solution.py:583
  239.7 16.8 %all-to-all-start.6 = ((bf16[4,144,1024]{2,1,0:T(8,128)(2,1)}), bf16[4,144,1024]{2,1,0:T(8,128)(2,1)}, u32[]{:S(2)}, u32[]{:S(2)}) async-start(bf16[4,144,1024]{2,1,0:T(8,128)(2,1)} %broadcast_in_dim.168), calls=%async_computation.6 | async-start | bytes 2359296 | tf_op jit(solution)/shard_map/all_to_all | solution.py:583
  269.7 36.4 %all-to-all-start.7 = ((bf16[32,2,48,128]{3,2,1,0:T(8,128)(2,1)}), bf16[32,2,48,128]{3,2,1,0:T(8,128)(2,1)}, u32[]{:S(2)}, u32[]{:S(2)}) async-start(bf16[32,2,48,128]{3,2,1,0:T(8,128)(2,1)} %bitcast.278), calls=%async_computation.7 | async-start | bytes 1572864 | tf_op jit(solution)/shard_map/all_to_all | solution.py:583
  313.4 30.1 %collective-permute-start.19 = (bf16[4,128,1024]{2,1,0:T(8,128)(2,1)}, bf16[4,128,1024]{2,1,0:T(8,128)(2,1)}, u32[]{:S(2)}, u32[]{:S(2)}) collective-permute-start(bf16[4,128,1024]{2,1,0:T(8,128)(2,1)} %dynamic-slice_bitcast_fusion.2), channel_id=1, source_target_pairs={{0,4},{4,0},{8,12},{12,8},{16,20},{20,16},{24,28},{28,24},{32,36},... | collective-permute-start | bytes 3145736 | tf_op jit(solution)/shard_map/ppermute | solution.py:943
  313.6 21.6 %all-to-all-start.9 = ((bf16[32,2,48,128]{3,2,1,0:T(8,128)(2,1)}), bf16[32,2,48,128]{3,2,1,0:T(8,128)(2,1)}, u32[]{:S(2)}, u32[]{:S(2)}) async-start(bf16[32,2,48,128]{3,2,1,0:T(8,128)(2,1)} %copy-done.12), calls=%async_computation.9 | async-start | bytes 1572864 | tf_op jit(solution)/shard_map/all_to_all | solution.py:583
  321.0 26.1 %collective-permute-start.20 = (bf16[512,1024]{1,0:T(8,128)(2,1)}, bf16[512,1024]{1,0:T(8,128)(2,1)}, u32[]{:S(2)}, u32[]{:S(2)}) collective-permute-start(bf16[512,1024]{1,0:T(8,128)(2,1)} %get-tuple-element.132), channel_id=1, source_target_pairs={{0,4},{4,0},{8,12},{12,8},{16,20},{20,16},{24,28},{28,24},{32,36},... | collective-permute-start | bytes 3145736 | tf_op jit(solution)/shard_map/ppermute | solution.py:949
  335.2 36.6 %all-to-all-start.8 = ((bf16[16,4,2,64,128]{4,3,2,1,0:T(8,128)(2,1)}), bf16[16,4,2,64,128]{4,3,2,1,0:T(8,128)(2,1)}, u32[]{:S(2)}, u32[]{:S(2)}) async-start(bf16[16,4,2,64,128]{4,3,2,1,0:T(8,128)(2,1)} %add_convert_fusion), calls=%async_computation.8 | async-start | bytes 4194304 | tf_op jit(solution)/shard_map/all_to_all | solution.py:1057
  371.9 44.9 %all-to-all-start.10 = ((bf16[16,4,8,2048]{3,2,1,0:T(8,128)(2,1)}), bf16[16,4,8,2048]{3,2,1,0:T(8,128)(2,1)S(1)}, u32[]{:S(2)}, u32[]{:S(2)}) async-start(bf16[16,4,8,2048]{3,2,1,0:T(8,128)(2,1)} %copy-done.2), calls=%async_computation.10 | async-start | bytes 4194304 | tf_op jit(solution)/shard_map/all_to_all | solution.py:1057
  391.9 24.9 %collective-permute-start.26 = (bf16[4,128,1280]{2,1,0:T(8,128)(2,1)}, bf16[4,128,1280]{2,1,0:T(8,128)(2,1)}, u32[]{:S(2)}, u32[]{:S(2)}) collective-permute-start(bf16[4,128,1280]{2,1,0:T(8,128)(2,1)} %get-tuple-element.92), channel_id=1, source_target_pairs={{0,4},{4,0},{8,12},{12,8},{16,20},{20,16},{24,28},{28,24},{32,36},... | collective-permute-start | bytes 3932168 | tf_op jit(solution)/shard_map/ppermute | solution.py:943
  398.6 18.1 %collective-permute-start.27 = (bf16[4,128,128]{2,1,0:T(8,128)(2,1)S(1)}, bf16[4,128,128]{2,1,0:T(8,128)(2,1)S(1)}, u32[]{:S(2)}, u32[]{:S(2)}) collective-permute-start(bf16[4,128,128]{2,1,0:T(8,128)(2,1)S(1)} %get-tuple-element.114), channel_id=1, source_target_pairs={{0,4},{4,0},{8,12},{12,8},{16,20},{20,16},{24,28},{28,24},{32,36},... | collective-permute-start | bytes 393224 | tf_op jit(solution)/shard_map/ppermute | solution.py:943
  411.8 22.9 %collective-permute-start.25 = (bf16[3,1024]{1,0:T(4,128)(2,1)S(1)}, bf16[3,1024]{1,0:T(4,128)(2,1)S(1)}, u32[]{:S(2)}, u32[]{:S(2)}) collective-permute-start(bf16[3,1024]{1,0:T(4,128)(2,1)S(1)} %get-tuple-element.113), channel_id=1, source_target_pairs={{0,4},{4,8},{8,12},{12,16},{16,20},{20,24},{24,28},{28,32},{32,36}... | collective-permute-start | bytes 18440 | tf_op jit(solution)/shard_map/ppermute | solution.py:1077
  420.8 28.8 %all-to-all-start.11 = ((bf16[16,4,8,1408]{3,2,1,0:T(8,128)(2,1)}), bf16[16,4,8,1408]{3,2,1,0:T(8,128)(2,1)}, u32[]{:S(2)}, u32[]{:S(2)}) async-start(bf16[16,4,8,1408]{3,2,1,0:T(8,128)(2,1)} %copy-done.19), calls=%async_computation.11 | async-start | bytes 2883584 | tf_op jit(solution)/shard_map/all_to_all | solution.py:1057
  (162 other events, 1362.0 us)
Sparse Core Ops, SparseCore 0:
  72.5 53.7 all-gather.2
